TPU v7x, 32 devices: a whole 2x2x4 slice. The times are simulated.
32 devices in a mesh: row: 8 (over z, x), col: 2 (over y), ch: 2 (over core).
Axes of the slice: x: 2, y: 2, z: 4, core: 2. Of those that a mesh axis runs over, the one named last changes fastest.
Arguments:
- pair: bfloat16 [192, 192, 128], P('row', 'col'), may hold values from -6 to 6
- cotangent: bfloat16 [192, 192, 128], P('row', 'col', 'ch'), may hold values from -6 to 6
- w_gate_a: bfloat16 [128, 128], P(None, 'ch'), may hold values from -0.5 to 0.5
- w_proj_a: bfloat16 [128, 128], P(None, 'ch'), may hold values from -0.5 to 0.5
- w_gate_b: bfloat16 [128, 128], P(None, 'ch'), may hold values from -0.5 to 0.5
- w_proj_b: bfloat16 [128, 128], P(None, 'ch'), may hold values from -0.5 to 0.5
- w_gate_out: bfloat16 [128, 128], P(None, 'ch'), may hold values from -0.5 to 0.5
- w_out: bfloat16 [128, 128], P(None, 'ch'), may hold values from -0.5 to 0.5
Outputs:
- updated: bfloat16 [192, 192, 128], P('row', 'col', 'ch')
- grad_pair: bfloat16 [192, 192, 128], P('row', 'col', 'ch')
- grad_gate_a: float32 [128, 128], P(None, 'ch')
- grad_proj_a: float32 [128, 128], P(None, 'ch')
- grad_gate_b: float32 [128, 128], P(None, 'ch')
- grad_proj_b: float32 [128, 128], P(None, 'ch')
- grad_gate_out: float32 [128, 128], P(None, 'ch')
- grad_out: float32 [128, 128], P(None, 'ch')
All inputs are finite; a program needn't handle non-finite values.
Results may differ from a plain program's by a relative error of at most 0.022.
Values may be sent and summed in bfloat16 or wider, within the bound.
No kernel may reach another device: no remote copies, remote signals or barrier semaphores. Data moves between devices by JAX's collectives and lax.ppermute only.
A program may use at most 64 MiB of HBM per device.

v0:
```python
import functools

import jax
import jax.numpy as jnp
import numpy as np
from jax import lax
from jax.experimental import pallas as pl
from jax.experimental.pallas import tpu as pltpu
from jax.sharding import PartitionSpec as P

epsilon = 1e-05


def layer_norm(values):
    average = jnp.mean(values, -1, keepdims=True)
    centred = values - average
    spread = jnp.mean(centred * centred, -1, keepdims=True)
    inverse = lax.rsqrt(spread + epsilon)
    return (centred * inverse, inverse)


def matmul(first, second):
    return jnp.dot(first, second, preferred_element_type=jnp.float32)


def by_rows(pair, cotangent, w_gate_a, w_proj_a, w_gate_b, w_proj_b, w_gate_out, w_out):
    row_count, col_count, channels = pair.shape
    hidden = w_gate_a.shape[1]
    total_hidden = hidden * lax.axis_size("ch")
    out_width = cotangent.shape[2]
    length = row_count * lax.axis_size("row")
    grad_scale = 1.0 / length
    pair_hat, pair_rstd = layer_norm(pair.astype(jnp.float32))
    flat_norm = pair_hat.astype(jnp.bfloat16).reshape(row_count * col_count, channels)
    w_four = jnp.concatenate([w_gate_a, w_proj_a, w_gate_b, w_proj_b], axis=1)
    projected = matmul(flat_norm, w_four)
    gate_a = jax.nn.sigmoid(projected[:, :hidden])
    proj_a = projected[:, hidden : 2 * hidden]
    gate_b = jax.nn.sigmoid(projected[:, 2 * hidden : 3 * hidden])
    proj_b = projected[:, 3 * hidden :]
    left_edge = (gate_a * proj_a).astype(jnp.bfloat16).reshape(row_count, col_count, hidden)
    right_edge = (gate_b * proj_b).astype(jnp.bfloat16).reshape(row_count, col_count, hidden)
    right_all = lax.all_gather(right_edge, "row", axis=0, tiled=True)
    mixed_swap = lax.psum_scatter(
        jnp.einsum("jkh,ikh->jih", right_all, left_edge, preferred_element_type=jnp.float32).astype(
            jnp.bfloat16
        ),
        "col",
        scatter_dimension=0,
        tiled=True,
    ).astype(jnp.float32)
    mixed = jnp.swapaxes(mixed_swap, 0, 1).reshape(row_count * col_count, hidden)
    hidden_sums = lax.psum((jnp.sum(mixed, -1), jnp.sum(mixed * mixed, -1)), "ch")
    hidden_mean = (hidden_sums[0] / total_hidden)[:, None]
    hidden_var = (hidden_sums[1] / total_hidden)[:, None] - hidden_mean * hidden_mean
    hidden_rstd = lax.rsqrt(hidden_var + epsilon)
    mixed_hat = (mixed - hidden_mean) * hidden_rstd
    mixed_norm = mixed_hat.astype(jnp.bfloat16)
    norm_full = lax.all_gather(mixed_norm, "ch", axis=1, tiled=True)
    gate_out = jax.nn.sigmoid(matmul(flat_norm, w_gate_out))
    proj_out = matmul(norm_full, w_out)
    updated = (gate_out * proj_out).astype(jnp.bfloat16).reshape(row_count, col_count, out_width)
    upstream = cotangent.reshape(row_count * col_count, out_width).astype(jnp.float32)
    d_proj = (upstream * gate_out).astype(jnp.bfloat16)
    d_gate = (upstream * proj_out * gate_out * (1.0 - gate_out)).astype(jnp.bfloat16)
    head_grads = lax.psum(
        (matmul(norm_full.T, d_proj) * grad_scale, matmul(flat_norm.T, d_gate) * grad_scale),
        ("row", "col"),
    )
    d_norm = lax.psum_scatter(
        matmul(d_proj, w_out.T).astype(jnp.bfloat16), "ch", scatter_dimension=1, tiled=True
    ).astype(jnp.float32)
    back_sums = lax.psum((jnp.sum(d_norm, -1), jnp.sum(d_norm * mixed_hat, -1)), "ch")
    d_mixed = hidden_rstd * (
        d_norm
        - (back_sums[0] / total_hidden)[:, None]
        - mixed_hat * (back_sums[1] / total_hidden)[:, None]
    )
    d_mixed = d_mixed.astype(jnp.bfloat16).reshape(row_count, col_count, hidden)
    d_rows = lax.all_gather(d_mixed, "col", axis=1, tiled=True)
    right_back = lax.all_gather(right_edge, "row", axis=0, tiled=True)
    d_left = jnp.einsum("ijh,jkh->ikh", d_rows, right_back, preferred_element_type=jnp.float32)
    d_left = d_left.reshape(row_count * col_count, hidden)
    left_all = lax.all_gather(left_edge, "row", axis=0, tiled=True)
    d_columns = lax.all_to_all(d_rows, "row", split_axis=1, concat_axis=0, tiled=True)
    d_right = jnp.einsum("ijh,ikh->jkh", d_columns, left_all, preferred_element_type=jnp.float32)
    d_right = d_right.reshape(row_count * col_count, hidden)
    grad_pa = (d_left * gate_a).astype(jnp.bfloat16)
    grad_ga = (d_left * proj_a * gate_a * (1.0 - gate_a)).astype(jnp.bfloat16)
    grad_pb = (d_right * gate_b).astype(jnp.bfloat16)
    grad_gb = (d_right * proj_b * gate_b * (1.0 - gate_b)).astype(jnp.bfloat16)
    d_four = jnp.concatenate([grad_ga, grad_pa, grad_gb, grad_pb], axis=1)
    weight_terms = matmul(flat_norm.T, d_four) * grad_scale
    summed = lax.psum(weight_terms, ("row", "col"))
    d_flat = matmul(d_four, w_four.T) + matmul(d_gate, w_gate_out.T)
    hat_all = pair_hat.reshape(row_count * col_count, channels)
    rstd_flat = pair_rstd.reshape(row_count * col_count, 1)
    offset = lax.axis_index("ch") * out_width
    grad_whole = lax.psum(d_flat.astype(jnp.bfloat16), "ch").astype(jnp.float32)
    grad_full = rstd_flat * (
        grad_whole
        - jnp.mean(grad_whole, -1, keepdims=True)
        - hat_all * jnp.mean(grad_whole * hat_all, -1, keepdims=True)
    )
    grad_pair = lax.dynamic_slice_in_dim(grad_full, offset, out_width, 1)
    grad_pair = grad_pair.astype(jnp.bfloat16).reshape(row_count, col_count, out_width)
    return (
        updated,
        grad_pair,
        summed[:, :hidden],
        summed[:, hidden : 2 * hidden],
        summed[:, 2 * hidden : 3 * hidden],
        summed[:, 3 * hidden :],
        head_grads[1],
        head_grads[0],
    )


everyone = ("col", "row", "ch")
f32, bf16 = jnp.float32, jnp.bfloat16


def dot(first, second, over):
    return lax.dot_general(
        first, second, (((over[0],), (over[1],)), ((), ())), preferred_element_type=f32
    )


def call(kernel, outs, args, scratch=(), far=(), outs_far=False, room=16):
    whole = pl.BlockSpec(memory_space=pltpu.VMEM)
    anywhere = pl.BlockSpec(memory_space=pl.ANY)
    return pl.pallas_call(
        kernel,
        out_shape=tuple(jax.ShapeDtypeStruct(*out) for out in outs),
        in_specs=[anywhere if at in far else whole for at in range(len(args))],
        out_specs=tuple(anywhere if outs_far else whole for _ in outs),
        scratch_shapes=scratch,
        compiler_params=pltpu.CompilerParams(vmem_limit_bytes=room * 2**20),
    )(*args)


def grouping(hidden, share):
    shape = (2 * hidden, 2 * hidden)
    rows = lax.broadcasted_iota(jnp.int32, shape, 0)
    columns = lax.broadcasted_iota(jnp.int32, shape, 1)
    group, within = rows // (2 * share), lax.rem(rows, 2 * share)
    side = within // share
    wanted = side * hidden + group * share + within - side * share
    return jnp.where(columns == wanted, 1.0, 0.0).astype(bf16)


def start_all(copies):
    for copy in copies:
        copy.start()


def wait_all(copies):
    for copy in copies:
        copy.wait()


def prepare(share, ga, pa, gb, pb, go, wo, pair_far, out, normed, gates, values, last, pair, arrivals):
    hidden = go.shape[0]
    count = pair.shape[0]
    rows = pl.ds(lax.axis_index("ch") * count, count)
    fetch = pltpu.make_async_copy(pair_far.at[rows], pair, arrivals.at[6])
    fetch.start()
    width = 2 * hidden
    copies = []
    for at, (held, low, high) in enumerate(((gates, ga, gb), (values, pa, pb), (last, go, wo))):
        copies.append(pltpu.make_async_copy(low, held.at[0:hidden], arrivals.at[2 * at]))
        copies.append(pltpu.make_async_copy(high, held.at[hidden:width], arrivals.at[2 * at + 1]))
    start_all(copies)
    order = grouping(hidden, share)
    wait_all(copies)
    out[:width] = dot(order, gates[...], (1, 0)).astype(bf16)
    out[width : 2 * width] = dot(order, values[...], (1, 0)).astype(bf16)
    out[2 * width :] = last[...]
    fetch.wait()
    normed[...] = normalized(pair[...])[0].astype(bf16)


def rows_of(weights, start, count):
    return jnp.concatenate([weights[c, start : start + count] for c in range(weights.shape[0])], 0)


def normalized(pair):
    count, cols, channels = pair.shape
    values = pair.astype(f32).reshape(count * cols, channels).T
    centred = values - jnp.mean(values, 0, keepdims=True)
    rstd = lax.rsqrt(jnp.mean(centred * centred, 0, keepdims=True) + epsilon)
    return centred * rstd, rstd


def edges(width, normed, weights, send):
    gate = jax.nn.sigmoid(dot(rows_of(weights, 0, width), normed[...], (1, 0)))
    value = dot(rows_of(weights, width, width), normed[...], (1, 0))
    send[...] = (gate * value).reshape(send.shape).astype(bf16)


def spread_rows(block, cols, arrived, held):
    devices, q, flat = arrived.shape
    rows = flat // cols
    for s in range(devices):
        tile = arrived[s].astype(f32)
        for i in range(rows):
            start = (s * rows + i) * block
            held[start : start + q, 0:cols] = tile[:, i * cols : (i + 1) * cols]


def pack_rows(block, cols, held, send):
    devices, q, flat = send.shape
    rows = flat // cols
    for s in range(devices):
        starts = [(s * rows + i) * block for i in range(rows)]
        whole = jnp.concatenate([held[start : start + block, 0:cols] for start in starts], axis=1)
        send[s] = whole[:q].astype(bf16)


def square(block, parts, cols, held, e):
    tokens = parts * cols
    return jnp.concatenate(
        [
            held[pl.ds(p * tokens * block + e, tokens, stride=block), 0:cols]
            for p in range(parts)
        ],
        axis=1,
    ).astype(bf16)


def put_square(block, parts, cols, held, e, values):
    tokens = parts * cols
    for p in range(parts):
        held[pl.ds(p * tokens * block + e, tokens, stride=block), 0:cols] = values[
            :, p * cols : (p + 1) * cols
        ]


def mix(parts, cols, arrived, send, kept, held, result):
    block = 8
    q = arrived.shape[1]
    spread_rows(block, cols, arrived, held)
    for e in range(q // 2):
        left = square(block, parts, cols, held, e)
        right = square(block, parts, cols, held, q // 2 + e)
        kept[e] = left
        kept[q // 2 + e] = right
        put_square(block, parts, cols, result, e, dot(left, right, (1, 1)))
    pack_rows(block, cols, result, send)


def unmix(parts, cols, arrived, kept_far, send, held, result, kept, arrival):
    block = 8
    q = arrived.shape[1]
    copy = pltpu.make_async_copy(kept_far, kept, arrival)
    copy.start()
    spread_rows(block, cols, arrived, held)
    copy.wait()
    for e in range(q):
        d_mixed = square(block, parts, cols, held, e)
        put_square(block, parts, cols, result, e, dot(d_mixed, kept[q + e], (1, 0)))
        put_square(block, parts, cols, result, q + e, dot(d_mixed, kept[e], (0, 0)))
    pack_rows(block, cols, result, send)


def split_rows(cols, values, own, other):
    hidden = values.shape[0] // 2
    first = lax.axis_index("ch") == 0
    low, high = values[:hidden], values[hidden:]
    mine = jnp.where(first, low, high)
    yours = jnp.where(first, high, low)
    for i in range(own.shape[0]):
        own[i] = mine[:, i * cols : (i + 1) * cols].astype(bf16)
        other[i] = yours[:, i * cols : (i + 1) * cols].astype(bf16)


def head(
    width, scale, arrived, weights, normed_far, own_far, other_far,
    send, d_gate, terms, updated_own, updated_other,
    normed, own, other, upstream, arrivals,
):
    parts, total, _ = weights.shape
    hidden = (total - 2 * width) // 2
    devices, q, flat = arrived.shape
    count, _, cols = other.shape
    core = lax.axis_index("ch")
    copies = [
        pltpu.make_async_copy(normed_far, normed, arrivals.at[0]),
        pltpu.make_async_copy(own_far.at[pl.ds(core * count, count)], own, arrivals.at[1]),
        pltpu.make_async_copy(other_far, other, arrivals.at[2]),
    ]
    start_all(copies)
    mixed = jnp.concatenate([arrived[s].astype(f32) for s in range(devices)], 0)
    average = jnp.mean(mixed, 0, keepdims=True)
    spread = jnp.mean(mixed * mixed, 0, keepdims=True) - average * average
    inverse = lax.rsqrt(spread + epsilon)
    hat = (mixed - average) * inverse
    hat_rounded = hat.astype(bf16)
    w_out = rows_of(weights, 2 * width + hidden, hidden)
    proj = dot(w_out, hat_rounded, (1, 0))
    wait_all(copies)
    for part, side in ((own, core), (other, 1 - core)):
        upstream[pl.ds(pl.multiple_of(side * hidden, hidden), hidden)] = jnp.concatenate(
            [part[i].astype(f32) for i in range(count)], axis=1
        )
    gate = jax.nn.sigmoid(dot(rows_of(weights, 2 * width, hidden), normed[...], (1, 0)))
    up = upstream[...]
    d_proj = (up * gate).astype(bf16)
    d_gate[...] = (up * proj * gate * (1.0 - gate)).astype(bf16)
    d_norm = dot(w_out, d_proj, (0, 0))
    d_mixed = inverse * (
        d_norm
        - jnp.mean(d_norm, 0, keepdims=True)
        - hat * jnp.mean(d_norm * hat, 0, keepdims=True)
    )
    for s in range(devices):
        send[s] = d_mixed[s * q : (s + 1) * q].astype(bf16)
    by_gate = dot(d_gate[...], normed[...], (1, 1)) * scale
    by_out = dot(d_proj, hat_rounded, (1, 1)) * scale
    for c in range(parts):
        terms[c, :hidden] = by_gate[c * hidden : (c + 1) * hidden]
        terms[c, hidden:] = by_out[c * hidden : (c + 1) * hidden]
    split_rows(cols, gate * proj, updated_own, updated_other)


def tail(
    width, scale, arrived, weights, pair_far, d_gate_far, head_terms,
    send, grad_own, grad_other,
    pair, d_gate, whole, arrivals,
):
    parts, total, channels = weights.shape
    hidden = (total - 2 * width) // 2
    devices, q, flat = arrived.shape
    count, cols, _ = pair.shape
    core = lax.axis_index("ch")
    copies = [
        pltpu.make_async_copy(pair_far.at[pl.ds(core * count, count)], pair, arrivals.at[0]),
        pltpu.make_async_copy(d_gate_far, d_gate, arrivals.at[1]),
    ]
    start_all(copies)
    wait_all(copies)
    hat, inverse = normalized(pair[...])
    normed = hat.astype(bf16)
    w_gate, w_value = rows_of(weights, 0, width), rows_of(weights, width, width)
    gate = jax.nn.sigmoid(dot(w_gate, normed, (1, 0)))
    value = dot(w_value, normed, (1, 0))
    grad = arrived[...].astype(f32).reshape(devices * q, flat)
    by_value = grad * gate
    by_gate = (by_value * (value * (1.0 - gate))).astype(bf16)
    by_value = by_value.astype(bf16)
    terms = [dot(by_gate, normed, (1, 1)) * scale, dot(by_value, normed, (1, 1)) * scale]
    for c in range(parts):
        for at, term in enumerate(terms):
            start = c * total + at * width
            whole[start : start + width] = term[c * width : (c + 1) * width]
        whole[c * total + 2 * width : (c + 1) * total] = head_terms[c]
    per = send.shape[1]
    for s in range(devices):
        send[s] = whole[s * per : (s + 1) * per].astype(bf16)
    d_input = dot(w_gate, by_gate, (0, 0)) + dot(w_value, by_value, (0, 0))
    d_input = d_input + dot(rows_of(weights, 2 * width, hidden), d_gate[...], (0, 0))
    back = inverse * (
        d_input
        - jnp.mean(d_input, 0, keepdims=True)
        - hat * jnp.mean(d_input * hat, 0, keepdims=True)
    )
    split_rows(cols, back, grad_own, grad_other)


def add_up(arrived, out):
    total = jnp.sum(arrived[...].astype(f32), 0).astype(bf16)
    for s in range(out.shape[0]):
        out[s] = total


def turn_back(share, sums, *refs):
    outs, whole, results, leaves = refs[:6], refs[6], refs[7], refs[8]
    _, hidden, channels = results.shape
    width = 2 * hidden
    per = sums.shape[1]
    for s in range(sums.shape[0]):
        whole[s * per : (s + 1) * per] = sums[s].astype(f32)
    order = grouping(hidden, share)
    for at in range(2):
        both = dot(order, whole[at * width : (at + 1) * width].astype(bf16), (0, 0))
        results[at] = both[:hidden]
        results[2 + at] = both[hidden:]
    results[4] = whole[2 * width : 2 * width + hidden]
    results[5] = whole[2 * width + hidden :]
    copies = [
        pltpu.make_async_copy(results.at[at], out, leaves.at[at]) for at, out in enumerate(outs)
    ]
    start_all(copies)
    wait_all(copies)


def join_rows(own, other, out, leaves):
    count = own.shape[0]
    core = lax.axis_index("ch")
    copies = [
        pltpu.make_async_copy(own, out.at[pl.ds(core * count, count)], leaves.at[0]),
        pltpu.make_async_copy(other, out.at[pl.ds((1 - core) * count, count)], leaves.at[1]),
    ]
    start_all(copies)
    wait_all(copies)


def by_channels(pair, cotangent, w_gate_a, w_proj_a, w_gate_b, w_proj_b, w_gate_out, w_out):
    row_count, cols, channels = pair.shape
    hidden = w_gate_a.shape[1]
    parts, col_parts, row_parts = lax.axis_size("ch"), lax.axis_size("col"), lax.axis_size("row")
    devices = parts * col_parts * row_parts
    share = hidden * parts // devices
    width = 2 * hidden
    count = row_count // parts
    flat = count * cols
    tokens = cols * col_parts
    scale = 1.0 / tokens
    swap = [(c, parts - 1 - c) for c in range(parts)]
    whole_weight = pltpu.VMEM((2 * hidden, channels), bf16)
    weights, normed = call(
        functools.partial(prepare, share),
        [((2 * width + 2 * hidden, channels), bf16), ((channels, flat), bf16)],
        (w_gate_a.T, w_proj_a.T, w_gate_b.T, w_proj_b.T, w_gate_out.T, w_out.T, pair),
        (
            whole_weight,
            whole_weight,
            whole_weight,
            pltpu.VMEM((count, cols, channels), bf16),
            pltpu.SemaphoreType.DMA((7,)),
        ),
        far=range(7),
        room=60,
    )
    weights = lax.all_gather(weights, "ch")
    own = jnp.swapaxes(cotangent, 1, 2)
    other = lax.dynamic_slice_in_dim(own, (1 - lax.axis_index("ch")) * count, count, 0)
    other = lax.ppermute(other, "ch", swap)
    (send,) = call(
        functools.partial(edges, width), [((devices, 2 * share, flat), bf16)], (normed, weights)
    )
    arrived = lax.all_to_all(send, everyone, 0, 0)
    room = pltpu.VMEM((col_parts * tokens * 8, -(-cols // 128) * 128), f32)
    send, kept = call(
        functools.partial(mix, col_parts, cols),
        [((devices, share, flat), bf16), ((2 * share, tokens, tokens), bf16)],
        (arrived,),
        (room, room),
    )
    arrived = lax.all_to_all(send, everyone, 0, 0)
    part = ((count, hidden, cols), bf16)
    send, d_gate, head_terms, updated_own, updated_other = call(
        functools.partial(head, width, scale),
        [
            ((devices, share, flat), bf16),
            ((hidden * parts, flat), bf16),
            ((parts, 2 * hidden, channels), f32),
            part,
            part,
        ],
        (arrived, weights, normed, own, other),
        (
            pltpu.VMEM((channels, flat), bf16),
            pltpu.VMEM(*part),
            pltpu.VMEM(*part),
            pltpu.VMEM((hidden * parts, flat), f32),
            pltpu.SemaphoreType.DMA((3,)),
        ),
        far=(2, 3, 4),
    )
    arrived = lax.all_to_all(send, everyone, 0, 0)
    updated_other = lax.ppermute(updated_other, "ch", swap)
    (send,) = call(
        functools.partial(unmix, col_parts, cols),
        [((devices, 2 * share, flat), bf16)],
        (arrived, kept),
        (room, room, pltpu.VMEM(kept.shape, bf16), pltpu.SemaphoreType.DMA),
        far=(1,),
    )
    arrived = lax.all_to_all(send, everyone, 0, 0)
    rows = [((row_count, hidden, cols), bf16)]
    two = pltpu.SemaphoreType.DMA((2,))
    (updated,) = call(join_rows, rows, (updated_own, updated_other), (two,), (0, 1), True)
    arrived, updated = lax.optimization_barrier((arrived, updated))
    total = 2 * width + 2 * hidden
    per = total * parts // devices
    send, grad_own, grad_other = call(
        functools.partial(tail, width, scale),
        [((devices, per, channels), bf16), part, part],
        (arrived, weights, pair, d_gate, head_terms),
        (
            pltpu.VMEM((count, cols, channels), bf16),
            pltpu.VMEM((hidden * parts, flat), bf16),
            pltpu.VMEM((total * parts, channels), f32),
            two,
        ),
        far=(2, 3),
    )
    arrived = lax.all_to_all(send, ("ch", "row", "col"), 0, 0)
    grad_other = lax.ppermute(grad_other, "ch", swap)
    (grad_pair,) = call(join_rows, rows, (grad_own, grad_other), (two,), (0, 1), True)
    rest = devices // parts
    (sums,) = call(add_up, [((rest, per, channels), bf16)], (arrived,))
    sums = lax.all_to_all(sums, ("row", "col"), 0, 0)
    sums, grad_pair = lax.optimization_barrier((sums, grad_pair))
    grads = call(
        functools.partial(turn_back, share),
        [((hidden, channels), f32)] * 6,
        (sums,),
        (
            pltpu.VMEM((total, channels), f32),
            pltpu.VMEM((6, hidden, channels), f32),
            pltpu.SemaphoreType.DMA((6,)),
        ),
        outs_far=True,
    )
    return jnp.swapaxes(updated, 1, 2), jnp.swapaxes(grad_pair, 1, 2), *(g.T for g in grads)


def on_device(*arrays):
    row_count, cols, _ = arrays[0].shape
    parts, devices = lax.axis_size("ch"), lax.axis_size(everyone)
    hidden = arrays[2].shape[1]
    share = hidden * parts // devices
    fits = (
        share * devices == hidden * parts
        and parts == 2
        and 2 * share == 8
        and row_count % parts == 0
        and 6 * hidden * parts % devices == 0
        and arrays[1].shape[2] == hidden
        and cols % 16 == 0
    )
    return by_channels(*arrays) if fits else by_rows(*arrays)


def solution(mesh):
    in_specs = (
        P("row", "col", None),
        P("row", "col", "ch"),
        P(None, "ch"),
        P(None, "ch"),
        P(None, "ch"),
        P(None, "ch"),
        P(None, "ch"),
        P(None, "ch"),
    )
    out_specs = (
        P("row", "col", "ch"),
        P("row", "col", "ch"),
        P(None, "ch"),
        P(None, "ch"),
        P(None, "ch"),
        P(None, "ch"),
        P(None, "ch"),
        P(None, "ch"),
    )
    return jax.shard_map(
        on_device, mesh=mesh, in_specs=in_specs, out_specs=out_specs, check_vma=False
    )
```

profile of v0, /device:TPU:0, one launch (start us, length us, event | category | flops | bytes accessed | tf_op | source)
XLA Modules:
  0.0 109.7 jit_solution(5674280554501123597)
XLA Ops:
  0.6 2.1 %shard_map.143 = (bf16[384,128]{1,0:T(8,128)(2,1)}, bf16[128,1152]{1,0:T(8,128)(2,1)}) custom-call(bf16[64,128]{1,0:T(8,128)(2,1)} %bitcast.24, bf16[64,128]{1,0:T(8,128)(2,1)} %bitcast.25, bf16[64,128]{1,0:T(8,128)(2,1)} %bitcast.26, bf16[64,128]{1,0:T(8,128)(2,1)} %bitcast.27, bf16[64,128]{1,0:T(8,128)(2,1)} %bitcast.28, bf16[64,128]{1,0:T(8,128)(2,1)} %bitcast.29, ...), custom_call_target="tpu_custom_call" | custom-call | tf_op jit(solution)/shard_map/pallas_call | solution.py:132
  2.8 0.0 copy-start.1
  2.8 2.4 %all-gather = bf16[768,128]{1,0:T(8,128)(2,1)S(1)} all-gather(bf16[384,128]{1,0:T(8,128)(2,1)} %get-tuple-element.31), channel_id=2, replica_groups=mesh['row'=8,'col'=2,'ch'=2] {'ch'}, dimensions={0}, use_global_device_ids=true | all-gather | bytes 294912 | tf_op jit(solution)/shard_map/all_gather | solution.py:435
  5.2 0.0 copy-done.1
  5.2 0.5 shard_map.144
  5.6 24.3 %all_to_all.30.arrived = bf16[32,8,1152]{2,1,0:T(8,128)(2,1)S(1)} all-to-all(bf16[32,8,1152]{2,1,0:T(8,128)(2,1)S(1)} %shard_map.144), channel_id=1, replica_groups=mesh['row'=8,'col'=2,'ch'=2] {'col','row','ch'}, dimensions={0} | all-to-all | bytes 1179648 | tf_op jit(solution)/shard_map/all_to_all | solution.py:442
  30.0 2.3 %shard_map.145 = (bf16[32,4,1152]{2,1,0:T(4,128)(2,1)}, bf16[8,192,192]{2,1,0:T(8,128)(2,1)S(1)}) custom-call(bf16[32,8,1152]{2,1,0:T(8,128)(2,1)S(1)} %all_to_all.30.arrived), custom_call_target="tpu_custom_call" | custom-call | tf_op jit(solution)/shard_map/pallas_call | solution.py:132
  32.2 0.0 copy-start.2
  32.2 2.7 %all-to-all-start.1 = ((bf16[32,4,1152]{2,1,0:T(4,128)(2,1)}), bf16[32,4,1152]{2,1,0:T(4,128)(2,1)S(1)}, u32[]{:S(2)}, u32[]{:S(2)}) async-start(bf16[32,4,1152]{2,1,0:T(4,128)(2,1)} %get-tuple-element.32), calls=%async_computation.1 | async-start | bytes 589824 | tf_op jit(solution)/shard_map/all_to_all | solution.py:450
  34.9 0.0 copy-done.2
  35.0 0.2 collective-permute-start
  35.2 1.3 %collective-permute-done.other_far = bf16[12,64,96]{2,1,0:T(8,128)(2,1)S(1)} collective-permute-done((bf16[12,64,96]{2,1,0:T(8,128)(2,1)S(1)}, bf16[12,64,96]{2,1,0:T(8,128)(2,1)S(1)}, u32[]{:S(2)}, u32[]{:S(2)}) %collective-permute-start) | collective-permute-done | bytes 147488 | tf_op jit(solution)/shard_map/ppermute | solution.py:438
  36.5 9.5 %all-to-all-done.1.arrived = bf16[32,4,1152]{2,1,0:T(4,128)(2,1)S(1)} async-done(((bf16[32,4,1152]{2,1,0:T(4,128)(2,1)}), bf16[32,4,1152]{2,1,0:T(4,128)(2,1)S(1)}, u32[]{:S(2)}, u32[]{:S(2)}) %all-to-all-start.1) | async-done | bytes 294944 | tf_op jit(solution)/shard_map/all_to_all | solution.py:450
  45.9 1.9 %shard_map.146 = (bf16[32,4,1152]{2,1,0:T(4,128)(2,1)S(1)}, bf16[128,1152]{1,0:T(8,128)(2,1)S(1)}, f32[2,128,128]{2,1,0:T(8,128)S(1)}, bf16[12,64,96]{2,1,0:T(8,128)(2,1)S(1)}, bf16[12,64,96]{2,1,0:T(8,128)(2,1)S(1)}) custom-call(bf16[32,4,1152]{2,1,0:T(4,128)(2,1)S(1)} %all-to-all-done.1.arrived, bf16[2,384,128]{2,1,0:T(8,128)(2,1)S(1)} %bitcast.19, ...), custom_call_target="tpu_custom_call" | custom-call | tf_op jit(solution)/shard_map/pallas_call | solution.py:132
  47.8 13.2 %all_to_all.31.arrived = bf16[32,4,1152]{2,1,0:T(4,128)(2,1)S(1)} all-to-all(bf16[32,4,1152]{2,1,0:T(4,128)(2,1)S(1)} %get-tuple-element.33), channel_id=1, replica_groups=mesh['row'=8,'col'=2,'ch'=2] {'col','row','ch'}, dimensions={0} | all-to-all | bytes 589824 | tf_op jit(solution)/shard_map/all_to_all | solution.py:471
  61.0 2.4 %shard_map.147 = bf16[32,8,1152]{2,1,0:T(8,128)(2,1)} custom-call(bf16[32,4,1152]{2,1,0:T(4,128)(2,1)S(1)} %all_to_all.31.arrived, bf16[8,192,192]{2,1,0:T(8,128)(2,1)S(1)} %get-tuple-element.34.kept_far), custom_call_target="tpu_custom_call" | custom-call | tf_op jit(solution)/shard_map/pallas_call | solution.py:132
  63.5 2.6 %all-to-all-start.3 = ((bf16[32,8,1152]{2,1,0:T(8,128)(2,1)}), bf16[32,8,1152]{2,1,0:T(8,128)(2,1)S(1)}, u32[]{:S(2)}, u32[]{:S(2)}) async-start(bf16[32,8,1152]{2,1,0:T(8,128)(2,1)} %shard_map.147), calls=%async_computation.3 | async-start | bytes 1179648 | tf_op jit(solution)/shard_map/all_to_all | solution.py:480
  66.1 0.0 copy-start
  66.1 0.2 collective-permute-start.1
  66.3 1.3 %collective-permute-done.1.other = bf16[12,64,96]{2,1,0:T(8,128)(2,1)S(1)} collective-permute-done((bf16[12,64,96]{2,1,0:T(8,128)(2,1)S(1)}, bf16[12,64,96]{2,1,0:T(8,128)(2,1)S(1)}, u32[]{:S(2)}, u32[]{:S(2)}) %collective-permute-start.1) | collective-permute-done | bytes 147488 | tf_op jit(solution)/shard_map/ppermute | solution.py:472
  67.6 0.8 shard_map.148
  68.4 15.0 %all-to-all-done.3.arrived = bf16[32,8,1152]{2,1,0:T(8,128)(2,1)S(1)} async-done(((bf16[32,8,1152]{2,1,0:T(8,128)(2,1)}), bf16[32,8,1152]{2,1,0:T(8,128)(2,1)S(1)}, u32[]{:S(2)}, u32[]{:S(2)}) %all-to-all-start.3) | async-done | bytes 589856 | tf_op jit(solution)/shard_map/all_to_all | solution.py:480
  83.4 0.0 copy-done
  83.4 1.7 %shard_map.149 = (bf16[32,24,128]{2,1,0:T(8,128)(2,1)S(1)}, bf16[12,64,96]{2,1,0:T(8,128)(2,1)S(1)}, bf16[12,64,96]{2,1,0:T(8,128)(2,1)S(1)}) custom-call(bf16[32,8,1152]{2,1,0:T(8,128)(2,1)S(1)} %all-to-all-done.3.arrived, bf16[2,384,128]{2,1,0:T(8,128)(2,1)S(1)} %bitcast.20, bf16[24,96,128]{2,1,0:T(8,128)(2,1)S(1)} %copy-done, ...), custom_call_target="tpu_custom_call" | custom-call | tf_op jit(solution)/shard_map/pallas_call | solution.py:132
  85.2 11.8 %all_to_all.32.arrived = bf16[32,24,128]{2,1,0:T(8,128)(2,1)S(1)} all-to-all(bf16[32,24,128]{2,1,0:T(8,128)(2,1)S(1)} %get-tuple-element.41), channel_id=1, replica_groups=mesh['row'=8,'col'=2,'ch'=2] {'ch','row','col'}, dimensions={0} | all-to-all | bytes 393216 | tf_op jit(solution)/shard_map/all_to_all | solution.py:499
  96.9 0.7 shard_map.150
  97.6 3.5 %all-to-all-start.5 = ((bf16[16,24,128]{2,1,0:T(8,128)(2,1)}), bf16[16,24,128]{2,1,0:T(8,128)(2,1)S(1)}, u32[]{:S(2)}, u32[]{:S(2)}) async-start(bf16[16,24,128]{2,1,0:T(8,128)(2,1)} %shard_map.150), calls=%async_computation.5 | async-start | bytes 196608 | tf_op jit(solution)/shard_map/all_to_all | solution.py:504
  101.1 0.1 collective-permute-start.2
  101.2 1.4 %collective-permute-done.2.other = bf16[12,64,96]{2,1,0:T(8,128)(2,1)S(1)} collective-permute-done((bf16[12,64,96]{2,1,0:T(8,128)(2,1)S(1)}, bf16[12,64,96]{2,1,0:T(8,128)(2,1)S(1)}, u32[]{:S(2)}, u32[]{:S(2)}) %collective-permute-start.2) | collective-permute-done | bytes 147488 | tf_op jit(solution)/shard_map/ppermute | solution.py:500
  102.6 0.8 shard_map.151
  103.4 5.4 %all-to-all-done.5.sums = bf16[16,24,128]{2,1,0:T(8,128)(2,1)S(1)} async-done(((bf16[16,24,128]{2,1,0:T(8,128)(2,1)}), bf16[16,24,128]{2,1,0:T(8,128)(2,1)S(1)}, u32[]{:S(2)}, u32[]{:S(2)}) %all-to-all-start.5) | async-done | bytes 98336 | tf_op jit(solution)/shard_map/all_to_all | solution.py:504
  108.8 0.9 shard_map.152
  (1 shorter events, 0.0 us)
Async XLA Ops:
  2.8 2.4 %copy-start.1 = (bf16[128,1152]{1,0:T(8,128)(2,1)S(1)}, bf16[128,1152]{1,0:T(8,128)(2,1)}, u32[]{:S(2)}) copy-start(bf16[128,1152]{1,0:T(8,128)(2,1)} %get-tuple-element.30.normed.normed_far) | copy-start | bytes 884740
  32.2 2.7 %copy-start.2 = (bf16[24,96,64]{1,2,0:T(8,128)(2,1)S(1)}, bf16[24,96,64]{1,2,0:T(8,128)(2,1)}, u32[]{:S(2)}) copy-start(bf16[24,96,64]{1,2,0:T(8,128)(2,1)} %param.9) | copy-start | bytes 884740
  32.2 13.7 %all-to-all-start.1 = ((bf16[32,4,1152]{2,1,0:T(4,128)(2,1)}), bf16[32,4,1152]{2,1,0:T(4,128)(2,1)S(1)}, u32[]{:S(2)}, u32[]{:S(2)}) async-start(bf16[32,4,1152]{2,1,0:T(4,128)(2,1)} %get-tuple-element.32), calls=%async_computation.1 | async-start | bytes 589824 | tf_op jit(solution)/shard_map/all_to_all | solution.py:450
  35.0 1.5 %collective-permute-start = (bf16[12,64,96]{2,1,0:T(8,128)(2,1)S(1)}, bf16[12,64,96]{2,1,0:T(8,128)(2,1)S(1)}, u32[]{:S(2)}, u32[]{:S(2)}) collective-permute-start(bf16[12,64,96]{2,1,0:T(8,128)(2,1)S(1)} %dynamic-slice_bitcast_fusion), channel_id=1, source_target_pairs={{0,1},{1,0},{2,3},{3,2},{4,5},{5,4},{6,7},{7,6},{8,9},{9,8},{10,11... | collective-permute-start | bytes 442376 | tf_op jit(solution)/shard_map/ppermute | solution.py:438
  63.5 20.0 %all-to-all-start.3 = ((bf16[32,8,1152]{2,1,0:T(8,128)(2,1)}), bf16[32,8,1152]{2,1,0:T(8,128)(2,1)S(1)}, u32[]{:S(2)}, u32[]{:S(2)}) async-start(bf16[32,8,1152]{2,1,0:T(8,128)(2,1)} %shard_map.147), calls=%async_computation.3 | async-start | bytes 1179648 | tf_op jit(solution)/shard_map/all_to_all | solution.py:480
  66.1 17.3 %copy-start = (bf16[24,96,128]{2,1,0:T(8,128)(2,1)S(1)}, bf16[24,96,128]{2,1,0:T(8,128)(2,1)}, u32[]{:S(2)}) copy-start(bf16[24,96,128]{2,1,0:T(8,128)(2,1)} %pair_far.3) | copy-start | bytes 1769476
  66.1 1.5 %collective-permute-start.1 = (bf16[12,64,96]{2,1,0:T(8,128)(2,1)S(1)}, bf16[12,64,96]{2,1,0:T(8,128)(2,1)S(1)}, u32[]{:S(2)}, u32[]{:S(2)}) collective-permute-start(bf16[12,64,96]{2,1,0:T(8,128)(2,1)S(1)} %get-tuple-element.36), channel_id=1, source_target_pairs={{0,1},{1,0},{2,3},{3,2},{4,5},{5,4},{6,7},{7,6},{8,9},{9,8},{10,11... | collective-permute-start | bytes 442376 | tf_op jit(solution)/shard_map/ppermute | solution.py:472
  97.6 11.1 %all-to-all-start.5 = ((bf16[16,24,128]{2,1,0:T(8,128)(2,1)}), bf16[16,24,128]{2,1,0:T(8,128)(2,1)S(1)}, u32[]{:S(2)}, u32[]{:S(2)}) async-start(bf16[16,24,128]{2,1,0:T(8,128)(2,1)} %shard_map.150), calls=%async_computation.5 | async-start | bytes 196608 | tf_op jit(solution)/shard_map/all_to_all | solution.py:504
  101.1 1.5 %collective-permute-start.2 = (bf16[12,64,96]{2,1,0:T(8,128)(2,1)S(1)}, bf16[12,64,96]{2,1,0:T(8,128)(2,1)S(1)}, u32[]{:S(2)}, u32[]{:S(2)}) collective-permute-start(bf16[12,64,96]{2,1,0:T(8,128)(2,1)S(1)} %get-tuple-element.43), channel_id=1, source_target_pairs={{0,1},{1,0},{2,3},{3,2},{4,5},{5,4},{6,7},{7,6},{8,9},{9,8},{10,11... | collective-permute-start | bytes 442376 | tf_op jit(solution)/shard_map/ppermute | solution.py:500
where the time goes:
time: 110 us
  blocking collectives  51.7 us (47%)
  waiting for transfers between devices  33.9 us (31%)
  Pallas kernels  14 us (13%)
  starting transfers between devices  9.29 us (8%)
    all_to_all x2, blocking collectives, by_channels(): arrived = lax.all_to_all(send, everyone, 0, 0)  37.5 us
    all_to_all x2, waiting for transfers between devices, by_channels(): arrived = lax.all_to_all(send, everyone, 0, 0)  24.5 us
    pallas_call x10, Pallas kernels, call(): pl.pallas_call(kernel, out_shape=tuple((jax.ShapeDtypeStruct(*out) for ou...  14 us
    all_to_all x1, blocking collectives, by_channels(): arrived = lax.all_to_all(send, ('ch', 'row', 'col'), 0, 0)  11.8 us
    all_to_all x1, waiting for transfers between devices, by_channels(): sums = lax.all_to_all(sums, ('row', 'col'), 0, 0)  5.36 us
    all_to_all x2, starting transfers between devices, by_channels(): arrived = lax.all_to_all(send, everyone, 0, 0)  5.35 us
    all_to_all x1, starting transfers between devices, by_channels(): sums = lax.all_to_all(sums, ('row', 'col'), 0, 0)  3.51 us
    all_gather x1, blocking collectives, by_channels(): weights = lax.all_gather(weights, 'ch')  2.39 us
  transfers between devices with their start and end apart: 6, of which 6 were waited for; matrix products, arithmetic and copies ran while one was open for 0% of the time, Pallas kernels for 1%

commit v1 on v0

--- a/solution.py
+++ b/solution.py
@@ -192,10 +192,13 @@
     return centred * rstd, rstd
 
 
-def edges(width, normed, weights, send):
-    gate = jax.nn.sigmoid(dot(rows_of(weights, 0, width), normed[...], (1, 0)))
-    value = dot(rows_of(weights, width, width), normed[...], (1, 0))
-    send[...] = (gate * value).reshape(send.shape).astype(bf16)
+def edges(width, normed, weights, *sends):
+    for c, send in enumerate(sends):
+        gate = jax.nn.sigmoid(dot(weights[c, :width], normed[...], (1, 0)))
+        edge = gate * dot(weights[c, width : 2 * width], normed[...], (1, 0))
+        q = send.shape[1]
+        for s in range(send.shape[0]):
+            send[s] = edge[s * q : (s + 1) * q].astype(bf16)
 
 
 def spread_rows(block, cols, arrived, held):
@@ -275,13 +278,13 @@
 
 
 def head(
-    width, scale, arrived, weights, normed_far, own_far, other_far,
-    send, d_gate, terms, updated_own, updated_other,
-    normed, own, other, upstream, arrivals,
+    width, scale, first, second, weights, normed_far, own_far, other_far,
+    first_send, second_send, d_gate, terms, updated_own, updated_other,
+    normed, own, other, upstream, mixed, arrivals,
 ):
     parts, total, _ = weights.shape
     hidden = (total - 2 * width) // 2
-    devices, q, flat = arrived.shape
+    devices, q, flat = first.shape
     count, _, cols = other.shape
     core = lax.axis_index("ch")
     copies = [
@@ -290,7 +293,11 @@
         pltpu.make_async_copy(other_far, other, arrivals.at[2]),
     ]
     start_all(copies)
-    mixed = jnp.concatenate([arrived[s].astype(f32) for s in range(devices)], 0)
+    for c, arrived in enumerate((first, second)):
+        for s in range(devices):
+            start = (c * devices + s) * q
+            mixed[start : start + q] = arrived[s].astype(f32)
+    mixed = mixed[...]
     average = jnp.mean(mixed, 0, keepdims=True)
     spread = jnp.mean(mixed * mixed, 0, keepdims=True) - average * average
     inverse = lax.rsqrt(spread + epsilon)
@@ -313,8 +320,10 @@
         - jnp.mean(d_norm, 0, keepdims=True)
         - hat * jnp.mean(d_norm * hat, 0, keepdims=True)
     )
-    for s in range(devices):
-        send[s] = d_mixed[s * q : (s + 1) * q].astype(bf16)
+    for c, send in enumerate((first_send, second_send)):
+        for s in range(devices):
+            start = (c * devices + s) * q
+            send[s] = d_mixed[start : start + q].astype(bf16)
     by_gate = dot(d_gate[...], normed[...], (1, 1)) * scale
     by_out = dot(d_proj, hat_rounded, (1, 1)) * scale
     for c in range(parts):
@@ -324,13 +333,13 @@
 
 
 def tail(
-    width, scale, arrived, weights, pair_far, d_gate_far, head_terms,
+    width, scale, first, second, weights, pair_far, d_gate_far, head_terms,
     send, grad_own, grad_other,
     pair, d_gate, whole, arrivals,
 ):
     parts, total, channels = weights.shape
     hidden = (total - 2 * width) // 2
-    devices, q, flat = arrived.shape
+    devices = first.shape[0]
     count, cols, _ = pair.shape
     core = lax.axis_index("ch")
     copies = [
@@ -344,7 +353,7 @@
     w_gate, w_value = rows_of(weights, 0, width), rows_of(weights, width, width)
     gate = jax.nn.sigmoid(dot(w_gate, normed, (1, 0)))
     value = dot(w_value, normed, (1, 0))
-    grad = arrived[...].astype(f32).reshape(devices * q, flat)
+    grad = jnp.concatenate([part[s].astype(f32) for part in (first, second) for s in range(devices)], 0)
     by_value = grad * gate
     by_gate = (by_value * (value * (1.0 - gate))).astype(bf16)
     by_value = by_value.astype(bf16)
@@ -410,7 +419,7 @@
     hidden = w_gate_a.shape[1]
     parts, col_parts, row_parts = lax.axis_size("ch"), lax.axis_size("col"), lax.axis_size("row")
     devices = parts * col_parts * row_parts
-    share = hidden * parts // devices
+    share = hidden // devices
     width = 2 * hidden
     count = row_count // parts
     flat = count * cols
@@ -436,65 +445,70 @@
     own = jnp.swapaxes(cotangent, 1, 2)
     other = lax.dynamic_slice_in_dim(own, (1 - lax.axis_index("ch")) * count, count, 0)
     other = lax.ppermute(other, "ch", swap)
-    (send,) = call(
-        functools.partial(edges, width), [((devices, 2 * share, flat), bf16)], (normed, weights)
-    )
-    arrived = lax.all_to_all(send, everyone, 0, 0)
+    edge = ((devices, 2 * share, flat), bf16)
+    block = ((devices, share, flat), bf16)
+    sends = call(functools.partial(edges, width), [edge] * parts, (normed, weights))
+    arrived = [lax.all_to_all(send, everyone, 0, 0) for send in sends]
     room = pltpu.VMEM((col_parts * tokens * 8, -(-cols // 128) * 128), f32)
-    send, kept = call(
-        functools.partial(mix, col_parts, cols),
-        [((devices, share, flat), bf16), ((2 * share, tokens, tokens), bf16)],
-        (arrived,),
-        (room, room),
-    )
-    arrived = lax.all_to_all(send, everyone, 0, 0)
+    kept = [None] * parts
+    for c in range(parts):
+        send, kept[c] = call(
+            functools.partial(mix, col_parts, cols),
+            [block, ((2 * share, tokens, tokens), bf16)],
+            (arrived[c],),
+            (room, room),
+        )
+        arrived[c] = lax.all_to_all(send, everyone, 0, 0)
     part = ((count, hidden, cols), bf16)
-    send, d_gate, head_terms, updated_own, updated_other = call(
+    *sends, d_gate, head_terms, updated_own, updated_other = call(
         functools.partial(head, width, scale),
         [
-            ((devices, share, flat), bf16),
+            block,
+            block,
             ((hidden * parts, flat), bf16),
             ((parts, 2 * hidden, channels), f32),
             part,
             part,
         ],
-        (arrived, weights, normed, own, other),
+        (*arrived, weights, normed, own, other),
         (
             pltpu.VMEM((channels, flat), bf16),
             pltpu.VMEM(*part),
             pltpu.VMEM(*part),
             pltpu.VMEM((hidden * parts, flat), f32),
+            pltpu.VMEM((hidden * parts, flat), f32),
             pltpu.SemaphoreType.DMA((3,)),
         ),
-        far=(2, 3, 4),
-    )
-    arrived = lax.all_to_all(send, everyone, 0, 0)
+        far=(3, 4, 5),
+    )
+    arrived = [lax.all_to_all(send, everyone, 0, 0) for send in sends]
     updated_other = lax.ppermute(updated_other, "ch", swap)
-    (send,) = call(
-        functools.partial(unmix, col_parts, cols),
-        [((devices, 2 * share, flat), bf16)],
-        (arrived, kept),
-        (room, room, pltpu.VMEM(kept.shape, bf16), pltpu.SemaphoreType.DMA),
-        far=(1,),
-    )
-    arrived = lax.all_to_all(send, everyone, 0, 0)
+    for c in range(parts):
+        (send,) = call(
+            functools.partial(unmix, col_parts, cols),
+            [edge],
+            (arrived[c], kept[c]),
+            (room, room, pltpu.VMEM(kept[c].shape, bf16), pltpu.SemaphoreType.DMA),
+            far=(1,),
+        )
+        arrived[c] = lax.all_to_all(send, everyone, 0, 0)
     rows = [((row_count, hidden, cols), bf16)]
     two = pltpu.SemaphoreType.DMA((2,))
     (updated,) = call(join_rows, rows, (updated_own, updated_other), (two,), (0, 1), True)
-    arrived, updated = lax.optimization_barrier((arrived, updated))
+    arrived[-1], updated = lax.optimization_barrier((arrived[-1], updated))
     total = 2 * width + 2 * hidden
     per = total * parts // devices
     send, grad_own, grad_other = call(
         functools.partial(tail, width, scale),
         [((devices, per, channels), bf16), part, part],
-        (arrived, weights, pair, d_gate, head_terms),
+        (*arrived, weights, pair, d_gate, head_terms),
         (
             pltpu.VMEM((count, cols, channels), bf16),
             pltpu.VMEM((hidden * parts, flat), bf16),
             pltpu.VMEM((total * parts, channels), f32),
             two,
         ),
-        far=(2, 3),
+        far=(3, 4),
     )
     arrived = lax.all_to_all(send, ("ch", "row", "col"), 0, 0)
     grad_other = lax.ppermute(grad_other, "ch", swap)
@@ -521,11 +535,11 @@
     row_count, cols, _ = arrays[0].shape
     parts, devices = lax.axis_size("ch"), lax.axis_size(everyone)
     hidden = arrays[2].shape[1]
-    share = hidden * parts // devices
+    share = hidden // devices
     fits = (
-        share * devices == hidden * parts
+        share * devices == hidden
         and parts == 2
-        and 2 * share == 8
+        and 1 <= share <= 4
         and row_count % parts == 0
         and 6 * hidden * parts % devices == 0
         and arrays[1].shape[2] == hidden

time: 110 us -> 138 us (1.25)
  waiting for transfers between devices: 33.9 us -> 56.6 us
  starting transfers between devices: 9.29 us -> 19.6 us
  blocking collectives: 51.7 us -> 42.5 us
  Pallas kernels: 14 us -> 17.9 us
    all_to_all x2 -> x6, waiting for transfers between devices: 24.5 us -> 47.1 us  [the longest x4 31.4 us: by_channels(): arrived[c] = lax.all_to_all(send, everyone, 0, 0)]
    all_to_all x2 -> x6, starting transfers between devices: 5.35 us -> 15.6 us  [the longest x4 10.5 us: by_channels(): arrived[c] = lax.all_to_all(send, everyone, 0, 0)]
    all_to_all x2, blocking collectives: 37.5 us -> 28.1 us  [by_channels(): arrived = [lax.all_to_all(send, everyone, 0, 0) for send in sends]]
    pallas_call x10 -> x12, Pallas kernels: 14 us -> 17.9 us  [call(): pl.pallas_call(kernel, out_shape=tuple((jax.ShapeDtypeStruct(*out) for ou...]
  transfers between devices with their start and end apart: 6 -> 10, of which waited for: 6 -> 10; matrix products, arithmetic and copies ran while one was open for 0% -> 0% of each run, Pallas kernels for 1% -> 6%
where the time goes in v1:
time: 138 us; the launch traced here: 137 us
  waiting for transfers between devices  56.6 us (41%)
  blocking collectives  42.5 us (31%)
  starting transfers between devices  19.6 us (14%)
  Pallas kernels  17.9 us (13%)
    all_to_all x4, waiting for transfers between devices, by_channels(): arrived[c] = lax.all_to_all(send, everyone, 0, 0)  31.4 us
    all_to_all x2, blocking collectives, by_channels(): arrived = [lax.all_to_all(send, everyone, 0, 0) for send in sends]  28.1 us
    pallas_call x12, Pallas kernels, call(): pl.pallas_call(kernel, out_shape=tuple((jax.ShapeDtypeStruct(*out) for ou...  17.9 us
    all_to_all x2, waiting for transfers between devices, by_channels(): arrived = [lax.all_to_all(send, everyone, 0, 0) for send in sends]  15.8 us
    all_to_all x1, blocking collectives, by_channels(): arrived = lax.all_to_all(send, ('ch', 'row', 'col'), 0, 0)  12 us
    all_to_all x4, starting transfers between devices, by_channels(): arrived[c] = lax.all_to_all(send, everyone, 0, 0)  10.5 us
    all_to_all x1, waiting for transfers between devices, by_channels(): sums = lax.all_to_all(sums, ('row', 'col'), 0, 0)  5.36 us
    all_to_all x2, starting transfers between devices, by_channels(): arrived = [lax.all_to_all(send, everyone, 0, 0) for send in sends]  5.17 us
  transfers between devices with their start and end apart: 10, of which 10 were waited for; matrix products, arithmetic and copies ran while one was open for 0% of the time, Pallas kernels for 6%

profile of v1, /device:TPU:0, one launch (start us, length us, event | category | flops | bytes accessed | tf_op | source)
XLA Modules:
  0.0 137.5 jit_solution(10364163345135634985)
XLA Ops:
  0.6 2.1 %shard_map.143 = (bf16[384,128]{1,0:T(8,128)(2,1)}, bf16[128,1152]{1,0:T(8,128)(2,1)}) custom-call(bf16[64,128]{1,0:T(8,128)(2,1)} %bitcast.24, bf16[64,128]{1,0:T(8,128)(2,1)} %bitcast.25, bf16[64,128]{1,0:T(8,128)(2,1)} %bitcast.26, bf16[64,128]{1,0:T(8,128)(2,1)} %bitcast.27, bf16[64,128]{1,0:T(8,128)(2,1)} %bitcast.28, bf16[64,128]{1,0:T(8,128)(2,1)} %bitcast.29, ...), custom_call_target="tpu_custom_call" | custom-call | tf_op jit(solution)/shard_map/pallas_call | solution.py:132
  2.8 0.0 copy-start.1
  2.8 2.4 %all-gather = bf16[768,128]{1,0:T(8,128)(2,1)S(1)} all-gather(bf16[384,128]{1,0:T(8,128)(2,1)} %get-tuple-element.36), channel_id=2, replica_groups=mesh['row'=8,'col'=2,'ch'=2] {'ch'}, dimensions={0}, use_global_device_ids=true | all-gather | bytes 294912 | tf_op jit(solution)/shard_map/all_gather | solution.py:444
  5.2 0.0 copy-done.1
  5.2 1.1 shard_map.144
  6.2 18.0 %all_to_all.50.arrived = bf16[32,4,1152]{2,1,0:T(4,128)(2,1)S(1)} all-to-all(bf16[32,4,1152]{2,1,0:T(4,128)(2,1)S(1)} %get-tuple-element.39), channel_id=1, replica_groups=mesh['row'=8,'col'=2,'ch'=2] {'col','row','ch'}, dimensions={0} | all-to-all | bytes 589824 | tf_op jit(solution)/shard_map/all_to_all | solution.py:451
  24.2 2.6 %all-to-all-start = ((bf16[32,4,1152]{2,1,0:T(4,128)(2,1)}), bf16[32,4,1152]{2,1,0:T(4,128)(2,1)S(1)}, u32[]{:S(2)}, u32[]{:S(2)}) async-start(bf16[32,4,1152]{2,1,0:T(4,128)(2,1)} %get-tuple-element.37), calls=%async_computation | async-start | bytes 589824 | tf_op jit(solution)/shard_map/all_to_all | solution.py:451
  26.8 1.6 %shard_map.146 = (bf16[32,2,1152]{2,1,0:T(2,128)(2,1)}, bf16[4,192,192]{2,1,0:T(8,128)(2,1)S(1)}) custom-call(bf16[32,4,1152]{2,1,0:T(4,128)(2,1)S(1)} %all_to_all.50.arrived), custom_call_target="tpu_custom_call" | custom-call | tf_op jit(solution)/shard_map/pallas_call | solution.py:132
  28.4 9.4 %all-to-all-done.arrived = bf16[32,4,1152]{2,1,0:T(4,128)(2,1)S(1)} async-done(((bf16[32,4,1152]{2,1,0:T(4,128)(2,1)}), bf16[32,4,1152]{2,1,0:T(4,128)(2,1)S(1)}, u32[]{:S(2)}, u32[]{:S(2)}) %all-to-all-start) | async-done | bytes 294944 | tf_op jit(solution)/shard_map/all_to_all | solution.py:451
  37.8 0.0 copy-start.2
  37.8 2.7 %all-to-all-start.3 = ((bf16[32,2,1152]{2,1,0:T(2,128)(2,1)}), bf16[32,2,1152]{2,1,0:T(2,128)(2,1)S(1)}, u32[]{:S(2)}, u32[]{:S(2)}) async-start(bf16[32,2,1152]{2,1,0:T(2,128)(2,1)} %get-tuple-element.40), calls=%async_computation.3 | async-start | bytes 294912 | tf_op jit(solution)/shard_map/all_to_all | solution.py:461
  40.5 1.6 %shard_map.145 = (bf16[32,2,1152]{2,1,0:T(2,128)(2,1)}, bf16[4,192,192]{2,1,0:T(8,128)(2,1)S(1)}) custom-call(bf16[32,4,1152]{2,1,0:T(4,128)(2,1)S(1)} %all-to-all-done.arrived), custom_call_target="tpu_custom_call" | custom-call | tf_op jit(solution)/shard_map/pallas_call | solution.py:132
  42.2 6.8 %all-to-all-done.3.second = bf16[32,2,1152]{2,1,0:T(2,128)(2,1)S(1)} async-done(((bf16[32,2,1152]{2,1,0:T(2,128)(2,1)}), bf16[32,2,1152]{2,1,0:T(2,128)(2,1)S(1)}, u32[]{:S(2)}, u32[]{:S(2)}) %all-to-all-start.3) | async-done | bytes 147488 | tf_op jit(solution)/shard_map/all_to_all | solution.py:461
  48.9 2.6 %all-to-all-start.1 = ((bf16[32,2,1152]{2,1,0:T(2,128)(2,1)}), bf16[32,2,1152]{2,1,0:T(2,128)(2,1)S(1)}, u32[]{:S(2)}, u32[]{:S(2)}) async-start(bf16[32,2,1152]{2,1,0:T(2,128)(2,1)} %get-tuple-element.38), calls=%async_computation.1 | async-start | bytes 294912 | tf_op jit(solution)/shard_map/all_to_all | solution.py:461
  51.5 0.0 copy-done.2
  51.6 0.2 collective-permute-start
  51.7 1.3 collective-permute-done.other_far
  53.1 6.9 %all-to-all-done.1.first = bf16[32,2,1152]{2,1,0:T(2,128)(2,1)S(1)} async-done(((bf16[32,2,1152]{2,1,0:T(2,128)(2,1)}), bf16[32,2,1152]{2,1,0:T(2,128)(2,1)S(1)}, u32[]{:S(2)}, u32[]{:S(2)}) %all-to-all-start.1) | async-done | bytes 147488 | tf_op jit(solution)/shard_map/all_to_all | solution.py:461
  59.9 2.6 %shard_map.147 = (bf16[32,2,1152]{2,1,0:T(2,128)(2,1)}, bf16[32,2,1152]{2,1,0:T(2,128)(2,1)S(1)}, bf16[128,1152]{1,0:T(8,128)(2,1)S(1)}, f32[2,128,128]{2,1,0:T(...) custom-call(bf16[32,2,1152]{2,1,0:T(2,128)(2,1)S(1)} %all-to-all-done.1.first, ...), custom_call_target="tpu_custom_call" | custom-call | tf_op jit(solution)/shard_map/pallas_call | solution.py:132
  62.6 10.2 %all_to_all.51.arrived = bf16[32,2,1152]{2,1,0:T(2,128)(2,1)S(1)} all-to-all(bf16[32,2,1152]{2,1,0:T(2,128)(2,1)S(1)} %get-tuple-element.41), channel_id=1, replica_groups=mesh['row'=8,'col'=2,'ch'=2] {'col','row','ch'}, dimensions={0} | all-to-all | bytes 294912 | tf_op jit(solution)/shard_map/all_to_all | solution.py:484
  72.7 2.6 %all-to-all-start.6 = ((bf16[32,2,1152]{2,1,0:T(2,128)(2,1)}), bf16[32,2,1152]{2,1,0:T(2,128)(2,1)S(1)}, u32[]{:S(2)}, u32[]{:S(2)}) async-start(bf16[32,2,1152]{2,1,0:T(2,128)(2,1)} %get-tuple-element.46), calls=%async_computation.6 | async-start | bytes 294912 | tf_op jit(solution)/shard_map/all_to_all | solution.py:484
  75.3 2.0 %shard_map.148 = bf16[32,4,1152]{2,1,0:T(4,128)(2,1)} custom-call(bf16[32,2,1152]{2,1,0:T(2,128)(2,1)S(1)} %all_to_all.51.arrived, bf16[4,192,192]{2,1,0:T(8,128)(2,1)S(1)} %get-tuple-element.42.kept_far), custom_call_target="tpu_custom_call" | custom-call | tf_op jit(solution)/shard_map/pallas_call | solution.py:132
  77.3 6.4 %all-to-all-done.6.arrived = bf16[32,2,1152]{2,1,0:T(2,128)(2,1)S(1)} async-done(((bf16[32,2,1152]{2,1,0:T(2,128)(2,1)}), bf16[32,2,1152]{2,1,0:T(2,128)(2,1)S(1)}, u32[]{:S(2)}, u32[]{:S(2)}) %all-to-all-start.6) | async-done | bytes 147488 | tf_op jit(solution)/shard_map/all_to_all | solution.py:484
  83.7 2.6 %all-to-all-start.5 = ((bf16[32,4,1152]{2,1,0:T(4,128)(2,1)}), bf16[32,4,1152]{2,1,0:T(4,128)(2,1)S(1)}, u32[]{:S(2)}, u32[]{:S(2)}) async-start(bf16[32,4,1152]{2,1,0:T(4,128)(2,1)} %shard_map.148), calls=%async_computation.5 | async-start | bytes 589824 | tf_op jit(solution)/shard_map/all_to_all | solution.py:494
  86.3 2.0 %shard_map.150 = bf16[32,4,1152]{2,1,0:T(4,128)(2,1)} custom-call(bf16[32,2,1152]{2,1,0:T(2,128)(2,1)S(1)} %all-to-all-done.6.arrived, bf16[4,192,192]{2,1,0:T(8,128)(2,1)S(1)} %get-tuple-element.47.kept_far), custom_call_target="tpu_custom_call" | custom-call | tf_op jit(solution)/shard_map/pallas_call | solution.py:132
  88.3 0.0 copy-start
  88.4 9.0 %all-to-all-done.5.second = bf16[32,4,1152]{2,1,0:T(4,128)(2,1)S(1)} async-done(((bf16[32,4,1152]{2,1,0:T(4,128)(2,1)}), bf16[32,4,1152]{2,1,0:T(4,128)(2,1)S(1)}, u32[]{:S(2)}, u32[]{:S(2)}) %all-to-all-start.5) | async-done | bytes 294944 | tf_op jit(solution)/shard_map/all_to_all | solution.py:494
  97.3 2.6 %all-to-all-start.7 = ((bf16[32,4,1152]{2,1,0:T(4,128)(2,1)}), bf16[32,4,1152]{2,1,0:T(4,128)(2,1)S(1)}, u32[]{:S(2)}, u32[]{:S(2)}) async-start(bf16[32,4,1152]{2,1,0:T(4,128)(2,1)} %shard_map.150), calls=%async_computation.7 | async-start | bytes 589824 | tf_op jit(solution)/shard_map/all_to_all | solution.py:494
  99.9 0.2 collective-permute-start.1
  100.1 1.3 collective-permute-done.1.other
  101.4 0.8 shard_map.149
  102.2 8.7 %all-to-all-done.7.first = bf16[32,4,1152]{2,1,0:T(4,128)(2,1)S(1)} async-done(((bf16[32,4,1152]{2,1,0:T(4,128)(2,1)}), bf16[32,4,1152]{2,1,0:T(4,128)(2,1)S(1)}, u32[]{:S(2)}, u32[]{:S(2)}) %all-to-all-start.7) | async-done | bytes 294944 | tf_op jit(solution)/shard_map/all_to_all | solution.py:494
  110.9 0.0 copy-done
  110.9 1.8 %shard_map.151 = (bf16[32,24,128]{2,1,0:T(8,128)(2,1)S(1)}, bf16[12,64,96]{2,1,0:T(8,128)(2,1)S(1)}, bf16[12,64,96]{2,1,0:T(8,128)(2,1)S(1)}) custom-call(bf16[32,4,1152]{2,1,0:T(4,128)(2,1)S(1)} %all-to-all-done.7.first, bf16[32,4,1152]{2,1,0:T(4,128)(2,1)S(1)} %all-to-all-done.5.second, bf16[2,384,128]{2,1,0:T(8,128)(2,1)S(1)} %bitcast.20, ...), custom_call_target="tpu_custom_call" | custom-call | tf_op jit(solution)/shard_map/pallas_call | solution.py:132
  112.7 12.0 %all_to_all.52.arrived = bf16[32,24,128]{2,1,0:T(8,128)(2,1)S(1)} all-to-all(bf16[32,24,128]{2,1,0:T(8,128)(2,1)S(1)} %get-tuple-element.51), channel_id=1, replica_groups=mesh['row'=8,'col'=2,'ch'=2] {'ch','row','col'}, dimensions={0} | all-to-all | bytes 393216 | tf_op jit(solution)/shard_map/all_to_all | solution.py:513
  124.7 0.7 shard_map.152
  125.4 3.5 %all-to-all-start.9 = ((bf16[16,24,128]{2,1,0:T(8,128)(2,1)}), bf16[16,24,128]{2,1,0:T(8,128)(2,1)S(1)}, u32[]{:S(2)}, u32[]{:S(2)}) async-start(bf16[16,24,128]{2,1,0:T(8,128)(2,1)} %shard_map.152), calls=%async_computation.9 | async-start | bytes 196608 | tf_op jit(solution)/shard_map/all_to_all | solution.py:518
  128.9 0.1 collective-permute-start.2
  129.0 1.4 %collective-permute-done.2.other = bf16[12,64,96]{2,1,0:T(8,128)(2,1)S(1)} collective-permute-done((bf16[12,64,96]{2,1,0:T(8,128)(2,1)S(1)}, bf16[12,64,96]{2,1,0:T(8,128)(2,1)S(1)}, u32[]{:S(2)}, u32[]{:S(2)}) %collective-permute-start.2) | collective-permute-done | bytes 147488 | tf_op jit(solution)/shard_map/ppermute | solution.py:514
  130.4 0.8 shard_map.153
  131.2 5.4 %all-to-all-done.9.sums = bf16[16,24,128]{2,1,0:T(8,128)(2,1)S(1)} async-done(((bf16[16,24,128]{2,1,0:T(8,128)(2,1)}), bf16[16,24,128]{2,1,0:T(8,128)(2,1)S(1)}, u32[]{:S(2)}, u32[]{:S(2)}) %all-to-all-start.9) | async-done | bytes 98336 | tf_op jit(solution)/shard_map/all_to_all | solution.py:518
  136.5 0.9 shard_map.154
  (1 shorter events, 0.0 us)
Async XLA Ops:
  2.8 2.4 %copy-start.1 = (bf16[128,1152]{1,0:T(8,128)(2,1)S(1)}, bf16[128,1152]{1,0:T(8,128)(2,1)}, u32[]{:S(2)}) copy-start(bf16[128,1152]{1,0:T(8,128)(2,1)} %get-tuple-element.35.normed.normed_far) | copy-start | bytes 884740
  24.2 13.6 %all-to-all-start = ((bf16[32,4,1152]{2,1,0:T(4,128)(2,1)}), bf16[32,4,1152]{2,1,0:T(4,128)(2,1)S(1)}, u32[]{:S(2)}, u32[]{:S(2)}) async-start(bf16[32,4,1152]{2,1,0:T(4,128)(2,1)} %get-tuple-element.37), calls=%async_computation | async-start | bytes 589824 | tf_op jit(solution)/shard_map/all_to_all | solution.py:451
  37.8 13.7 %copy-start.2 = (bf16[24,96,64]{1,2,0:T(8,128)(2,1)S(1)}, bf16[24,96,64]{1,2,0:T(8,128)(2,1)}, u32[]{:S(2)}) copy-start(bf16[24,96,64]{1,2,0:T(8,128)(2,1)} %param.9) | copy-start | bytes 884740
  37.8 11.1 %all-to-all-start.3 = ((bf16[32,2,1152]{2,1,0:T(2,128)(2,1)}), bf16[32,2,1152]{2,1,0:T(2,128)(2,1)S(1)}, u32[]{:S(2)}, u32[]{:S(2)}) async-start(bf16[32,2,1152]{2,1,0:T(2,128)(2,1)} %get-tuple-element.40), calls=%async_computation.3 | async-start | bytes 294912 | tf_op jit(solution)/shard_map/all_to_all | solution.py:461
  48.9 11.0 %all-to-all-start.1 = ((bf16[32,2,1152]{2,1,0:T(2,128)(2,1)}), bf16[32,2,1152]{2,1,0:T(2,128)(2,1)S(1)}, u32[]{:S(2)}, u32[]{:S(2)}) async-start(bf16[32,2,1152]{2,1,0:T(2,128)(2,1)} %get-tuple-element.38), calls=%async_computation.1 | async-start | bytes 294912 | tf_op jit(solution)/shard_map/all_to_all | solution.py:461
  51.6 1.5 %collective-permute-start = (bf16[12,64,96]{2,1,0:T(8,128)(2,1)S(1)}, bf16[12,64,96]{2,1,0:T(8,128)(2,1)S(1)}, u32[]{:S(2)}, u32[]{:S(2)}) collective-permute-start(bf16[12,64,96]{2,1,0:T(8,128)(2,1)S(1)} %dynamic-slice_bitcast_fusion), channel_id=1, source_target_pairs={{0,1},{1,0},{2,3},{3,2},{4,5},{5,4},{6,7},{7,6},{8,9},{9,8},{10,11... | collective-permute-start | bytes 442376 | tf_op jit(solution)/shard_map/ppermute | solution.py:447
  72.7 11.0 %all-to-all-start.6 = ((bf16[32,2,1152]{2,1,0:T(2,128)(2,1)}), bf16[32,2,1152]{2,1,0:T(2,128)(2,1)S(1)}, u32[]{:S(2)}, u32[]{:S(2)}) async-start(bf16[32,2,1152]{2,1,0:T(2,128)(2,1)} %get-tuple-element.46), calls=%async_computation.6 | async-start | bytes 294912 | tf_op jit(solution)/shard_map/all_to_all | solution.py:484
  83.7 13.6 %all-to-all-start.5 = ((bf16[32,4,1152]{2,1,0:T(4,128)(2,1)}), bf16[32,4,1152]{2,1,0:T(4,128)(2,1)S(1)}, u32[]{:S(2)}, u32[]{:S(2)}) async-start(bf16[32,4,1152]{2,1,0:T(4,128)(2,1)} %shard_map.148), calls=%async_computation.5 | async-start | bytes 589824 | tf_op jit(solution)/shard_map/all_to_all | solution.py:494
  88.3 22.6 %copy-start = (bf16[24,96,128]{2,1,0:T(8,128)(2,1)S(1)}, bf16[24,96,128]{2,1,0:T(8,128)(2,1)}, u32[]{:S(2)}) copy-start(bf16[24,96,128]{2,1,0:T(8,128)(2,1)} %pair_far.3) | copy-start | bytes 1769476
  97.3 13.6 %all-to-all-start.7 = ((bf16[32,4,1152]{2,1,0:T(4,128)(2,1)}), bf16[32,4,1152]{2,1,0:T(4,128)(2,1)S(1)}, u32[]{:S(2)}, u32[]{:S(2)}) async-start(bf16[32,4,1152]{2,1,0:T(4,128)(2,1)} %shard_map.150), calls=%async_computation.7 | async-start | bytes 589824 | tf_op jit(solution)/shard_map/all_to_all | solution.py:494
  99.9 1.5 %collective-permute-start.1 = (bf16[12,64,96]{2,1,0:T(8,128)(2,1)S(1)}, bf16[12,64,96]{2,1,0:T(8,128)(2,1)S(1)}, u32[]{:S(2)}, u32[]{:S(2)}) collective-permute-start(bf16[12,64,96]{2,1,0:T(8,128)(2,1)S(1)} %get-tuple-element.44), channel_id=1, source_target_pairs={{0,1},{1,0},{2,3},{3,2},{4,5},{5,4},{6,7},{7,6},{8,9},{9,8},{10,11... | collective-permute-start | bytes 442376 | tf_op jit(solution)/shard_map/ppermute | solution.py:485
  125.4 11.1 %all-to-all-start.9 = ((bf16[16,24,128]{2,1,0:T(8,128)(2,1)}), bf16[16,24,128]{2,1,0:T(8,128)(2,1)S(1)}, u32[]{:S(2)}, u32[]{:S(2)}) async-start(bf16[16,24,128]{2,1,0:T(8,128)(2,1)} %shard_map.152), calls=%async_computation.9 | async-start | bytes 196608 | tf_op jit(solution)/shard_map/all_to_all | solution.py:518
  128.9 1.5 %collective-permute-start.2 = (bf16[12,64,96]{2,1,0:T(8,128)(2,1)S(1)}, bf16[12,64,96]{2,1,0:T(8,128)(2,1)S(1)}, u32[]{:S(2)}, u32[]{:S(2)}) collective-permute-start(bf16[12,64,96]{2,1,0:T(8,128)(2,1)S(1)} %get-tuple-element.53), channel_id=1, source_target_pairs={{0,1},{1,0},{2,3},{3,2},{4,5},{5,4},{6,7},{7,6},{8,9},{9,8},{10,11... | collective-permute-start | bytes 442376 | tf_op jit(solution)/shard_map/ppermute | solution.py:514

commit v2 on v0

--- a/solution.py
+++ b/solution.py
@@ -116,7 +116,8 @@
     )
 
 
-everyone = ("col", "row", "ch")
+everyone = ("ch", "col", "row")
+one_core = ("col", "row")
 f32, bf16 = jnp.float32, jnp.bfloat16
 
 
@@ -159,27 +160,6 @@
         copy.wait()
 
 
-def prepare(share, ga, pa, gb, pb, go, wo, pair_far, out, normed, gates, values, last, pair, arrivals):
-    hidden = go.shape[0]
-    count = pair.shape[0]
-    rows = pl.ds(lax.axis_index("ch") * count, count)
-    fetch = pltpu.make_async_copy(pair_far.at[rows], pair, arrivals.at[6])
-    fetch.start()
-    width = 2 * hidden
-    copies = []
-    for at, (held, low, high) in enumerate(((gates, ga, gb), (values, pa, pb), (last, go, wo))):
-        copies.append(pltpu.make_async_copy(low, held.at[0:hidden], arrivals.at[2 * at]))
-        copies.append(pltpu.make_async_copy(high, held.at[hidden:width], arrivals.at[2 * at + 1]))
-    start_all(copies)
-    order = grouping(hidden, share)
-    wait_all(copies)
-    out[:width] = dot(order, gates[...], (1, 0)).astype(bf16)
-    out[width : 2 * width] = dot(order, values[...], (1, 0)).astype(bf16)
-    out[2 * width :] = last[...]
-    fetch.wait()
-    normed[...] = normalized(pair[...])[0].astype(bf16)
-
-
 def rows_of(weights, start, count):
     return jnp.concatenate([weights[c, start : start + count] for c in range(weights.shape[0])], 0)
 
@@ -192,27 +172,64 @@
     return centred * rstd, rstd
 
 
-def edges(width, normed, weights, send):
-    gate = jax.nn.sigmoid(dot(rows_of(weights, 0, width), normed[...], (1, 0)))
-    value = dot(rows_of(weights, width, width), normed[...], (1, 0))
-    send[...] = (gate * value).reshape(send.shape).astype(bf16)
-
-
-def spread_rows(block, cols, arrived, held):
+def edges(
+    share, ga, pa, gb, pb, go, wo, pair_far, weights, normed, send,
+    gates, values, last, pair, both, arrivals,
+):
+    hidden = go.shape[0]
+    width = 2 * hidden
+    parts = both.shape[0]
+    flat = both.shape[2]
+    count = pair.shape[0] // parts
+    copies = []
+    for at, (held, low, high) in enumerate(((gates, ga, gb), (values, pa, pb), (last, go, wo))):
+        copies.append(pltpu.make_async_copy(low, held.at[0:hidden], arrivals.at[2 * at]))
+        copies.append(pltpu.make_async_copy(high, held.at[hidden:width], arrivals.at[2 * at + 1]))
+    rows = [pl.ds(c * count, count) for c in range(parts)]
+    fetches = [
+        pltpu.make_async_copy(pair_far.at[rows[c]], pair.at[rows[c]], arrivals.at[6 + c])
+        for c in range(parts)
+    ]
+    start_all(copies + fetches)
+    order = grouping(hidden, share)
+    wait_all(copies)
+    w_gate = dot(order, gates[...], (1, 0)).astype(bf16)
+    w_value = dot(order, values[...], (1, 0)).astype(bf16)
+    weights[:width] = w_gate
+    weights[width : 2 * width] = w_value
+    weights[2 * width :] = last[...]
+    for c, fetch in enumerate(fetches):
+        fetch.wait()
+        hat = normalized(pair[rows[c]])[0].astype(bf16)
+        both[c] = hat
+        edge = jax.nn.sigmoid(dot(w_gate, hat, (1, 0))) * dot(w_value, hat, (1, 0))
+        send[:, :, c * flat : (c + 1) * flat] = edge.reshape(
+            send.shape[0], send.shape[1], flat
+        ).astype(bf16)
+    normed[...] = both[lax.axis_index("ch")]
+
+
+def first_row(s, devices, cores, rows):
+    line = devices // cores
+    return (s % line) * cores * rows + (s // line) * rows
+
+
+def spread_rows(block, cores, cols, arrived, held):
     devices, q, flat = arrived.shape
     rows = flat // cols
     for s in range(devices):
         tile = arrived[s].astype(f32)
         for i in range(rows):
-            start = (s * rows + i) * block
+            start = (first_row(s, devices, cores, rows) + i) * block
             held[start : start + q, 0:cols] = tile[:, i * cols : (i + 1) * cols]
 
 
-def pack_rows(block, cols, held, send):
+def pack_rows(block, cores, cols, held, send):
     devices, q, flat = send.shape
     rows = flat // cols
     for s in range(devices):
-        starts = [(s * rows + i) * block for i in range(rows)]
+        first = first_row(s, devices, cores, rows)
+        starts = [(first + i) * block for i in range(rows)]
         whole = jnp.concatenate([held[start : start + block, 0:cols] for start in starts], axis=1)
         send[s] = whole[:q].astype(bf16)
 
@@ -236,31 +253,37 @@
         ]
 
 
-def mix(parts, cols, arrived, send, kept, held, result):
+def mix(parts, cores, cols, arrived, send, kept, held, result):
     block = 8
     q = arrived.shape[1]
-    spread_rows(block, cols, arrived, held)
+    spread_rows(block, 1, cols, arrived, held)
     for e in range(q // 2):
         left = square(block, parts, cols, held, e)
         right = square(block, parts, cols, held, q // 2 + e)
         kept[e] = left
         kept[q // 2 + e] = right
         put_square(block, parts, cols, result, e, dot(left, right, (1, 1)))
-    pack_rows(block, cols, result, send)
-
-
-def unmix(parts, cols, arrived, kept_far, send, held, result, kept, arrival):
+    pack_rows(block, cores, cols, result, send)
+
+
+def unmix(parts, cores, cols, arrived, kept_far, send, held, result, kept, arrival):
     block = 8
     q = arrived.shape[1]
     copy = pltpu.make_async_copy(kept_far, kept, arrival)
     copy.start()
-    spread_rows(block, cols, arrived, held)
+    spread_rows(block, cores, cols, arrived, held)
     copy.wait()
     for e in range(q):
         d_mixed = square(block, parts, cols, held, e)
         put_square(block, parts, cols, result, e, dot(d_mixed, kept[q + e], (1, 0)))
         put_square(block, parts, cols, result, q + e, dot(d_mixed, kept[e], (0, 0)))
-    pack_rows(block, cols, result, send)
+    pack_rows(block, cores, cols, result, send)
+
+
+def order_weights(own, other, weights):
+    core = lax.axis_index("ch")
+    weights[core] = own[...]
+    weights[1 - core] = other[...]
 
 
 def split_rows(cols, values, own, other):
@@ -275,11 +298,12 @@
 
 
 def head(
-    width, scale, arrived, weights, normed_far, own_far, other_far,
+    width, scale, arrived, own_weights, other_weights, normed_far, own_far, other_far,
     send, d_gate, terms, updated_own, updated_other,
-    normed, own, other, upstream, arrivals,
+    normed, own, other, upstream, weights, arrivals,
 ):
     parts, total, _ = weights.shape
+    order_weights(own_weights, other_weights, weights)
     hidden = (total - 2 * width) // 2
     devices, q, flat = arrived.shape
     count, _, cols = other.shape
@@ -324,9 +348,9 @@
 
 
 def tail(
-    width, scale, arrived, weights, pair_far, d_gate_far, head_terms,
+    width, scale, arrived, own_weights, other_weights, pair_far, d_gate_far, head_terms,
     send, grad_own, grad_other,
-    pair, d_gate, whole, arrivals,
+    pair, d_gate, whole, weights, arrivals,
 ):
     parts, total, channels = weights.shape
     hidden = (total - 2 * width) // 2
@@ -338,6 +362,7 @@
         pltpu.make_async_copy(d_gate_far, d_gate, arrivals.at[1]),
     ]
     start_all(copies)
+    order_weights(own_weights, other_weights, weights)
     wait_all(copies)
     hat, inverse = normalized(pair[...])
     normed = hat.astype(bf16)
@@ -418,31 +443,31 @@
     scale = 1.0 / tokens
     swap = [(c, parts - 1 - c) for c in range(parts)]
     whole_weight = pltpu.VMEM((2 * hidden, channels), bf16)
-    weights, normed = call(
-        functools.partial(prepare, share),
-        [((2 * width + 2 * hidden, channels), bf16), ((channels, flat), bf16)],
+    rest = devices // parts
+    weight = (2 * width + 2 * hidden, channels)
+    weights, normed, send = call(
+        functools.partial(edges, share),
+        [(weight, bf16), ((channels, flat), bf16), ((rest, 2 * share, row_count * cols), bf16)],
         (w_gate_a.T, w_proj_a.T, w_gate_b.T, w_proj_b.T, w_gate_out.T, w_out.T, pair),
         (
             whole_weight,
             whole_weight,
             whole_weight,
-            pltpu.VMEM((count, cols, channels), bf16),
-            pltpu.SemaphoreType.DMA((7,)),
+            pltpu.VMEM(pair.shape, bf16),
+            pltpu.VMEM((parts, channels, flat), bf16),
+            pltpu.SemaphoreType.DMA((6 + parts,)),
         ),
         far=range(7),
         room=60,
     )
-    weights = lax.all_gather(weights, "ch")
+    arrived = lax.all_to_all(send, one_core, 0, 0)
+    weights = (weights, lax.ppermute(weights, "ch", swap))
     own = jnp.swapaxes(cotangent, 1, 2)
     other = lax.dynamic_slice_in_dim(own, (1 - lax.axis_index("ch")) * count, count, 0)
     other = lax.ppermute(other, "ch", swap)
-    (send,) = call(
-        functools.partial(edges, width), [((devices, 2 * share, flat), bf16)], (normed, weights)
-    )
-    arrived = lax.all_to_all(send, everyone, 0, 0)
     room = pltpu.VMEM((col_parts * tokens * 8, -(-cols // 128) * 128), f32)
     send, kept = call(
-        functools.partial(mix, col_parts, cols),
+        functools.partial(mix, col_parts, parts, cols),
         [((devices, share, flat), bf16), ((2 * share, tokens, tokens), bf16)],
         (arrived,),
         (room, room),
@@ -458,20 +483,21 @@
             part,
             part,
         ],
-        (arrived, weights, normed, own, other),
+        (arrived, *weights, normed, own, other),
         (
             pltpu.VMEM((channels, flat), bf16),
             pltpu.VMEM(*part),
             pltpu.VMEM(*part),
             pltpu.VMEM((hidden * parts, flat), f32),
+            pltpu.VMEM((parts, *weight), bf16),
             pltpu.SemaphoreType.DMA((3,)),
         ),
-        far=(2, 3, 4),
+        far=(3, 4, 5),
     )
     arrived = lax.all_to_all(send, everyone, 0, 0)
     updated_other = lax.ppermute(updated_other, "ch", swap)
     (send,) = call(
-        functools.partial(unmix, col_parts, cols),
+        functools.partial(unmix, col_parts, parts, cols),
         [((devices, 2 * share, flat), bf16)],
         (arrived, kept),
         (room, room, pltpu.VMEM(kept.shape, bf16), pltpu.SemaphoreType.DMA),
@@ -487,19 +513,19 @@
     send, grad_own, grad_other = call(
         functools.partial(tail, width, scale),
         [((devices, per, channels), bf16), part, part],
-        (arrived, weights, pair, d_gate, head_terms),
+        (arrived, *weights, pair, d_gate, head_terms),
         (
             pltpu.VMEM((count, cols, channels), bf16),
             pltpu.VMEM((hidden * parts, flat), bf16),
             pltpu.VMEM((total * parts, channels), f32),
+            pltpu.VMEM((parts, *weight), bf16),
             two,
         ),
-        far=(2, 3),
+        far=(3, 4),
     )
     arrived = lax.all_to_all(send, ("ch", "row", "col"), 0, 0)
     grad_other = lax.ppermute(grad_other, "ch", swap)
     (grad_pair,) = call(join_rows, rows, (grad_own, grad_other), (two,), (0, 1), True)
-    rest = devices // parts
     (sums,) = call(add_up, [((rest, per, channels), bf16)], (arrived,))
     sums = lax.all_to_all(sums, ("row", "col"), 0, 0)
     sums, grad_pair = lax.optimization_barrier((sums, grad_pair))

time: 110 us -> 111 us (level)
    all_to_all x0 -> x1, blocking collectives: none -> 25.8 us  [by_channels(): arrived = lax.all_to_all(send, one_core, 0, 0)]
    all_to_all x2 -> x1, blocking collectives: 37.5 us -> 13.4 us  [by_channels(): arrived = lax.all_to_all(send, everyone, 0, 0)]
    all_gather x1 -> x0, blocking collectives: 2.39 us -> none  [by_channels(): weights = lax.all_gather(weights, 'ch')]
    ppermute x1, waiting for transfers between devices: 1.33 us -> 0.01 us  [by_channels(): other = lax.ppermute(other, 'ch', swap)]
    ppermute x0 -> x1, waiting for transfers between devices: none -> 1.19 us  [by_channels(): weights = (weights, lax.ppermute(weights, 'ch', swap))]
    pallas_call x10 -> x9, Pallas kernels: 14 us -> 14.6 us  [call(): pl.pallas_call(kernel, out_shape=tuple((jax.ShapeDtypeStruct(*out) for ou...]
  transfers between devices with their start and end apart: 6 -> 7, of which waited for: 6 -> 6; matrix products, arithmetic and copies ran while one was open for 0% -> 0% of each run, Pallas kernels for 1% -> 1%
where the time goes in v2:
time: 111 us; the launch traced here: 110 us
  blocking collectives  51 us (46%)
  waiting for transfers between devices  33.9 us (31%)
  Pallas kernels  14.6 us (13%)
  starting transfers between devices  9.39 us (8%)
    all_to_all x1, blocking collectives, by_channels(): arrived = lax.all_to_all(send, one_core, 0, 0)  25.8 us
    all_to_all x2, waiting for transfers between devices, by_channels(): arrived = lax.all_to_all(send, everyone, 0, 0)  24.6 us
    pallas_call x9, Pallas kernels, call(): pl.pallas_call(kernel, out_shape=tuple((jax.ShapeDtypeStruct(*out) for ou...  14.6 us
    all_to_all x1, blocking collectives, by_channels(): arrived = lax.all_to_all(send, everyone, 0, 0)  13.4 us
    all_to_all x1, blocking collectives, by_channels(): arrived = lax.all_to_all(send, ('ch', 'row', 'col'), 0, 0)  11.8 us
    all_to_all x1, waiting for transfers between devices, by_channels(): sums = lax.all_to_all(sums, ('row', 'col'), 0, 0)  5.36 us
    all_to_all x2, starting transfers between devices, by_channels(): arrived = lax.all_to_all(send, everyone, 0, 0)  5.35 us
    all_to_all x1, starting transfers between devices, by_channels(): sums = lax.all_to_all(sums, ('row', 'col'), 0, 0)  3.51 us
  transfers between devices with their start and end apart: 7, of which 6 were waited for; matrix products, arithmetic and copies ran while one was open for 0% of the time, Pallas kernels for 1%

profile of v2, /device:TPU:0, one launch (start us, length us, event | category | flops | bytes accessed | tf_op | source)
XLA Modules:
  0.0 110.5 jit_solution(6216054809846675595)
XLA Ops:
  0.6 3.1 %shard_map.143 = (bf16[384,128]{1,0:T(8,128)(2,1)}, bf16[128,1152]{1,0:T(8,128)(2,1)}, bf16[16,8,2304]{2,1,0:T(8,128)(2,1)}) custom-call(bf16[64,128]{1,0:T(8,128)(2,1)} %bitcast.20, bf16[64,128]{1,0:T(8,128)(2,1)} %bitcast.21, bf16[64,128]{1,0:T(8,128)(2,1)} %bitcast.22, bf16[64,128]{1,0:T(8,128)(2,1)} %bitcast.23, bf16[64,128]{1,0:T(8,128)(2,1)} %bitcast.24, ...), custom_call_target="tpu_custom_call" | custom-call | tf_op jit(solution)/shard_map/pallas_call | solution.py:133
  3.8 25.8 %all_to_all.30.arrived = bf16[16,8,2304]{2,1,0:T(8,128)(2,1)S(1)} all-to-all(bf16[16,8,2304]{2,1,0:T(8,128)(2,1)} %get-tuple-element.31), channel_id=1, replica_groups=mesh['row'=8,'col'=2,'ch'=2] {'col','row'}, dimensions={0} | all-to-all | bytes 1179648 | tf_op jit(solution)/shard_map/all_to_all | solution.py:463
  29.6 2.3 %shard_map.144 = (bf16[32,4,1152]{2,1,0:T(4,128)(2,1)}, bf16[8,192,192]{2,1,0:T(8,128)(2,1)S(1)}) custom-call(bf16[16,8,2304]{2,1,0:T(8,128)(2,1)S(1)} %all_to_all.30.arrived), custom_call_target="tpu_custom_call" | custom-call | tf_op jit(solution)/shard_map/pallas_call | solution.py:133
  31.8 0.0 copy-start.1
  31.8 2.7 %all-to-all-start.1 = ((bf16[32,4,1152]{2,1,0:T(4,128)(2,1)}), bf16[32,4,1152]{2,1,0:T(4,128)(2,1)S(1)}, u32[]{:S(2)}, u32[]{:S(2)}) async-start(bf16[32,4,1152]{2,1,0:T(4,128)(2,1)} %get-tuple-element.32), calls=%async_computation.1 | async-start | bytes 589824 | tf_op jit(solution)/shard_map/all_to_all | solution.py:475
  34.6 0.0 copy-start.3
  34.6 0.0 copy-done.1
  34.6 0.0 copy-start.2
  34.6 0.2 collective-permute-start.1
  34.8 0.7 copy-done.2
  35.5 0.1 collective-permute-start
  35.6 1.2 %collective-permute-done.other_weights = bf16[384,128]{1,0:T(8,128)(2,1)S(1)} collective-permute-done((bf16[384,128]{1,0:T(8,128)(2,1)S(1)}, bf16[384,128]{1,0:T(8,128)(2,1)S(1)}, u32[]{:S(2)}, u32[]{:S(2)}) %collective-permute-start) | collective-permute-done | bytes 98336 | tf_op jit(solution)/shard_map/ppermute | solution.py:464
  36.8 0.0 collective-permute-done.1.other_far
  36.8 9.2 %all-to-all-done.1.arrived = bf16[32,4,1152]{2,1,0:T(4,128)(2,1)S(1)} async-done(((bf16[32,4,1152]{2,1,0:T(4,128)(2,1)}), bf16[32,4,1152]{2,1,0:T(4,128)(2,1)S(1)}, u32[]{:S(2)}, u32[]{:S(2)}) %all-to-all-start.1) | async-done | bytes 294944 | tf_op jit(solution)/shard_map/all_to_all | solution.py:475
  46.0 0.0 copy-done.3
  46.0 1.9 %shard_map.145 = (bf16[32,4,1152]{2,1,0:T(4,128)(2,1)S(1)}, bf16[128,1152]{1,0:T(8,128)(2,1)S(1)}, f32[2,128,128]{2,1,0:T(8,128)S(1)}, bf16[12,64,96]{2,1,0:T(8,128)(2,1)S(1)}, bf16[12,64,96]{2,1,0:T(8,128)(2,1)S(1)}) custom-call(bf16[32,4,1152]{2,1,0:T(4,128)(2,1)S(1)} %all-to-all-done.1.arrived, bf16[384,128]{1,0:T(8,128)(2,1)S(1)} %copy-done.2, ...), custom_call_target="tpu_custom_call" | custom-call | tf_op jit(solution)/shard_map/pallas_call | solution.py:133
  47.9 13.4 %all_to_all.31.arrived = bf16[32,4,1152]{2,1,0:T(4,128)(2,1)S(1)} all-to-all(bf16[32,4,1152]{2,1,0:T(4,128)(2,1)S(1)} %get-tuple-element.35), channel_id=1, replica_groups=mesh['row'=8,'col'=2,'ch'=2] {'ch','col','row'}, dimensions={0} | all-to-all | bytes 589824 | tf_op jit(solution)/shard_map/all_to_all | solution.py:497
  61.3 2.4 %shard_map.146 = bf16[32,8,1152]{2,1,0:T(8,128)(2,1)} custom-call(bf16[32,4,1152]{2,1,0:T(4,128)(2,1)S(1)} %all_to_all.31.arrived, bf16[8,192,192]{2,1,0:T(8,128)(2,1)S(1)} %get-tuple-element.36.kept_far), custom_call_target="tpu_custom_call" | custom-call | tf_op jit(solution)/shard_map/pallas_call | solution.py:133
  63.8 2.6 %all-to-all-start.3 = ((bf16[32,8,1152]{2,1,0:T(8,128)(2,1)}), bf16[32,8,1152]{2,1,0:T(8,128)(2,1)S(1)}, u32[]{:S(2)}, u32[]{:S(2)}) async-start(bf16[32,8,1152]{2,1,0:T(8,128)(2,1)} %shard_map.146), calls=%async_computation.3 | async-start | bytes 1179648 | tf_op jit(solution)/shard_map/all_to_all | solution.py:506
  66.4 0.0 copy-start
  66.4 0.2 collective-permute-start.2
  66.6 1.3 %collective-permute-done.2.other = bf16[12,64,96]{2,1,0:T(8,128)(2,1)S(1)} collective-permute-done((bf16[12,64,96]{2,1,0:T(8,128)(2,1)S(1)}, bf16[12,64,96]{2,1,0:T(8,128)(2,1)S(1)}, u32[]{:S(2)}, u32[]{:S(2)}) %collective-permute-start.2) | collective-permute-done | bytes 147488 | tf_op jit(solution)/shard_map/ppermute | solution.py:498
  67.9 0.8 shard_map.147
  68.7 15.5 %all-to-all-done.3.arrived = bf16[32,8,1152]{2,1,0:T(8,128)(2,1)S(1)} async-done(((bf16[32,8,1152]{2,1,0:T(8,128)(2,1)}), bf16[32,8,1152]{2,1,0:T(8,128)(2,1)S(1)}, u32[]{:S(2)}, u32[]{:S(2)}) %all-to-all-start.3) | async-done | bytes 589856 | tf_op jit(solution)/shard_map/all_to_all | solution.py:506
  84.2 0.0 copy-done
  84.2 1.7 %shard_map.148 = (bf16[32,24,128]{2,1,0:T(8,128)(2,1)S(1)}, bf16[12,64,96]{2,1,0:T(8,128)(2,1)S(1)}, bf16[12,64,96]{2,1,0:T(8,128)(2,1)S(1)}) custom-call(bf16[32,8,1152]{2,1,0:T(8,128)(2,1)S(1)} %all-to-all-done.3.arrived, bf16[384,128]{1,0:T(8,128)(2,1)S(1)} %copy-done.2, bf16[384,128]{1,0:T(8,128)(2,1)S(1)} %collective-permute-done.other_weights, ...), custom_call_target="tpu_custom_call" | custom-call | tf_op jit(solution)/shard_map/pallas_call | solution.py:133
  85.9 11.8 %all_to_all.32.arrived = bf16[32,24,128]{2,1,0:T(8,128)(2,1)S(1)} all-to-all(bf16[32,24,128]{2,1,0:T(8,128)(2,1)S(1)} %get-tuple-element.43), channel_id=1, replica_groups=mesh['row'=8,'col'=2,'ch'=2] {'ch','row','col'}, dimensions={0} | all-to-all | bytes 393216 | tf_op jit(solution)/shard_map/all_to_all | solution.py:526
  97.7 0.7 shard_map.149
  98.4 3.5 %all-to-all-start.5 = ((bf16[16,24,128]{2,1,0:T(8,128)(2,1)}), bf16[16,24,128]{2,1,0:T(8,128)(2,1)S(1)}, u32[]{:S(2)}, u32[]{:S(2)}) async-start(bf16[16,24,128]{2,1,0:T(8,128)(2,1)} %shard_map.149), calls=%async_computation.5 | async-start | bytes 196608 | tf_op jit(solution)/shard_map/all_to_all | solution.py:530
  101.9 0.1 collective-permute-start.3
  102.0 1.4 %collective-permute-done.3.other = bf16[12,64,96]{2,1,0:T(8,128)(2,1)S(1)} collective-permute-done((bf16[12,64,96]{2,1,0:T(8,128)(2,1)S(1)}, bf16[12,64,96]{2,1,0:T(8,128)(2,1)S(1)}, u32[]{:S(2)}, u32[]{:S(2)}) %collective-permute-start.3) | collective-permute-done | bytes 147488 | tf_op jit(solution)/shard_map/ppermute | solution.py:527
  103.4 0.8 shard_map.150
  104.2 5.4 %all-to-all-done.5.sums = bf16[16,24,128]{2,1,0:T(8,128)(2,1)S(1)} async-done(((bf16[16,24,128]{2,1,0:T(8,128)(2,1)}), bf16[16,24,128]{2,1,0:T(8,128)(2,1)S(1)}, u32[]{:S(2)}, u32[]{:S(2)}) %all-to-all-start.5) | async-done | bytes 98336 | tf_op jit(solution)/shard_map/all_to_all | solution.py:530
  109.5 0.9 shard_map.151
  (1 shorter events, 0.0 us)
Async XLA Ops:
  31.8 2.7 %copy-start.1 = (bf16[24,96,64]{1,2,0:T(8,128)(2,1)S(1)}, bf16[24,96,64]{1,2,0:T(8,128)(2,1)}, u32[]{:S(2)}) copy-start(bf16[24,96,64]{1,2,0:T(8,128)(2,1)} %param.9) | copy-start | bytes 884740
  31.8 14.2 %all-to-all-start.1 = ((bf16[32,4,1152]{2,1,0:T(4,128)(2,1)}), bf16[32,4,1152]{2,1,0:T(4,128)(2,1)S(1)}, u32[]{:S(2)}, u32[]{:S(2)}) async-start(bf16[32,4,1152]{2,1,0:T(4,128)(2,1)} %get-tuple-element.32), calls=%async_computation.1 | async-start | bytes 589824 | tf_op jit(solution)/shard_map/all_to_all | solution.py:475
  34.6 11.4 %copy-start.3 = (bf16[128,1152]{1,0:T(8,128)(2,1)S(1)}, bf16[128,1152]{1,0:T(8,128)(2,1)}, u32[]{:S(2)}) copy-start(bf16[128,1152]{1,0:T(8,128)(2,1)} %get-tuple-element.34.normed_far) | copy-start | bytes 884740
  34.6 0.9 copy-start.2
  34.6 2.2 %collective-permute-start.1 = (bf16[12,64,96]{2,1,0:T(8,128)(2,1)S(1)}, bf16[12,64,96]{2,1,0:T(8,128)(2,1)S(1)}, u32[]{:S(2)}, u32[]{:S(2)}) collective-permute-start(bf16[12,64,96]{2,1,0:T(8,128)(2,1)S(1)} %dynamic-slice_bitcast_fusion), channel_id=1, source_target_pairs={{0,1},{1,0},{2,3},{3,2},{4,5},{5,4},{6,7},{7,6},{8,9},{9,8},{10,11... | collective-permute-start | bytes 442376 | tf_op jit(solution)/shard_map/ppermute | solution.py:467
  35.5 1.3 %collective-permute-start = (bf16[384,128]{1,0:T(8,128)(2,1)S(1)}, bf16[384,128]{1,0:T(8,128)(2,1)S(1)}, u32[]{:S(2)}, u32[]{:S(2)}) collective-permute-start(bf16[384,128]{1,0:T(8,128)(2,1)S(1)} %copy-done.2), channel_id=1, source_target_pairs={{0,1},{1,0},{2,3},{3,2},{4,5},{5,4},{6,7},{7,6},{8,9},{9,8},{10,11... | collective-permute-start | bytes 294920 | tf_op jit(solution)/shard_map/ppermute | solution.py:464
  63.8 20.4 %all-to-all-start.3 = ((bf16[32,8,1152]{2,1,0:T(8,128)(2,1)}), bf16[32,8,1152]{2,1,0:T(8,128)(2,1)S(1)}, u32[]{:S(2)}, u32[]{:S(2)}) async-start(bf16[32,8,1152]{2,1,0:T(8,128)(2,1)} %shard_map.146), calls=%async_computation.3 | async-start | bytes 1179648 | tf_op jit(solution)/shard_map/all_to_all | solution.py:506
  66.4 17.8 %copy-start = (bf16[24,96,128]{2,1,0:T(8,128)(2,1)S(1)}, bf16[24,96,128]{2,1,0:T(8,128)(2,1)}, u32[]{:S(2)}) copy-start(bf16[24,96,128]{2,1,0:T(8,128)(2,1)} %pair_far.3) | copy-start | bytes 1769476
  66.4 1.5 %collective-permute-start.2 = (bf16[12,64,96]{2,1,0:T(8,128)(2,1)S(1)}, bf16[12,64,96]{2,1,0:T(8,128)(2,1)S(1)}, u32[]{:S(2)}, u32[]{:S(2)}) collective-permute-start(bf16[12,64,96]{2,1,0:T(8,128)(2,1)S(1)} %get-tuple-element.38), channel_id=1, source_target_pairs={{0,1},{1,0},{2,3},{3,2},{4,5},{5,4},{6,7},{7,6},{8,9},{9,8},{10,11... | collective-permute-start | bytes 442376 | tf_op jit(solution)/shard_map/ppermute | solution.py:498
  98.4 11.1 %all-to-all-start.5 = ((bf16[16,24,128]{2,1,0:T(8,128)(2,1)}), bf16[16,24,128]{2,1,0:T(8,128)(2,1)S(1)}, u32[]{:S(2)}, u32[]{:S(2)}) async-start(bf16[16,24,128]{2,1,0:T(8,128)(2,1)} %shard_map.149), calls=%async_computation.5 | async-start | bytes 196608 | tf_op jit(solution)/shard_map/all_to_all | solution.py:530
  101.9 1.5 %collective-permute-start.3 = (bf16[12,64,96]{2,1,0:T(8,128)(2,1)S(1)}, bf16[12,64,96]{2,1,0:T(8,128)(2,1)S(1)}, u32[]{:S(2)}, u32[]{:S(2)}) collective-permute-start(bf16[12,64,96]{2,1,0:T(8,128)(2,1)S(1)} %get-tuple-element.45), channel_id=1, source_target_pairs={{0,1},{1,0},{2,3},{3,2},{4,5},{5,4},{6,7},{7,6},{8,9},{9,8},{10,11... | collective-permute-start | bytes 442376 | tf_op jit(solution)/shard_map/ppermute | solution.py:527

commit v3 on v0

--- a/solution.py
+++ b/solution.py
@@ -159,12 +159,8 @@
         copy.wait()
 
 
-def prepare(share, ga, pa, gb, pb, go, wo, pair_far, out, normed, gates, values, last, pair, arrivals):
+def turn_weights(share, ga, pa, gb, pb, go, wo, out, gates, values, last, arrivals):
     hidden = go.shape[0]
-    count = pair.shape[0]
-    rows = pl.ds(lax.axis_index("ch") * count, count)
-    fetch = pltpu.make_async_copy(pair_far.at[rows], pair, arrivals.at[6])
-    fetch.start()
     width = 2 * hidden
     copies = []
     for at, (held, low, high) in enumerate(((gates, ga, gb), (values, pa, pb), (last, go, wo))):
@@ -176,8 +172,21 @@
     out[:width] = dot(order, gates[...], (1, 0)).astype(bf16)
     out[width : 2 * width] = dot(order, values[...], (1, 0)).astype(bf16)
     out[2 * width :] = last[...]
-    fetch.wait()
+
+
+def normalize(pair_far, normed, pair, arrival):
+    count = pair.shape[0]
+    rows = pl.ds(lax.axis_index("ch") * count, count)
+    copy = pltpu.make_async_copy(pair_far.at[rows], pair, arrival)
+    copy.start()
+    copy.wait()
     normed[...] = normalized(pair[...])[0].astype(bf16)
+
+
+def order_weights(own, other, weights):
+    core = lax.axis_index("ch")
+    weights[core] = own[...]
+    weights[1 - core] = other[...]
 
 
 def rows_of(weights, start, count):
@@ -192,7 +201,8 @@
     return centred * rstd, rstd
 
 
-def edges(width, normed, weights, send):
+def edges(width, normed, own_weights, other_weights, send, weights):
+    order_weights(own_weights, other_weights, weights)
     gate = jax.nn.sigmoid(dot(rows_of(weights, 0, width), normed[...], (1, 0)))
     value = dot(rows_of(weights, width, width), normed[...], (1, 0))
     send[...] = (gate * value).reshape(send.shape).astype(bf16)
@@ -275,9 +285,9 @@
 
 
 def head(
-    width, scale, arrived, weights, normed_far, own_far, other_far,
+    width, scale, arrived, own_weights, other_weights, normed_far, own_far, other_far,
     send, d_gate, terms, updated_own, updated_other,
-    normed, own, other, upstream, arrivals,
+    normed, own, other, upstream, weights, arrivals,
 ):
     parts, total, _ = weights.shape
     hidden = (total - 2 * width) // 2
@@ -290,6 +300,7 @@
         pltpu.make_async_copy(other_far, other, arrivals.at[2]),
     ]
     start_all(copies)
+    order_weights(own_weights, other_weights, weights)
     mixed = jnp.concatenate([arrived[s].astype(f32) for s in range(devices)], 0)
     average = jnp.mean(mixed, 0, keepdims=True)
     spread = jnp.mean(mixed * mixed, 0, keepdims=True) - average * average
@@ -324,9 +335,9 @@
 
 
 def tail(
-    width, scale, arrived, weights, pair_far, d_gate_far, head_terms,
-    send, grad_own, grad_other,
-    pair, d_gate, whole, arrivals,
+    width, scale, arrived, own_weights, other_weights, pair_far, d_gate_far, head_terms, updated_other,
+    send, grad_own, others,
+    pair, d_gate, whole, weights, arrivals,
 ):
     parts, total, channels = weights.shape
     hidden = (total - 2 * width) // 2
@@ -338,6 +349,8 @@
         pltpu.make_async_copy(d_gate_far, d_gate, arrivals.at[1]),
     ]
     start_all(copies)
+    order_weights(own_weights, other_weights, weights)
+    others[0] = updated_other[...]
     wait_all(copies)
     hat, inverse = normalized(pair[...])
     normed = hat.astype(bf16)
@@ -364,7 +377,7 @@
         - jnp.mean(d_input, 0, keepdims=True)
         - hat * jnp.mean(d_input * hat, 0, keepdims=True)
     )
-    split_rows(cols, back, grad_own, grad_other)
+    split_rows(cols, back, grad_own, others.at[1])
 
 
 def add_up(arrived, out):
@@ -394,13 +407,14 @@
     wait_all(copies)
 
 
-def join_rows(own, other, out, leaves):
-    count = own.shape[0]
+def join_rows(updated_own, grad_own, others, updated, grad, leaves):
+    count = updated_own.shape[0]
     core = lax.axis_index("ch")
-    copies = [
-        pltpu.make_async_copy(own, out.at[pl.ds(core * count, count)], leaves.at[0]),
-        pltpu.make_async_copy(other, out.at[pl.ds((1 - core) * count, count)], leaves.at[1]),
-    ]
+    here, there = pl.ds(core * count, count), pl.ds((1 - core) * count, count)
+    copies = []
+    for at, (own, out) in enumerate(((updated_own, updated), (grad_own, grad))):
+        copies.append(pltpu.make_async_copy(own, out.at[here], leaves.at[2 * at]))
+        copies.append(pltpu.make_async_copy(others.at[at], out.at[there], leaves.at[2 * at + 1]))
     start_all(copies)
     wait_all(copies)
 
@@ -418,26 +432,31 @@
     scale = 1.0 / tokens
     swap = [(c, parts - 1 - c) for c in range(parts)]
     whole_weight = pltpu.VMEM((2 * hidden, channels), bf16)
-    weights, normed = call(
-        functools.partial(prepare, share),
-        [((2 * width + 2 * hidden, channels), bf16), ((channels, flat), bf16)],
-        (w_gate_a.T, w_proj_a.T, w_gate_b.T, w_proj_b.T, w_gate_out.T, w_out.T, pair),
-        (
-            whole_weight,
-            whole_weight,
-            whole_weight,
-            pltpu.VMEM((count, cols, channels), bf16),
-            pltpu.SemaphoreType.DMA((7,)),
-        ),
-        far=range(7),
-        room=60,
-    )
-    weights = lax.all_gather(weights, "ch")
+    weight = ((2 * width + 2 * hidden, channels), bf16)
     own = jnp.swapaxes(cotangent, 1, 2)
     other = lax.dynamic_slice_in_dim(own, (1 - lax.axis_index("ch")) * count, count, 0)
     other = lax.ppermute(other, "ch", swap)
+    (weights,) = call(
+        functools.partial(turn_weights, share),
+        [weight],
+        (w_gate_a.T, w_proj_a.T, w_gate_b.T, w_proj_b.T, w_gate_out.T, w_out.T),
+        (whole_weight, whole_weight, whole_weight, pltpu.SemaphoreType.DMA((6,))),
+        far=range(6),
+        room=60,
+    )
+    weights = (weights, lax.ppermute(weights, "ch", swap))
+    (normed,) = call(
+        normalize,
+        [((channels, flat), bf16)],
+        (pair,),
+        (pltpu.VMEM((count, cols, channels), bf16), pltpu.SemaphoreType.DMA),
+        far=(0,),
+        room=60,
+    )
+    normed, other = lax.optimization_barrier((normed, other))
     (send,) = call(
-        functools.partial(edges, width), [((devices, 2 * share, flat), bf16)], (normed, weights)
+        functools.partial(edges, width), [((devices, 2 * share, flat), bf16)], (normed, *weights),
+        (pltpu.VMEM((parts, *weight[0]), bf16),),
     )
     arrived = lax.all_to_all(send, everyone, 0, 0)
     room = pltpu.VMEM((col_parts * tokens * 8, -(-cols // 128) * 128), f32)
@@ -458,18 +477,18 @@
             part,
             part,
         ],
-        (arrived, weights, normed, own, other),
+        (arrived, *weights, normed, own, other),
         (
             pltpu.VMEM((channels, flat), bf16),
             pltpu.VMEM(*part),
             pltpu.VMEM(*part),
             pltpu.VMEM((hidden * parts, flat), f32),
+            pltpu.VMEM((parts, *weight[0]), bf16),
             pltpu.SemaphoreType.DMA((3,)),
         ),
-        far=(2, 3, 4),
+        far=(3, 4, 5),
     )
     arrived = lax.all_to_all(send, everyone, 0, 0)
-    updated_other = lax.ppermute(updated_other, "ch", swap)
     (send,) = call(
         functools.partial(unmix, col_parts, cols),
         [((devices, 2 * share, flat), bf16)],
@@ -478,31 +497,35 @@
         far=(1,),
     )
     arrived = lax.all_to_all(send, everyone, 0, 0)
-    rows = [((row_count, hidden, cols), bf16)]
-    two = pltpu.SemaphoreType.DMA((2,))
-    (updated,) = call(join_rows, rows, (updated_own, updated_other), (two,), (0, 1), True)
-    arrived, updated = lax.optimization_barrier((arrived, updated))
     total = 2 * width + 2 * hidden
     per = total * parts // devices
-    send, grad_own, grad_other = call(
+    send, grad_own, others = call(
         functools.partial(tail, width, scale),
-        [((devices, per, channels), bf16), part, part],
-        (arrived, weights, pair, d_gate, head_terms),
+        [((devices, per, channels), bf16), part, ((2, *part[0]), bf16)],
+        (arrived, *weights, pair, d_gate, head_terms, updated_other),
         (
             pltpu.VMEM((count, cols, channels), bf16),
             pltpu.VMEM((hidden * parts, flat), bf16),
             pltpu.VMEM((total * parts, channels), f32),
-            two,
+            pltpu.VMEM((parts, *weight[0]), bf16),
+            pltpu.SemaphoreType.DMA((2,)),
         ),
-        far=(2, 3),
+        far=(3, 4),
     )
     arrived = lax.all_to_all(send, ("ch", "row", "col"), 0, 0)
-    grad_other = lax.ppermute(grad_other, "ch", swap)
-    (grad_pair,) = call(join_rows, rows, (grad_own, grad_other), (two,), (0, 1), True)
     rest = devices // parts
     (sums,) = call(add_up, [((rest, per, channels), bf16)], (arrived,))
+    sums, others = lax.optimization_barrier((sums, others))
     sums = lax.all_to_all(sums, ("row", "col"), 0, 0)
-    sums, grad_pair = lax.optimization_barrier((sums, grad_pair))
+    updated, grad_pair = call(
+        join_rows,
+        [((row_count, hidden, cols), bf16)] * 2,
+        (updated_own, grad_own, lax.ppermute(others, "ch", swap)),
+        (pltpu.SemaphoreType.DMA((4,)),),
+        (0, 1, 2),
+        True,
+    )
+    sums, updated, grad_pair = lax.optimization_barrier((sums, updated, grad_pair))
     grads = call(
         functools.partial(turn_back, share),
         [((hidden, channels), f32)] * 6,

time: 110 us -> 110 us (level)
  blocking collectives: 51.7 us -> 82.3 us
  waiting for transfers between devices: 33.9 us -> 7.02 us
  starting transfers between devices: 9.29 us -> 4.15 us
  local copies, waits for them, and re-layouts: 0.04 us -> 1.92 us
    all_to_all x2 -> x4, blocking collectives: 37.5 us -> 70.4 us  [by_channels(): arrived = lax.all_to_all(send, everyone, 0, 0)]
    all_to_all x2 -> x0, waiting for transfers between devices: 24.5 us -> none  [by_channels(): arrived = lax.all_to_all(send, everyone, 0, 0)]
    all_to_all x2 -> x0, starting transfers between devices: 5.35 us -> none  [by_channels(): arrived = lax.all_to_all(send, everyone, 0, 0)]
    ppermute x2, waiting for transfers between devices: 2.74 us -> 0.01 us  [the longest x1 0.01 us: by_channels(): weights = (weights, lax.ppermute(weights, 'ch', swap))]
    all_gather x1 -> x0, blocking collectives: 2.39 us -> none  [by_channels(): weights = lax.all_gather(weights, 'ch')]
    all_to_all x1, waiting for transfers between devices: 5.36 us -> 7.02 us  [by_channels(): sums = lax.all_to_all(sums, ('row', 'col'), 0, 0)]
    ppermute x1, waiting for transfers between devices: 1.33 us -> 0.01 us  [by_channels(): other = lax.ppermute(other, 'ch', swap)]
  transfers between devices with their start and end apart: 6 -> 4, of which waited for: 6 -> 1; matrix products, arithmetic and copies ran while one was open for 0% -> 0% of each run, Pallas kernels for 1% -> 4%
where the time goes in v3:
time: 110 us
  blocking collectives  82.3 us (75%)
  Pallas kernels  13.4 us (12%)
  waiting for transfers between devices  7.02 us (6%)
  starting transfers between devices  4.15 us (4%)
  local copies, waits for them, and re-layouts  1.92 us (2%)
    all_to_all x4, blocking collectives, by_channels(): arrived = lax.all_to_all(send, everyone, 0, 0)  70.4 us
    pallas_call x10, Pallas kernels, call(): pl.pallas_call(kernel, out_shape=tuple((jax.ShapeDtypeStruct(*out) for ou...  13.4 us
    all_to_all x1, blocking collectives, by_channels(): arrived = lax.all_to_all(send, ('ch', 'row', 'col'), 0, 0)  11.9 us
    all_to_all x1, waiting for transfers between devices, by_channels(): sums = lax.all_to_all(sums, ('row', 'col'), 0, 0)  7.02 us
    all_to_all x1, starting transfers between devices, by_channels(): sums = lax.all_to_all(sums, ('row', 'col'), 0, 0)  3.51 us
  transfers between devices with their start and end apart: 4, of which 1 were waited for; matrix products, arithmetic and copies ran while one was open for 0% of the time, Pallas kernels for 4%

profile of v3, /device:TPU:0, one launch (start us, length us, event | category | flops | bytes accessed | tf_op | source)
XLA Modules:
  0.0 109.6 jit_solution(14743342723836679371)
XLA Ops:
  0.6 0.9 dynamic-slice_bitcast_fusion
  1.6 0.5 collective-permute-start
  2.1 1.6 %shard_map.144.own_weights = bf16[384,128]{1,0:T(8,128)(2,1)} custom-call(bf16[64,128]{1,0:T(8,128)(2,1)} %bitcast.18, bf16[64,128]{1,0:T(8,128)(2,1)} %bitcast.19, bf16[64,128]{1,0:T(8,128)(2,1)} %bitcast.20, bf16[64,128]{1,0:T(8,128)(2,1)} %bitcast.21, bf16[64,128]{1,0:T(8,128)(2,1)} %bitcast.22, bf16[64,128]{1,0:T(8,128)(2,1)} %bitcast.23), custom_call_target="tpu_custom_call" | custom-call | tf_op jit(solution)/shard_map/pallas_call | solution.py:132
  3.8 0.0 copy-start.3
  3.8 0.1 collective-permute-start.1
  3.9 2.0 %shard_map.143.normed.normed_far = bf16[128,1152]{1,0:T(8,128)(2,1)} custom-call(bf16[24,96,128]{2,1,0:T(8,128)(2,1)} %pair_far.3), custom_call_target="tpu_custom_call" | custom-call | tf_op jit(solution)/shard_map/pallas_call | solution.py:132
  5.9 0.0 collective-permute-done.other_far
  5.9 0.0 collective-permute-done.1.other_weights
  5.9 0.0 copy-done.3
  5.9 0.0 copy-start
  5.9 1.0 copy-done
  6.9 0.5 shard_map.145
  7.3 24.4 %all_to_all.30.arrived = bf16[32,8,1152]{2,1,0:T(8,128)(2,1)S(1)} all-to-all(bf16[32,8,1152]{2,1,0:T(8,128)(2,1)S(1)} %shard_map.145), channel_id=1, replica_groups=mesh['row'=8,'col'=2,'ch'=2] {'col','row','ch'}, dimensions={0} | all-to-all | bytes 1179648 | tf_op jit(solution)/shard_map/all_to_all | solution.py:461
  31.8 0.0 copy-start.4
  31.8 1.5 %shard_map.146 = (bf16[32,4,1152]{2,1,0:T(4,128)(2,1)S(1)}, bf16[8,192,192]{2,1,0:T(8,128)(2,1)S(1)}) custom-call(bf16[32,8,1152]{2,1,0:T(8,128)(2,1)S(1)} %all_to_all.30.arrived), custom_call_target="tpu_custom_call" | custom-call | tf_op jit(solution)/shard_map/pallas_call | solution.py:132
  33.3 0.0 copy-start.1
  33.3 13.1 %all_to_all.31.arrived = bf16[32,4,1152]{2,1,0:T(4,128)(2,1)S(1)} all-to-all(bf16[32,4,1152]{2,1,0:T(4,128)(2,1)S(1)} %get-tuple-element.34), channel_id=1, replica_groups=mesh['row'=8,'col'=2,'ch'=2] {'col','row','ch'}, dimensions={0} | all-to-all | bytes 589824 | tf_op jit(solution)/shard_map/all_to_all | solution.py:469
  46.4 0.0 copy-done.4
  46.4 0.0 copy-done.1
  46.4 1.9 %shard_map.147 = (bf16[32,4,1152]{2,1,0:T(4,128)(2,1)S(1)}, bf16[128,1152]{1,0:T(8,128)(2,1)S(1)}, f32[2,128,128]{2,1,0:T(8,128)S(1)}, bf16[12,64,96]{2,1,0:T(8,128)(2,1)S(1)}, bf16[12,64,96]{2,1,0:T(8,128)(2,1)S(1)}) custom-call(bf16[32,4,1152]{2,1,0:T(4,128)(2,1)S(1)} %all_to_all.31.arrived, bf16[384,128]{1,0:T(8,128)(2,1)S(1)} %copy-done.3, ...), custom_call_target="tpu_custom_call" | custom-call | tf_op jit(solution)/shard_map/pallas_call | solution.py:132
  48.3 13.3 %all_to_all.32.arrived = bf16[32,4,1152]{2,1,0:T(4,128)(2,1)S(1)} all-to-all(bf16[32,4,1152]{2,1,0:T(4,128)(2,1)S(1)} %get-tuple-element.36), channel_id=1, replica_groups=mesh['row'=8,'col'=2,'ch'=2] {'col','row','ch'}, dimensions={0} | all-to-all | bytes 589824 | tf_op jit(solution)/shard_map/all_to_all | solution.py:491
  61.6 1.6 %shard_map.148 = bf16[32,8,1152]{2,1,0:T(8,128)(2,1)S(1)} custom-call(bf16[32,4,1152]{2,1,0:T(4,128)(2,1)S(1)} %all_to_all.32.arrived, bf16[8,192,192]{2,1,0:T(8,128)(2,1)S(1)} %get-tuple-element.37.kept_far), custom_call_target="tpu_custom_call" | custom-call | tf_op jit(solution)/shard_map/pallas_call | solution.py:132
  63.2 0.0 copy-start.2
  63.2 19.6 %all_to_all.33.arrived = bf16[32,8,1152]{2,1,0:T(8,128)(2,1)S(1)} all-to-all(bf16[32,8,1152]{2,1,0:T(8,128)(2,1)S(1)} %shard_map.148), channel_id=1, replica_groups=mesh['row'=8,'col'=2,'ch'=2] {'col','row','ch'}, dimensions={0} | all-to-all | bytes 1179648 | tf_op jit(solution)/shard_map/all_to_all | solution.py:499
  82.9 0.0 copy-done.2
  82.9 1.8 %shard_map.149 = (bf16[32,24,128]{2,1,0:T(8,128)(2,1)S(1)}, bf16[12,64,96]{2,1,0:T(8,128)(2,1)S(1)}, bf16[2,12,64,96]{3,2,1,0:T(8,128)(2,1)S(1)}) custom-call(bf16[32,8,1152]{2,1,0:T(8,128)(2,1)S(1)} %all_to_all.33.arrived, bf16[384,128]{1,0:T(8,128)(2,1)S(1)} %copy-done.3, bf16[384,128]{1,0:T(8,128)(2,1)S(1)} %collective-permute-done.1.other_weights, ...), custom_call_target="tpu_custom_call" | custom-call | tf_op jit(solution)/shard_map/pallas_call | solution.py:132
  84.6 11.9 %all_to_all.34.arrived = bf16[32,24,128]{2,1,0:T(8,128)(2,1)S(1)} all-to-all(bf16[32,24,128]{2,1,0:T(8,128)(2,1)S(1)} %get-tuple-element.41), channel_id=1, replica_groups=mesh['row'=8,'col'=2,'ch'=2] {'ch','row','col'}, dimensions={0} | all-to-all | bytes 393216 | tf_op jit(solution)/shard_map/all_to_all | solution.py:515
  96.5 0.7 shard_map.150
  97.2 0.0 collective-permute-start.2
  97.2 3.5 %all-to-all-start.5 = ((bf16[16,24,128]{2,1,0:T(8,128)(2,1)}), bf16[16,24,128]{2,1,0:T(8,128)(2,1)S(1)}, u32[]{:S(2)}, u32[]{:S(2)}) async-start(bf16[16,24,128]{2,1,0:T(8,128)(2,1)} %shard_map.150), calls=%async_computation.5 | async-start | bytes 196608 | tf_op jit(solution)/shard_map/all_to_all | solution.py:519
  100.7 0.0 collective-permute-done.2.others
  100.7 0.9 shard_map.151
  101.6 7.0 %all-to-all-done.5.sums = bf16[16,24,128]{2,1,0:T(8,128)(2,1)S(1)} async-done(((bf16[16,24,128]{2,1,0:T(8,128)(2,1)}), bf16[16,24,128]{2,1,0:T(8,128)(2,1)S(1)}, u32[]{:S(2)}, u32[]{:S(2)}) %all-to-all-start.5) | async-done | bytes 98336 | tf_op jit(solution)/shard_map/all_to_all | solution.py:519
  108.7 0.9 shard_map.152
Async XLA Ops:
  1.6 4.3 %collective-permute-start = (bf16[12,64,96]{2,1,0:T(8,128)(2,1)S(1)}, bf16[12,64,96]{2,1,0:T(8,128)(2,1)S(1)}, u32[]{:S(2)}, u32[]{:S(2)}) collective-permute-start(bf16[12,64,96]{2,1,0:T(8,128)(2,1)S(1)} %dynamic-slice_bitcast_fusion), channel_id=1, source_target_pairs={{0,1},{1,0},{2,3},{3,2},{4,5},{5,4},{6,7},{7,6},{8,9},{9,8},{10,11... | collective-permute-start | bytes 442376 | tf_op jit(solution)/shard_map/ppermute | solution.py:438
  3.8 2.1 %copy-start.3 = (bf16[384,128]{1,0:T(8,128)(2,1)S(1)}, bf16[384,128]{1,0:T(8,128)(2,1)}, u32[]{:S(2)}) copy-start(bf16[384,128]{1,0:T(8,128)(2,1)} %shard_map.144.own_weights) | copy-start | bytes 294916
  3.8 2.1 %collective-permute-start.1 = (bf16[384,128]{1,0:T(8,128)(2,1)}, bf16[384,128]{1,0:T(8,128)(2,1)S(1)}, u32[]{:S(2)}, u32[]{:S(2)}) collective-permute-start(bf16[384,128]{1,0:T(8,128)(2,1)} %shard_map.144.own_weights), channel_id=1, source_target_pairs={{0,1},{1,0},{2,3},{3,2},{4,5},{5,4},{6,7},{7,6},{8,9},{9,8},{10,11... | collective-permute-start | bytes 294920 | tf_op jit(solution)/shard_map/ppermute | solution.py:447
  5.9 1.0 copy-start
  31.8 14.6 %copy-start.4 = (bf16[24,96,64]{1,2,0:T(8,128)(2,1)S(1)}, bf16[24,96,64]{1,2,0:T(8,128)(2,1)}, u32[]{:S(2)}) copy-start(bf16[24,96,64]{1,2,0:T(8,128)(2,1)} %param.9) | copy-start | bytes 884740
  33.3 13.1 %copy-start.1 = (bf16[128,1152]{1,0:T(8,128)(2,1)S(1)}, bf16[128,1152]{1,0:T(8,128)(2,1)}, u32[]{:S(2)}) copy-start(bf16[128,1152]{1,0:T(8,128)(2,1)} %shard_map.143.normed.normed_far) | copy-start | bytes 884740
  63.2 19.6 %copy-start.2 = (bf16[24,96,128]{2,1,0:T(8,128)(2,1)S(1)}, bf16[24,96,128]{2,1,0:T(8,128)(2,1)}, u32[]{:S(2)}) copy-start(bf16[24,96,128]{2,1,0:T(8,128)(2,1)} %pair_far.3) | copy-start | bytes 1769476
  97.2 3.5 %collective-permute-start.2 = (bf16[2,12,64,96]{3,2,1,0:T(8,128)(2,1)S(1)}, bf16[2,12,64,96]{3,2,1,0:T(8,128)(2,1)S(1)}, u32[]{:S(2)}, u32[]{:S(2)}) collective-permute-start(bf16[2,12,64,96]{3,2,1,0:T(8,128)(2,1)S(1)} %get-tuple-element.46), channel_id=1, source_target_pairs={{0,1},{1,0},{2,3},{3,2},{4,5},{5,4},{6,7},{7,6},{8,9},{9,8},{10,11... | collective-permute-start | bytes 884744 | tf_op jit(solution)/shard_map/ppermute | solution.py:523
  97.2 11.5 %all-to-all-start.5 = ((bf16[16,24,128]{2,1,0:T(8,128)(2,1)}), bf16[16,24,128]{2,1,0:T(8,128)(2,1)S(1)}, u32[]{:S(2)}, u32[]{:S(2)}) async-start(bf16[16,24,128]{2,1,0:T(8,128)(2,1)} %shard_map.150), calls=%async_computation.5 | async-start | bytes 196608 | tf_op jit(solution)/shard_map/all_to_all | solution.py:519

commit v4 on v3

--- a/solution.py
+++ b/solution.py
@@ -159,34 +159,38 @@
         copy.wait()
 
 
-def turn_weights(share, ga, pa, gb, pb, go, wo, out, gates, values, last, arrivals):
-    hidden = go.shape[0]
+def normalize(pair_far, cotangent_far, normed, other, pair, arrivals):
+    count = pair.shape[0]
+    core = lax.axis_index("ch")
+    fetch = pltpu.make_async_copy(pair_far.at[pl.ds(core * count, count)], pair, arrivals.at[0])
+    cut = pltpu.make_async_copy(
+        cotangent_far.at[pl.ds((1 - core) * count, count)], other, arrivals.at[1]
+    )
+    start_all([fetch, cut])
+    fetch.wait()
+    normed[...] = normalized(pair[...])[0].astype(bf16)
+    cut.wait()
+
+
+def stack_up(*refs):
+    parts, out, arrivals = refs[:-2], refs[-2], refs[-1]
+    rows = parts[0].shape[0]
+    copies = [
+        pltpu.make_async_copy(part, out.at[at * rows : (at + 1) * rows], arrivals.at[at])
+        for at, part in enumerate(parts)
+    ]
+    start_all(copies)
+    wait_all(copies)
+
+
+def group_weights(share, stack, weights):
+    hidden = stack.shape[0] // 6
     width = 2 * hidden
-    copies = []
-    for at, (held, low, high) in enumerate(((gates, ga, gb), (values, pa, pb), (last, go, wo))):
-        copies.append(pltpu.make_async_copy(low, held.at[0:hidden], arrivals.at[2 * at]))
-        copies.append(pltpu.make_async_copy(high, held.at[hidden:width], arrivals.at[2 * at + 1]))
-    start_all(copies)
+    ga, pa, gb, pb = [stack[at * hidden : (at + 1) * hidden] for at in range(4)]
     order = grouping(hidden, share)
-    wait_all(copies)
-    out[:width] = dot(order, gates[...], (1, 0)).astype(bf16)
-    out[width : 2 * width] = dot(order, values[...], (1, 0)).astype(bf16)
-    out[2 * width :] = last[...]
-
-
-def normalize(pair_far, normed, pair, arrival):
-    count = pair.shape[0]
-    rows = pl.ds(lax.axis_index("ch") * count, count)
-    copy = pltpu.make_async_copy(pair_far.at[rows], pair, arrival)
-    copy.start()
-    copy.wait()
-    normed[...] = normalized(pair[...])[0].astype(bf16)
-
-
-def order_weights(own, other, weights):
-    core = lax.axis_index("ch")
-    weights[core] = own[...]
-    weights[1 - core] = other[...]
+    weights[:width] = dot(order, jnp.concatenate([ga, gb], 0), (1, 0)).astype(bf16)
+    weights[width : 2 * width] = dot(order, jnp.concatenate([pa, pb], 0), (1, 0)).astype(bf16)
+    weights[2 * width :] = stack[4 * hidden :]
 
 
 def rows_of(weights, start, count):
@@ -201,8 +205,10 @@
     return centred * rstd, rstd
 
 
-def edges(width, normed, own_weights, other_weights, send, weights):
-    order_weights(own_weights, other_weights, weights)
+def edges(width, share, normed, own_stack, other_stack, send, weights):
+    core = lax.axis_index("ch")
+    group_weights(share, own_stack, weights.at[core])
+    group_weights(share, other_stack, weights.at[1 - core])
     gate = jax.nn.sigmoid(dot(rows_of(weights, 0, width), normed[...], (1, 0)))
     value = dot(rows_of(weights, width, width), normed[...], (1, 0))
     send[...] = (gate * value).reshape(send.shape).astype(bf16)
@@ -285,9 +291,9 @@
 
 
 def head(
-    width, scale, arrived, own_weights, other_weights, normed_far, own_far, other_far,
+    width, scale, arrived, weights, normed_far, own_far, other_far,
     send, d_gate, terms, updated_own, updated_other,
-    normed, own, other, upstream, weights, arrivals,
+    normed, own, other, upstream, arrivals,
 ):
     parts, total, _ = weights.shape
     hidden = (total - 2 * width) // 2
@@ -300,7 +306,6 @@
         pltpu.make_async_copy(other_far, other, arrivals.at[2]),
     ]
     start_all(copies)
-    order_weights(own_weights, other_weights, weights)
     mixed = jnp.concatenate([arrived[s].astype(f32) for s in range(devices)], 0)
     average = jnp.mean(mixed, 0, keepdims=True)
     spread = jnp.mean(mixed * mixed, 0, keepdims=True) - average * average
@@ -335,9 +340,9 @@
 
 
 def tail(
-    width, scale, arrived, own_weights, other_weights, pair_far, d_gate_far, head_terms, updated_other,
+    width, scale, arrived, weights, pair_far, d_gate_far, head_terms, updated_other,
     send, grad_own, others,
-    pair, d_gate, whole, weights, arrivals,
+    pair, d_gate, whole, arrivals,
 ):
     parts, total, channels = weights.shape
     hidden = (total - 2 * width) // 2
@@ -349,7 +354,6 @@
         pltpu.make_async_copy(d_gate_far, d_gate, arrivals.at[1]),
     ]
     start_all(copies)
-    order_weights(own_weights, other_weights, weights)
     others[0] = updated_other[...]
     wait_all(copies)
     hat, inverse = normalized(pair[...])
@@ -431,34 +435,34 @@
     tokens = cols * col_parts
     scale = 1.0 / tokens
     swap = [(c, parts - 1 - c) for c in range(parts)]
-    whole_weight = pltpu.VMEM((2 * hidden, channels), bf16)
     weight = ((2 * width + 2 * hidden, channels), bf16)
+    part = ((count, hidden, cols), bf16)
     own = jnp.swapaxes(cotangent, 1, 2)
-    other = lax.dynamic_slice_in_dim(own, (1 - lax.axis_index("ch")) * count, count, 0)
-    other = lax.ppermute(other, "ch", swap)
-    (weights,) = call(
-        functools.partial(turn_weights, share),
+    (stack,) = call(
+        stack_up,
         [weight],
         (w_gate_a.T, w_proj_a.T, w_gate_b.T, w_proj_b.T, w_gate_out.T, w_out.T),
-        (whole_weight, whole_weight, whole_weight, pltpu.SemaphoreType.DMA((6,))),
+        (pltpu.SemaphoreType.DMA((6,)),),
         far=range(6),
+        outs_far=True,
         room=60,
     )
-    weights = (weights, lax.ppermute(weights, "ch", swap))
-    (normed,) = call(
+    other_stack = lax.ppermute(stack, "ch", swap)
+    normed, other = call(
         normalize,
-        [((channels, flat), bf16)],
-        (pair,),
-        (pltpu.VMEM((count, cols, channels), bf16), pltpu.SemaphoreType.DMA),
-        far=(0,),
-        room=60,
-    )
-    normed, other = lax.optimization_barrier((normed, other))
-    (send,) = call(
-        functools.partial(edges, width), [((devices, 2 * share, flat), bf16)], (normed, *weights),
-        (pltpu.VMEM((parts, *weight[0]), bf16),),
+        [((channels, flat), bf16), part],
+        (pair, own),
+        (pltpu.VMEM((count, cols, channels), bf16), pltpu.SemaphoreType.DMA((2,))),
+        far=(0, 1),
+    )
+    send, weights = call(
+        functools.partial(edges, width, share),
+        [((devices, 2 * share, flat), bf16), ((parts, *weight[0]), bf16)],
+        (normed, stack, other_stack),
     )
     arrived = lax.all_to_all(send, everyone, 0, 0)
+    arrived, other = lax.optimization_barrier((arrived, other))
+    other = lax.ppermute(other, "ch", swap)
     room = pltpu.VMEM((col_parts * tokens * 8, -(-cols // 128) * 128), f32)
     send, kept = call(
         functools.partial(mix, col_parts, cols),
@@ -466,8 +470,8 @@
         (arrived,),
         (room, room),
     )
+    send, other = lax.optimization_barrier((send, other))
     arrived = lax.all_to_all(send, everyone, 0, 0)
-    part = ((count, hidden, cols), bf16)
     send, d_gate, head_terms, updated_own, updated_other = call(
         functools.partial(head, width, scale),
         [
@@ -477,16 +481,15 @@
             part,
             part,
         ],
-        (arrived, *weights, normed, own, other),
+        (arrived, weights, normed, own, other),
         (
             pltpu.VMEM((channels, flat), bf16),
             pltpu.VMEM(*part),
             pltpu.VMEM(*part),
             pltpu.VMEM((hidden * parts, flat), f32),
-            pltpu.VMEM((parts, *weight[0]), bf16),
             pltpu.SemaphoreType.DMA((3,)),
         ),
-        far=(3, 4, 5),
+        far=(2, 3, 4),
     )
     arrived = lax.all_to_all(send, everyone, 0, 0)
     (send,) = call(
@@ -502,15 +505,14 @@
     send, grad_own, others = call(
         functools.partial(tail, width, scale),
         [((devices, per, channels), bf16), part, ((2, *part[0]), bf16)],
-        (arrived, *weights, pair, d_gate, head_terms, updated_other),
+        (arrived, weights, pair, d_gate, head_terms, updated_other),
         (
             pltpu.VMEM((count, cols, channels), bf16),
             pltpu.VMEM((hidden * parts, flat), bf16),
             pltpu.VMEM((total * parts, channels), f32),
-            pltpu.VMEM((parts, *weight[0]), bf16),
             pltpu.SemaphoreType.DMA((2,)),
         ),
-        far=(3, 4),
+        far=(2, 3),
     )
     arrived = lax.all_to_all(send, ("ch", "row", "col"), 0, 0)
     rest = devices // parts

time: 110 us -> 111 us (level)
  Pallas kernels: 13.4 us -> 14.7 us
    unnamed x10, local copies, waits for them, and re-layouts: 0.98 us -> 2.33 us
    pallas_call x10, Pallas kernels: 13.4 us -> 14.7 us  [call(): pl.pallas_call(kernel, out_shape=tuple((jax.ShapeDtypeStruct(*out) for ou...]
  transfers between devices with their start and end apart: 4 -> 4, of which waited for: 1 -> 1; matrix products, arithmetic and copies ran while one was open for 0% -> 0% of each run, Pallas kernels for 4% -> 3%
where the time goes in v4:
time: 111 us
  blocking collectives  82.1 us (74%)
  Pallas kernels  14.7 us (13%)
  waiting for transfers between devices  7.02 us (6%)
  starting transfers between devices  4.03 us (4%)
  local copies, waits for them, and re-layouts  2.33 us (2%)
    all_to_all x4, blocking collectives, by_channels(): arrived = lax.all_to_all(send, everyone, 0, 0)  70.2 us
    pallas_call x10, Pallas kernels, call(): pl.pallas_call(kernel, out_shape=tuple((jax.ShapeDtypeStruct(*out) for ou...  14.7 us
    all_to_all x1, blocking collectives, by_channels(): arrived = lax.all_to_all(send, ('ch', 'row', 'col'), 0, 0)  11.9 us
    all_to_all x1, waiting for transfers between devices, by_channels(): sums = lax.all_to_all(sums, ('row', 'col'), 0, 0)  7.02 us
    all_to_all x1, starting transfers between devices, by_channels(): sums = lax.all_to_all(sums, ('row', 'col'), 0, 0)  3.51 us
    unnamed x10, local copies, waits for them, and re-layouts  2.33 us
  transfers between devices with their start and end apart: 4, of which 1 were waited for; matrix products, arithmetic and copies ran while one was open for 0% of the time, Pallas kernels for 3%

profile of v4, /device:TPU:0, one launch (start us, length us, event | category | flops | bytes accessed | tf_op | source)
XLA Modules:
  0.0 110.9 jit_solution(9766991840790054492)
XLA Ops:
  0.6 4.1 %shard_map.144.own_stack = bf16[384,128]{1,0:T(8,128)(2,1)} custom-call(bf16[64,128]{1,0:T(8,128)(2,1)} %bitcast.17, bf16[64,128]{1,0:T(8,128)(2,1)} %bitcast.18, bf16[64,128]{1,0:T(8,128)(2,1)} %bitcast.19, bf16[64,128]{1,0:T(8,128)(2,1)} %bitcast.20, bf16[64,128]{1,0:T(8,128)(2,1)} %bitcast.21, bf16[64,128]{1,0:T(8,128)(2,1)} %bitcast.22), custom_call_target="tpu_custom_call" | custom-call | tf_op jit(solution)/shard_map/pallas_call | solution.py:132
  4.8 0.5 collective-permute-start
  5.3 0.0 copy-start
  5.3 1.1 copy-done
  6.4 0.0 copy-start.2
  6.4 1.0 copy-done.2
  7.4 0.0 copy-start.4
  7.4 0.6 shard_map.143
  8.0 0.0 collective-permute-done.other_stack
  8.0 0.3 copy-done.4
  8.2 0.6 shard_map.145
  8.9 24.1 %all_to_all.30.arrived = bf16[32,8,1152]{2,1,0:T(8,128)(2,1)S(1)} all-to-all(bf16[32,8,1152]{2,1,0:T(8,128)(2,1)S(1)} %get-tuple-element.40), channel_id=1, replica_groups=mesh['row'=8,'col'=2,'ch'=2] {'col','row','ch'}, dimensions={0} | all-to-all | bytes 1179648 | tf_op jit(solution)/shard_map/all_to_all | solution.py:463
  33.0 0.0 collective-permute-start.1
  33.0 1.5 %shard_map.146 = (bf16[32,4,1152]{2,1,0:T(4,128)(2,1)S(1)}, bf16[8,192,192]{2,1,0:T(8,128)(2,1)S(1)}) custom-call(bf16[32,8,1152]{2,1,0:T(8,128)(2,1)S(1)} %all_to_all.30.arrived), custom_call_target="tpu_custom_call" | custom-call | tf_op jit(solution)/shard_map/pallas_call | solution.py:132
  34.5 0.0 copy-start.3
  34.5 0.0 collective-permute-done.1.other_far
  34.5 13.2 %all_to_all.31.arrived = bf16[32,4,1152]{2,1,0:T(4,128)(2,1)S(1)} all-to-all(bf16[32,4,1152]{2,1,0:T(4,128)(2,1)S(1)} %get-tuple-element.45), channel_id=1, replica_groups=mesh['row'=8,'col'=2,'ch'=2] {'col','row','ch'}, dimensions={0} | all-to-all | bytes 589824 | tf_op jit(solution)/shard_map/all_to_all | solution.py:474
  47.7 0.0 copy-done.3
  47.7 1.9 %shard_map.147 = (bf16[32,4,1152]{2,1,0:T(4,128)(2,1)S(1)}, bf16[128,1152]{1,0:T(8,128)(2,1)S(1)}, f32[2,128,128]{2,1,0:T(8,128)S(1)}, bf16[12,64,96]{2,1,0:T(8,128)(2,1)S(1)}, bf16[12,64,96]{2,1,0:T(8,128)(2,1)S(1)}) custom-call(bf16[32,4,1152]{2,1,0:T(4,128)(2,1)S(1)} %all_to_all.31.arrived, bf16[2,384,128]{2,1,0:T(8,128)(2,1)S(1)} %get-tuple-element.46.weights, ...), custom_call_target="tpu_custom_call" | custom-call | tf_op jit(solution)/shard_map/pallas_call | solution.py:132
  49.6 13.3 %all_to_all.32.arrived = bf16[32,4,1152]{2,1,0:T(4,128)(2,1)S(1)} all-to-all(bf16[32,4,1152]{2,1,0:T(4,128)(2,1)S(1)} %get-tuple-element.48), channel_id=1, replica_groups=mesh['row'=8,'col'=2,'ch'=2] {'col','row','ch'}, dimensions={0} | all-to-all | bytes 589824 | tf_op jit(solution)/shard_map/all_to_all | solution.py:494
  62.9 1.6 %shard_map.148 = bf16[32,8,1152]{2,1,0:T(8,128)(2,1)S(1)} custom-call(bf16[32,4,1152]{2,1,0:T(4,128)(2,1)S(1)} %all_to_all.32.arrived, bf16[8,192,192]{2,1,0:T(8,128)(2,1)S(1)} %get-tuple-element.49.kept_far), custom_call_target="tpu_custom_call" | custom-call | tf_op jit(solution)/shard_map/pallas_call | solution.py:132
  64.5 0.0 copy-start.1
  64.5 19.6 %all_to_all.33.arrived = bf16[32,8,1152]{2,1,0:T(8,128)(2,1)S(1)} all-to-all(bf16[32,8,1152]{2,1,0:T(8,128)(2,1)S(1)} %shard_map.148), channel_id=1, replica_groups=mesh['row'=8,'col'=2,'ch'=2] {'col','row','ch'}, dimensions={0} | all-to-all | bytes 1179648 | tf_op jit(solution)/shard_map/all_to_all | solution.py:502
  84.2 0.0 copy-done.1
  84.2 1.8 %shard_map.149 = (bf16[32,24,128]{2,1,0:T(8,128)(2,1)S(1)}, bf16[12,64,96]{2,1,0:T(8,128)(2,1)S(1)}, bf16[2,12,64,96]{3,2,1,0:T(8,128)(2,1)S(1)}) custom-call(bf16[32,8,1152]{2,1,0:T(8,128)(2,1)S(1)} %all_to_all.33.arrived, bf16[2,384,128]{2,1,0:T(8,128)(2,1)S(1)} %get-tuple-element.46.weights, bf16[24,96,128]{2,1,0:T(8,128)(2,1)S(1)} %copy-done.1, ...), custom_call_target="tpu_custom_call" | custom-call | tf_op jit(solution)/shard_map/pallas_call | solution.py:132
  85.9 11.9 %all_to_all.34.arrived = bf16[32,24,128]{2,1,0:T(8,128)(2,1)S(1)} all-to-all(bf16[32,24,128]{2,1,0:T(8,128)(2,1)S(1)} %get-tuple-element.53), channel_id=1, replica_groups=mesh['row'=8,'col'=2,'ch'=2] {'ch','row','col'}, dimensions={0} | all-to-all | bytes 393216 | tf_op jit(solution)/shard_map/all_to_all | solution.py:517
  97.8 0.7 shard_map.150
  98.5 0.0 collective-permute-start.2
  98.5 3.5 %all-to-all-start.5 = ((bf16[16,24,128]{2,1,0:T(8,128)(2,1)}), bf16[16,24,128]{2,1,0:T(8,128)(2,1)S(1)}, u32[]{:S(2)}, u32[]{:S(2)}) async-start(bf16[16,24,128]{2,1,0:T(8,128)(2,1)} %shard_map.150), calls=%async_computation.5 | async-start | bytes 196608 | tf_op jit(solution)/shard_map/all_to_all | solution.py:521
  102.0 0.0 collective-permute-done.2.others
  102.0 0.9 shard_map.151
  102.9 7.0 %all-to-all-done.5.sums = bf16[16,24,128]{2,1,0:T(8,128)(2,1)S(1)} async-done(((bf16[16,24,128]{2,1,0:T(8,128)(2,1)}), bf16[16,24,128]{2,1,0:T(8,128)(2,1)S(1)}, u32[]{:S(2)}, u32[]{:S(2)}) %all-to-all-start.5) | async-done | bytes 98336 | tf_op jit(solution)/shard_map/all_to_all | solution.py:521
  110.0 0.9 shard_map.152
Async XLA Ops:
  4.8 3.2 %collective-permute-start = (bf16[384,128]{1,0:T(8,128)(2,1)}, bf16[384,128]{1,0:T(8,128)(2,1)S(1)}, u32[]{:S(2)}, u32[]{:S(2)}) collective-permute-start(bf16[384,128]{1,0:T(8,128)(2,1)} %shard_map.144.own_stack), channel_id=1, source_target_pairs={{0,1},{1,0},{2,3},{3,2},{4,5},{5,4},{6,7},{7,6},{8,9},{9,8},{10,11... | collective-permute-start | bytes 294920 | tf_op jit(solution)/shard_map/ppermute | solution.py:450
  5.3 1.1 copy-start
  6.4 1.0 copy-start.2
  7.4 0.9 copy-start.4
  33.0 1.6 %collective-permute-start.1 = (bf16[12,64,96]{2,1,0:T(8,128)(2,1)S(1)}, bf16[12,64,96]{2,1,0:T(8,128)(2,1)S(1)}, u32[]{:S(2)}, u32[]{:S(2)}) collective-permute-start(bf16[12,64,96]{2,1,0:T(8,128)(2,1)S(1)} %get-tuple-element.44), channel_id=1, source_target_pairs={{0,1},{1,0},{2,3},{3,2},{4,5},{5,4},{6,7},{7,6},{8,9},{9,8},{10,11... | collective-permute-start | bytes 442376 | tf_op jit(solution)/shard_map/ppermute | solution.py:465
  34.5 13.2 %copy-start.3 = (bf16[24,96,64]{1,2,0:T(8,128)(2,1)S(1)}, bf16[24,96,64]{1,2,0:T(8,128)(2,1)}, u32[]{:S(2)}) copy-start(bf16[24,96,64]{1,2,0:T(8,128)(2,1)} %param.9) | copy-start | bytes 884740
  64.5 19.6 %copy-start.1 = (bf16[24,96,128]{2,1,0:T(8,128)(2,1)S(1)}, bf16[24,96,128]{2,1,0:T(8,128)(2,1)}, u32[]{:S(2)}) copy-start(bf16[24,96,128]{2,1,0:T(8,128)(2,1)} %pair_far.3) | copy-start | bytes 1769476
  98.5 3.5 %collective-permute-start.2 = (bf16[2,12,64,96]{3,2,1,0:T(8,128)(2,1)S(1)}, bf16[2,12,64,96]{3,2,1,0:T(8,128)(2,1)S(1)}, u32[]{:S(2)}, u32[]{:S(2)}) collective-permute-start(bf16[2,12,64,96]{3,2,1,0:T(8,128)(2,1)S(1)} %get-tuple-element.58), channel_id=1, source_target_pairs={{0,1},{1,0},{2,3},{3,2},{4,5},{5,4},{6,7},{7,6},{8,9},{9,8},{10,11... | collective-permute-start | bytes 884744 | tf_op jit(solution)/shard_map/ppermute | solution.py:525
  98.5 11.5 %all-to-all-start.5 = ((bf16[16,24,128]{2,1,0:T(8,128)(2,1)}), bf16[16,24,128]{2,1,0:T(8,128)(2,1)S(1)}, u32[]{:S(2)}, u32[]{:S(2)}) async-start(bf16[16,24,128]{2,1,0:T(8,128)(2,1)} %shard_map.150), calls=%async_computation.5 | async-start | bytes 196608 | tf_op jit(solution)/shard_map/all_to_all | solution.py:521

commit v5 on v4

--- a/solution.py
+++ b/solution.py
@@ -159,38 +159,31 @@
         copy.wait()
 
 
-def normalize(pair_far, cotangent_far, normed, other, pair, arrivals):
+def prepare(
+    share, ga, pa, gb, pb, go, wo, pair_far, cotangent_far, out, normed, other,
+    gates, values, last, pair, arrivals,
+):
+    hidden = go.shape[0]
+    width = 2 * hidden
     count = pair.shape[0]
     core = lax.axis_index("ch")
-    fetch = pltpu.make_async_copy(pair_far.at[pl.ds(core * count, count)], pair, arrivals.at[0])
+    copies = []
+    for at, (held, low, high) in enumerate(((gates, ga, gb), (values, pa, pb), (last, go, wo))):
+        copies.append(pltpu.make_async_copy(low, held.at[0:hidden], arrivals.at[2 * at]))
+        copies.append(pltpu.make_async_copy(high, held.at[hidden:width], arrivals.at[2 * at + 1]))
+    fetch = pltpu.make_async_copy(pair_far.at[pl.ds(core * count, count)], pair, arrivals.at[6])
     cut = pltpu.make_async_copy(
-        cotangent_far.at[pl.ds((1 - core) * count, count)], other, arrivals.at[1]
-    )
-    start_all([fetch, cut])
+        cotangent_far.at[pl.ds((1 - core) * count, count)], other, arrivals.at[7]
+    )
+    start_all(copies + [fetch, cut])
+    order = grouping(hidden, share)
+    wait_all(copies)
+    out[:width] = dot(order, gates[...], (1, 0)).astype(bf16)
+    out[width : 2 * width] = dot(order, values[...], (1, 0)).astype(bf16)
+    out[2 * width :] = last[...]
     fetch.wait()
     normed[...] = normalized(pair[...])[0].astype(bf16)
     cut.wait()
-
-
-def stack_up(*refs):
-    parts, out, arrivals = refs[:-2], refs[-2], refs[-1]
-    rows = parts[0].shape[0]
-    copies = [
-        pltpu.make_async_copy(part, out.at[at * rows : (at + 1) * rows], arrivals.at[at])
-        for at, part in enumerate(parts)
-    ]
-    start_all(copies)
-    wait_all(copies)
-
-
-def group_weights(share, stack, weights):
-    hidden = stack.shape[0] // 6
-    width = 2 * hidden
-    ga, pa, gb, pb = [stack[at * hidden : (at + 1) * hidden] for at in range(4)]
-    order = grouping(hidden, share)
-    weights[:width] = dot(order, jnp.concatenate([ga, gb], 0), (1, 0)).astype(bf16)
-    weights[width : 2 * width] = dot(order, jnp.concatenate([pa, pb], 0), (1, 0)).astype(bf16)
-    weights[2 * width :] = stack[4 * hidden :]
 
 
 def rows_of(weights, start, count):
@@ -205,10 +198,7 @@
     return centred * rstd, rstd
 
 
-def edges(width, share, normed, own_stack, other_stack, send, weights):
-    core = lax.axis_index("ch")
-    group_weights(share, own_stack, weights.at[core])
-    group_weights(share, other_stack, weights.at[1 - core])
+def edges(width, normed, weights, send):
     gate = jax.nn.sigmoid(dot(rows_of(weights, 0, width), normed[...], (1, 0)))
     value = dot(rows_of(weights, width, width), normed[...], (1, 0))
     send[...] = (gate * value).reshape(send.shape).astype(bf16)
@@ -438,27 +428,24 @@
     weight = ((2 * width + 2 * hidden, channels), bf16)
     part = ((count, hidden, cols), bf16)
     own = jnp.swapaxes(cotangent, 1, 2)
-    (stack,) = call(
-        stack_up,
-        [weight],
-        (w_gate_a.T, w_proj_a.T, w_gate_b.T, w_proj_b.T, w_gate_out.T, w_out.T),
-        (pltpu.SemaphoreType.DMA((6,)),),
-        far=range(6),
-        outs_far=True,
+    whole_weight = pltpu.VMEM((2 * hidden, channels), bf16)
+    weights, normed, other = call(
+        functools.partial(prepare, share),
+        [weight, ((channels, flat), bf16), part],
+        (w_gate_a.T, w_proj_a.T, w_gate_b.T, w_proj_b.T, w_gate_out.T, w_out.T, pair, own),
+        (
+            whole_weight,
+            whole_weight,
+            whole_weight,
+            pltpu.VMEM((count, cols, channels), bf16),
+            pltpu.SemaphoreType.DMA((8,)),
+        ),
+        far=range(8),
         room=60,
     )
-    other_stack = lax.ppermute(stack, "ch", swap)
-    normed, other = call(
-        normalize,
-        [((channels, flat), bf16), part],
-        (pair, own),
-        (pltpu.VMEM((count, cols, channels), bf16), pltpu.SemaphoreType.DMA((2,))),
-        far=(0, 1),
-    )
-    send, weights = call(
-        functools.partial(edges, width, share),
-        [((devices, 2 * share, flat), bf16), ((parts, *weight[0]), bf16)],
-        (normed, stack, other_stack),
+    weights = lax.all_gather(weights, "ch")
+    (send,) = call(
+        functools.partial(edges, width), [((devices, 2 * share, flat), bf16)], (normed, weights)
     )
     arrived = lax.all_to_all(send, everyone, 0, 0)
     arrived, other = lax.optimization_barrier((arrived, other))

time: 111 us -> 108 us (0.973)
  Pallas kernels: 14.7 us -> 12 us
  blocking collectives: 82.1 us -> 84.7 us
  local copies, waits for them, and re-layouts: 2.33 us -> 0.03 us
    pallas_call x10 -> x9, Pallas kernels: 14.7 us -> 12 us  [call(): pl.pallas_call(kernel, out_shape=tuple((jax.ShapeDtypeStruct(*out) for ou...]
    all_gather x0 -> x1, blocking collectives: none -> 2.39 us  [by_channels(): weights = lax.all_gather(weights, 'ch')]
    unnamed x10 -> x8, local copies, waits for them, and re-layouts: 2.33 us -> 0.03 us
  transfers between devices with their start and end apart: 4 -> 3, of which waited for: 1 -> 1; matrix products, arithmetic and copies ran while one was open for 0% -> 0% of each run, Pallas kernels for 3% -> 2%
where the time goes in v5:
time: 108 us
  blocking collectives  84.7 us (78%)
  Pallas kernels  12 us (11%)
  waiting for transfers between devices  7.02 us (6%)
  starting transfers between devices  3.51 us (3%)
    all_to_all x4, blocking collectives, by_channels(): arrived = lax.all_to_all(send, everyone, 0, 0)  70.5 us
    pallas_call x9, Pallas kernels, call(): pl.pallas_call(kernel, out_shape=tuple((jax.ShapeDtypeStruct(*out) for ou...  12 us
    all_to_all x1, blocking collectives, by_channels(): arrived = lax.all_to_all(send, ('ch', 'row', 'col'), 0, 0)  11.9 us
    all_to_all x1, waiting for transfers between devices, by_channels(): sums = lax.all_to_all(sums, ('row', 'col'), 0, 0)  7.02 us
    all_to_all x1, starting transfers between devices, by_channels(): sums = lax.all_to_all(sums, ('row', 'col'), 0, 0)  3.51 us
    all_gather x1, blocking collectives, by_channels(): weights = lax.all_gather(weights, 'ch')  2.39 us
  transfers between devices with their start and end apart: 3, of which 1 were waited for; matrix products, arithmetic and copies ran while one was open for 0% of the time, Pallas kernels for 2%

profile of v5, /device:TPU:0, one launch (start us, length us, event | category | flops | bytes accessed | tf_op | source)
XLA Modules:
  0.0 108.0 jit_solution(2529337350717553070)
XLA Ops:
  0.6 2.2 %shard_map.143 = (bf16[384,128]{1,0:T(8,128)(2,1)}, bf16[128,1152]{1,0:T(8,128)(2,1)}, bf16[12,64,96]{2,1,0:T(8,128)(2,1)}) custom-call(bf16[64,128]{1,0:T(8,128)(2,1)} %bitcast.21, bf16[64,128]{1,0:T(8,128)(2,1)} %bitcast.22, bf16[64,128]{1,0:T(8,128)(2,1)} %bitcast.23, bf16[64,128]{1,0:T(8,128)(2,1)} %bitcast.24, bf16[64,128]{1,0:T(8,128)(2,1)} %bitcast.25, ...), custom_call_target="tpu_custom_call" | custom-call | tf_op jit(solution)/shard_map/pallas_call | solution.py:132
  2.9 0.0 copy-start.2
  2.9 2.4 %all-gather = bf16[768,128]{1,0:T(8,128)(2,1)S(1)} all-gather(bf16[384,128]{1,0:T(8,128)(2,1)} %get-tuple-element.39), channel_id=2, replica_groups=mesh['row'=8,'col'=2,'ch'=2] {'ch'}, dimensions={0}, use_global_device_ids=true | all-gather | bytes 294912 | tf_op jit(solution)/shard_map/all_gather | solution.py:446
  5.3 0.0 copy-done.2
  5.3 0.5 shard_map.144
  5.7 0.0 copy-start.3
  5.7 24.3 %all_to_all.30.arrived = bf16[32,8,1152]{2,1,0:T(8,128)(2,1)S(1)} all-to-all(bf16[32,8,1152]{2,1,0:T(8,128)(2,1)S(1)} %shard_map.144), channel_id=1, replica_groups=mesh['row'=8,'col'=2,'ch'=2] {'col','row','ch'}, dimensions={0} | all-to-all | bytes 1179648 | tf_op jit(solution)/shard_map/all_to_all | solution.py:450
  30.1 0.0 copy-done.3
  30.1 0.0 collective-permute-start
  30.1 1.6 %shard_map.145 = (bf16[32,4,1152]{2,1,0:T(4,128)(2,1)S(1)}, bf16[8,192,192]{2,1,0:T(8,128)(2,1)S(1)}) custom-call(bf16[32,8,1152]{2,1,0:T(8,128)(2,1)S(1)} %all_to_all.30.arrived), custom_call_target="tpu_custom_call" | custom-call | tf_op jit(solution)/shard_map/pallas_call | solution.py:132
  31.6 0.0 copy-start.1
  31.7 0.0 collective-permute-done.other_far
  31.7 13.2 %all_to_all.31.arrived = bf16[32,4,1152]{2,1,0:T(4,128)(2,1)S(1)} all-to-all(bf16[32,4,1152]{2,1,0:T(4,128)(2,1)S(1)} %get-tuple-element.44), channel_id=1, replica_groups=mesh['row'=8,'col'=2,'ch'=2] {'col','row','ch'}, dimensions={0} | all-to-all | bytes 589824 | tf_op jit(solution)/shard_map/all_to_all | solution.py:461
  44.8 0.0 copy-done.1
  44.9 1.9 %shard_map.146 = (bf16[32,4,1152]{2,1,0:T(4,128)(2,1)S(1)}, bf16[128,1152]{1,0:T(8,128)(2,1)S(1)}, f32[2,128,128]{2,1,0:T(8,128)S(1)}, bf16[12,64,96]{2,1,0:T(8,128)(2,1)S(1)}, bf16[12,64,96]{2,1,0:T(8,128)(2,1)S(1)}) custom-call(bf16[32,4,1152]{2,1,0:T(4,128)(2,1)S(1)} %all_to_all.31.arrived, bf16[2,384,128]{2,1,0:T(8,128)(2,1)S(1)} %bitcast.17, ...), custom_call_target="tpu_custom_call" | custom-call | tf_op jit(solution)/shard_map/pallas_call | solution.py:132
  46.7 13.3 %all_to_all.32.arrived = bf16[32,4,1152]{2,1,0:T(4,128)(2,1)S(1)} all-to-all(bf16[32,4,1152]{2,1,0:T(4,128)(2,1)S(1)} %get-tuple-element.46), channel_id=1, replica_groups=mesh['row'=8,'col'=2,'ch'=2] {'col','row','ch'}, dimensions={0} | all-to-all | bytes 589824 | tf_op jit(solution)/shard_map/all_to_all | solution.py:481
  60.0 1.6 %shard_map.147 = bf16[32,8,1152]{2,1,0:T(8,128)(2,1)S(1)} custom-call(bf16[32,4,1152]{2,1,0:T(4,128)(2,1)S(1)} %all_to_all.32.arrived, bf16[8,192,192]{2,1,0:T(8,128)(2,1)S(1)} %get-tuple-element.47.kept_far), custom_call_target="tpu_custom_call" | custom-call | tf_op jit(solution)/shard_map/pallas_call | solution.py:132
  61.6 0.0 copy-start
  61.7 19.6 %all_to_all.33.arrived = bf16[32,8,1152]{2,1,0:T(8,128)(2,1)S(1)} all-to-all(bf16[32,8,1152]{2,1,0:T(8,128)(2,1)S(1)} %shard_map.147), channel_id=1, replica_groups=mesh['row'=8,'col'=2,'ch'=2] {'col','row','ch'}, dimensions={0} | all-to-all | bytes 1179648 | tf_op jit(solution)/shard_map/all_to_all | solution.py:489
  81.3 0.0 copy-done
  81.3 1.8 %shard_map.148 = (bf16[32,24,128]{2,1,0:T(8,128)(2,1)S(1)}, bf16[12,64,96]{2,1,0:T(8,128)(2,1)S(1)}, bf16[2,12,64,96]{3,2,1,0:T(8,128)(2,1)S(1)}) custom-call(bf16[32,8,1152]{2,1,0:T(8,128)(2,1)S(1)} %all_to_all.33.arrived, bf16[2,384,128]{2,1,0:T(8,128)(2,1)S(1)} %bitcast.18, bf16[24,96,128]{2,1,0:T(8,128)(2,1)S(1)} %copy-done, ...), custom_call_target="tpu_custom_call" | custom-call | tf_op jit(solution)/shard_map/pallas_call | solution.py:132
  83.1 11.9 %all_to_all.34.arrived = bf16[32,24,128]{2,1,0:T(8,128)(2,1)S(1)} all-to-all(bf16[32,24,128]{2,1,0:T(8,128)(2,1)S(1)} %get-tuple-element.51), channel_id=1, replica_groups=mesh['row'=8,'col'=2,'ch'=2] {'ch','row','col'}, dimensions={0} | all-to-all | bytes 393216 | tf_op jit(solution)/shard_map/all_to_all | solution.py:504
  94.9 0.7 shard_map.149
  95.6 0.0 collective-permute-start.1
  95.6 3.5 %all-to-all-start.5 = ((bf16[16,24,128]{2,1,0:T(8,128)(2,1)}), bf16[16,24,128]{2,1,0:T(8,128)(2,1)S(1)}, u32[]{:S(2)}, u32[]{:S(2)}) async-start(bf16[16,24,128]{2,1,0:T(8,128)(2,1)} %shard_map.149), calls=%async_computation.5 | async-start | bytes 196608 | tf_op jit(solution)/shard_map/all_to_all | solution.py:508
  99.1 0.0 collective-permute-done.1.others
  99.1 0.9 shard_map.150
  100.1 7.0 %all-to-all-done.5.sums = bf16[16,24,128]{2,1,0:T(8,128)(2,1)S(1)} async-done(((bf16[16,24,128]{2,1,0:T(8,128)(2,1)}), bf16[16,24,128]{2,1,0:T(8,128)(2,1)S(1)}, u32[]{:S(2)}, u32[]{:S(2)}) %all-to-all-start.5) | async-done | bytes 98336 | tf_op jit(solution)/shard_map/all_to_all | solution.py:508
  107.1 0.9 shard_map.151
Async XLA Ops:
  2.9 2.4 %copy-start.2 = (bf16[128,1152]{1,0:T(8,128)(2,1)S(1)}, bf16[128,1152]{1,0:T(8,128)(2,1)}, u32[]{:S(2)}) copy-start(bf16[128,1152]{1,0:T(8,128)(2,1)} %get-tuple-element.38.normed.normed_far) | copy-start | bytes 884740
  5.7 24.3 %copy-start.3 = (bf16[12,64,96]{2,1,0:T(8,128)(2,1)S(1)}, bf16[12,64,96]{2,1,0:T(8,128)(2,1)}, u32[]{:S(2)}) copy-start(bf16[12,64,96]{2,1,0:T(8,128)(2,1)} %get-tuple-element.43) | copy-start | bytes 442372
  30.1 1.6 %collective-permute-start = (bf16[12,64,96]{2,1,0:T(8,128)(2,1)S(1)}, bf16[12,64,96]{2,1,0:T(8,128)(2,1)S(1)}, u32[]{:S(2)}, u32[]{:S(2)}) collective-permute-start(bf16[12,64,96]{2,1,0:T(8,128)(2,1)S(1)} %copy-done.3), channel_id=1, source_target_pairs={{0,1},{1,0},{2,3},{3,2},{4,5},{5,4},{6,7},{7,6},{8,9},{9,8},{10,11... | collective-permute-start | bytes 442376 | tf_op jit(solution)/shard_map/ppermute | solution.py:452
  31.6 13.2 %copy-start.1 = (bf16[24,96,64]{1,2,0:T(8,128)(2,1)S(1)}, bf16[24,96,64]{1,2,0:T(8,128)(2,1)}, u32[]{:S(2)}) copy-start(bf16[24,96,64]{1,2,0:T(8,128)(2,1)} %param.9) | copy-start | bytes 884740
  61.6 19.6 %copy-start = (bf16[24,96,128]{2,1,0:T(8,128)(2,1)S(1)}, bf16[24,96,128]{2,1,0:T(8,128)(2,1)}, u32[]{:S(2)}) copy-start(bf16[24,96,128]{2,1,0:T(8,128)(2,1)} %pair_far.3) | copy-start | bytes 1769476
  95.6 3.5 %collective-permute-start.1 = (bf16[2,12,64,96]{3,2,1,0:T(8,128)(2,1)S(1)}, bf16[2,12,64,96]{3,2,1,0:T(8,128)(2,1)S(1)}, u32[]{:S(2)}, u32[]{:S(2)}) collective-permute-start(bf16[2,12,64,96]{3,2,1,0:T(8,128)(2,1)S(1)} %get-tuple-element.56), channel_id=1, source_target_pairs={{0,1},{1,0},{2,3},{3,2},{4,5},{5,4},{6,7},{7,6},{8,9},{9,8},{10,11... | collective-permute-start | bytes 884744 | tf_op jit(solution)/shard_map/ppermute | solution.py:512
  95.6 11.5 %all-to-all-start.5 = ((bf16[16,24,128]{2,1,0:T(8,128)(2,1)}), bf16[16,24,128]{2,1,0:T(8,128)(2,1)S(1)}, u32[]{:S(2)}, u32[]{:S(2)}) async-start(bf16[16,24,128]{2,1,0:T(8,128)(2,1)} %shard_map.149), calls=%async_computation.5 | async-start | bytes 196608 | tf_op jit(solution)/shard_map/all_to_all | solution.py:508

commit v6 on v5

--- a/solution.py
+++ b/solution.py
@@ -198,7 +198,10 @@
     return centred * rstd, rstd
 
 
-def edges(width, normed, weights, send):
+def edges(width, normed, own, other, send, weights):
+    core = lax.axis_index("ch")
+    weights[core] = own[...]
+    weights[1 - core] = other[...]
     gate = jax.nn.sigmoid(dot(rows_of(weights, 0, width), normed[...], (1, 0)))
     value = dot(rows_of(weights, width, width), normed[...], (1, 0))
     send[...] = (gate * value).reshape(send.shape).astype(bf16)
@@ -380,8 +383,16 @@
         out[s] = total
 
 
-def turn_back(share, sums, *refs):
-    outs, whole, results, leaves = refs[:6], refs[6], refs[7], refs[8]
+def finish(share, sums, updated_own, grad_own, others, *refs):
+    (updated, grad), outs, (whole, results, leaves) = refs[:2], refs[2:8], refs[8:]
+    count = updated_own.shape[0]
+    core = lax.axis_index("ch")
+    here, there = pl.ds(core * count, count), pl.ds((1 - core) * count, count)
+    joins = []
+    for at, (own, out) in enumerate(((updated_own, updated), (grad_own, grad))):
+        joins.append(pltpu.make_async_copy(own, out.at[here], leaves.at[2 * at]))
+        joins.append(pltpu.make_async_copy(others.at[at], out.at[there], leaves.at[2 * at + 1]))
+    start_all(joins)
     _, hidden, channels = results.shape
     width = 2 * hidden
     per = sums.shape[1]
@@ -395,22 +406,10 @@
     results[4] = whole[2 * width : 2 * width + hidden]
     results[5] = whole[2 * width + hidden :]
     copies = [
-        pltpu.make_async_copy(results.at[at], out, leaves.at[at]) for at, out in enumerate(outs)
+        pltpu.make_async_copy(results.at[at], out, leaves.at[4 + at]) for at, out in enumerate(outs)
     ]
     start_all(copies)
-    wait_all(copies)
-
-
-def join_rows(updated_own, grad_own, others, updated, grad, leaves):
-    count = updated_own.shape[0]
-    core = lax.axis_index("ch")
-    here, there = pl.ds(core * count, count), pl.ds((1 - core) * count, count)
-    copies = []
-    for at, (own, out) in enumerate(((updated_own, updated), (grad_own, grad))):
-        copies.append(pltpu.make_async_copy(own, out.at[here], leaves.at[2 * at]))
-        copies.append(pltpu.make_async_copy(others.at[at], out.at[there], leaves.at[2 * at + 1]))
-    start_all(copies)
-    wait_all(copies)
+    wait_all(joins + copies)
 
 
 def by_channels(pair, cotangent, w_gate_a, w_proj_a, w_gate_b, w_proj_b, w_gate_out, w_out):
@@ -443,9 +442,10 @@
         far=range(8),
         room=60,
     )
-    weights = lax.all_gather(weights, "ch")
-    (send,) = call(
-        functools.partial(edges, width), [((devices, 2 * share, flat), bf16)], (normed, weights)
+    send, weights = call(
+        functools.partial(edges, width),
+        [((devices, 2 * share, flat), bf16), ((parts, *weight[0]), bf16)],
+        (normed, weights, lax.ppermute(weights, "ch", swap)),
     )
     arrived = lax.all_to_all(send, everyone, 0, 0)
     arrived, other = lax.optimization_barrier((arrived, other))
@@ -504,27 +504,18 @@
     arrived = lax.all_to_all(send, ("ch", "row", "col"), 0, 0)
     rest = devices // parts
     (sums,) = call(add_up, [((rest, per, channels), bf16)], (arrived,))
-    sums, others = lax.optimization_barrier((sums, others))
     sums = lax.all_to_all(sums, ("row", "col"), 0, 0)
-    updated, grad_pair = call(
-        join_rows,
-        [((row_count, hidden, cols), bf16)] * 2,
-        (updated_own, grad_own, lax.ppermute(others, "ch", swap)),
-        (pltpu.SemaphoreType.DMA((4,)),),
-        (0, 1, 2),
-        True,
-    )
-    sums, updated, grad_pair = lax.optimization_barrier((sums, updated, grad_pair))
-    grads = call(
-        functools.partial(turn_back, share),
-        [((hidden, channels), f32)] * 6,
-        (sums,),
+    updated, grad_pair, *grads = call(
+        functools.partial(finish, share),
+        [((row_count, hidden, cols), bf16)] * 2 + [((hidden, channels), f32)] * 6,
+        (sums, updated_own, grad_own, lax.ppermute(others, "ch", swap)),
         (
             pltpu.VMEM((total, channels), f32),
             pltpu.VMEM((6, hidden, channels), f32),
-            pltpu.SemaphoreType.DMA((6,)),
+            pltpu.SemaphoreType.DMA((10,)),
         ),
-        outs_far=True,
+        (1, 2, 3),
+        True,
     )
     return jnp.swapaxes(updated, 1, 2), jnp.swapaxes(grad_pair, 1, 2), *(g.T for g in grads)
 

time: 108 us -> 110 us (1.019)
  blocking collectives: 84.7 us -> 70.5 us
  waiting for transfers between devices: 7.02 us -> 18.4 us
  starting transfers between devices: 3.51 us -> 6.8 us
  local copies, waits for them, and re-layouts: 0.03 us -> 1.88 us
    all_to_all x1 -> x0, blocking collectives: 11.9 us -> none  [by_channels(): arrived = lax.all_to_all(send, ('ch', 'row', 'col'), 0, 0)]
    all_to_all x0 -> x1, waiting for transfers between devices: none -> 9.63 us  [by_channels(): arrived = lax.all_to_all(send, ('ch', 'row', 'col'), 0, 0)]
    all_to_all x0 -> x1, starting transfers between devices: none -> 2.6 us  [by_channels(): arrived = lax.all_to_all(send, ('ch', 'row', 'col'), 0, 0)]
    all_gather x1 -> x0, blocking collectives: 2.39 us -> none  [by_channels(): weights = lax.all_gather(weights, 'ch')]
    unnamed x8 -> x12, local copies, waits for them, and re-layouts: 0.03 us -> 1.88 us
    ppermute x0 -> x1, waiting for transfers between devices: none -> 1.15 us  [by_channels(): lax.ppermute(weights, 'ch', swap)]
    pallas_call x9 -> x8, Pallas kernels: 12 us -> 11.8 us  [call(): pl.pallas_call(kernel, out_shape=tuple((jax.ShapeDtypeStruct(*out) for ou...]
  transfers between devices with their start and end apart: 3 -> 5, of which waited for: 1 -> 3; matrix products, arithmetic and copies ran while one was open for 0% -> 0% of each run, Pallas kernels for 2% -> 2%
where the time goes in v6:
time: 110 us
  blocking collectives  70.5 us (64%)
  waiting for transfers between devices  18.4 us (17%)
  Pallas kernels  11.8 us (11%)
  starting transfers between devices  6.8 us (6%)
  local copies, waits for them, and re-layouts  1.88 us (2%)
    all_to_all x4, blocking collectives, by_channels(): arrived = lax.all_to_all(send, everyone, 0, 0)  70.5 us
    pallas_call x8, Pallas kernels, call(): pl.pallas_call(kernel, out_shape=tuple((jax.ShapeDtypeStruct(*out) for ou...  11.8 us
    all_to_all x1, waiting for transfers between devices, by_channels(): arrived = lax.all_to_all(send, ('ch', 'row', 'col'), 0, 0)  9.63 us
    all_to_all x1, waiting for transfers between devices, by_channels(): sums = lax.all_to_all(sums, ('row', 'col'), 0, 0)  7.62 us
    all_to_all x1, starting transfers between devices, by_channels(): sums = lax.all_to_all(sums, ('row', 'col'), 0, 0)  3.51 us
    all_to_all x1, starting transfers between devices, by_channels(): arrived = lax.all_to_all(send, ('ch', 'row', 'col'), 0, 0)  2.6 us
  transfers between devices with their start and end apart: 5, of which 3 were waited for; matrix products, arithmetic and copies ran while one was open for 0% of the time, Pallas kernels for 2%

profile of v6, /device:TPU:0, one launch (start us, length us, event | category | flops | bytes accessed | tf_op | source)
XLA Modules:
  0.0 110.1 jit_solution(14446499626075355393)
XLA Ops:
  0.6 2.2 %shard_map.143 = (bf16[384,128]{1,0:T(8,128)(2,1)}, bf16[128,1152]{1,0:T(8,128)(2,1)}, bf16[12,64,96]{2,1,0:T(8,128)(2,1)}) custom-call(bf16[64,128]{1,0:T(8,128)(2,1)} %bitcast.17, bf16[64,128]{1,0:T(8,128)(2,1)} %bitcast.18, bf16[64,128]{1,0:T(8,128)(2,1)} %bitcast.19, bf16[64,128]{1,0:T(8,128)(2,1)} %bitcast.20, bf16[64,128]{1,0:T(8,128)(2,1)} %bitcast.21, ...), custom_call_target="tpu_custom_call" | custom-call | tf_op jit(solution)/shard_map/pallas_call | solution.py:132
  2.9 0.5 collective-permute-start
  3.4 1.2 %collective-permute-done.other = bf16[384,128]{1,0:T(8,128)(2,1)S(1)} collective-permute-done((bf16[384,128]{1,0:T(8,128)(2,1)}, bf16[384,128]{1,0:T(8,128)(2,1)S(1)}, u32[]{:S(2)}, u32[]{:S(2)}) %collective-permute-start) | collective-permute-done | bytes 98336 | tf_op jit(solution)/shard_map/ppermute | solution.py:448
  4.5 0.0 copy-start.2
  4.6 1.0 copy-done.2
  5.5 0.0 copy-start.4
  5.5 0.9 copy-done.4
  6.4 0.4 shard_map.144
  6.9 0.0 copy-start.5
  6.9 24.3 %all_to_all.30.arrived = bf16[32,8,1152]{2,1,0:T(8,128)(2,1)S(1)} all-to-all(bf16[32,8,1152]{2,1,0:T(8,128)(2,1)S(1)} %get-tuple-element.37), channel_id=1, replica_groups=mesh['row'=8,'col'=2,'ch'=2] {'col','row','ch'}, dimensions={0} | all-to-all | bytes 1179648 | tf_op jit(solution)/shard_map/all_to_all | solution.py:450
  31.2 0.0 copy-done.5
  31.2 0.0 collective-permute-start.1
  31.2 0.0 copy-start.3
  31.2 1.5 %shard_map.145 = (bf16[32,4,1152]{2,1,0:T(4,128)(2,1)S(1)}, bf16[8,192,192]{2,1,0:T(8,128)(2,1)S(1)}) custom-call(bf16[32,8,1152]{2,1,0:T(8,128)(2,1)S(1)} %all_to_all.30.arrived), custom_call_target="tpu_custom_call" | custom-call | tf_op jit(solution)/shard_map/pallas_call | solution.py:132
  32.8 0.0 copy-start.1
  32.8 0.0 collective-permute-done.1.other_far
  32.8 13.2 %all_to_all.31.arrived = bf16[32,4,1152]{2,1,0:T(4,128)(2,1)S(1)} all-to-all(bf16[32,4,1152]{2,1,0:T(4,128)(2,1)S(1)} %get-tuple-element.42), channel_id=1, replica_groups=mesh['row'=8,'col'=2,'ch'=2] {'col','row','ch'}, dimensions={0} | all-to-all | bytes 589824 | tf_op jit(solution)/shard_map/all_to_all | solution.py:461
  46.0 0.0 copy-done.3
  46.0 0.0 copy-done.1
  46.0 1.9 %shard_map.146 = (bf16[32,4,1152]{2,1,0:T(4,128)(2,1)S(1)}, bf16[128,1152]{1,0:T(8,128)(2,1)S(1)}, f32[2,128,128]{2,1,0:T(8,128)S(1)}, bf16[12,64,96]{2,1,0:T(8,128)(2,1)S(1)}, bf16[12,64,96]{2,1,0:T(8,128)(2,1)S(1)}) custom-call(bf16[32,4,1152]{2,1,0:T(4,128)(2,1)S(1)} %all_to_all.31.arrived, bf16[2,384,128]{2,1,0:T(8,128)(2,1)S(1)} %get-tuple-element.43.weights, ...), custom_call_target="tpu_custom_call" | custom-call | tf_op jit(solution)/shard_map/pallas_call | solution.py:132
  47.9 13.3 %all_to_all.32.arrived = bf16[32,4,1152]{2,1,0:T(4,128)(2,1)S(1)} all-to-all(bf16[32,4,1152]{2,1,0:T(4,128)(2,1)S(1)} %get-tuple-element.45), channel_id=1, replica_groups=mesh['row'=8,'col'=2,'ch'=2] {'col','row','ch'}, dimensions={0} | all-to-all | bytes 589824 | tf_op jit(solution)/shard_map/all_to_all | solution.py:481
  61.2 1.6 %shard_map.147 = bf16[32,8,1152]{2,1,0:T(8,128)(2,1)S(1)} custom-call(bf16[32,4,1152]{2,1,0:T(4,128)(2,1)S(1)} %all_to_all.32.arrived, bf16[8,192,192]{2,1,0:T(8,128)(2,1)S(1)} %get-tuple-element.46.kept_far), custom_call_target="tpu_custom_call" | custom-call | tf_op jit(solution)/shard_map/pallas_call | solution.py:132
  62.8 0.0 copy-start
  62.8 19.6 %all_to_all.33.arrived = bf16[32,8,1152]{2,1,0:T(8,128)(2,1)S(1)} all-to-all(bf16[32,8,1152]{2,1,0:T(8,128)(2,1)S(1)} %shard_map.147), channel_id=1, replica_groups=mesh['row'=8,'col'=2,'ch'=2] {'col','row','ch'}, dimensions={0} | all-to-all | bytes 1179648 | tf_op jit(solution)/shard_map/all_to_all | solution.py:489
  82.4 0.0 copy-done
  82.4 2.4 %shard_map.148 = (bf16[32,24,128]{2,1,0:T(8,128)(2,1)}, bf16[12,64,96]{2,1,0:T(8,128)(2,1)S(1)}, bf16[2,12,64,96]{3,2,1,0:T(8,128)(2,1)S(1)}) custom-call(bf16[32,8,1152]{2,1,0:T(8,128)(2,1)S(1)} %all_to_all.33.arrived, bf16[2,384,128]{2,1,0:T(8,128)(2,1)S(1)} %get-tuple-element.43.weights, bf16[24,96,128]{2,1,0:T(8,128)(2,1)S(1)} %copy-done, ...), custom_call_target="tpu_custom_call" | custom-call | tf_op jit(solution)/shard_map/pallas_call | solution.py:132
  84.8 2.6 %all-to-all-start.4 = ((bf16[32,24,128]{2,1,0:T(8,128)(2,1)}), bf16[32,24,128]{2,1,0:T(8,128)(2,1)S(1)}, u32[]{:S(2)}, u32[]{:S(2)}) async-start(bf16[32,24,128]{2,1,0:T(8,128)(2,1)} %get-tuple-element.50), calls=%async_computation.4 | async-start | bytes 393216 | tf_op jit(solution)/shard_map/all_to_all | solution.py:504
  87.4 0.2 collective-permute-start.2
  87.6 9.6 %all-to-all-done.4.arrived = bf16[32,24,128]{2,1,0:T(8,128)(2,1)S(1)} async-done(((bf16[32,24,128]{2,1,0:T(8,128)(2,1)}), bf16[32,24,128]{2,1,0:T(8,128)(2,1)S(1)}, u32[]{:S(2)}, u32[]{:S(2)}) %all-to-all-start.4) | async-done | bytes 196640 | tf_op jit(solution)/shard_map/all_to_all | solution.py:504
  97.2 0.7 shard_map.149
  97.9 3.5 %all-to-all-start.5 = ((bf16[16,24,128]{2,1,0:T(8,128)(2,1)}), bf16[16,24,128]{2,1,0:T(8,128)(2,1)S(1)}, u32[]{:S(2)}, u32[]{:S(2)}) async-start(bf16[16,24,128]{2,1,0:T(8,128)(2,1)} %shard_map.149), calls=%async_computation.5 | async-start | bytes 196608 | tf_op jit(solution)/shard_map/all_to_all | solution.py:507
  101.4 0.0 collective-permute-done.2.others
  101.4 7.6 %all-to-all-done.5.sums = bf16[16,24,128]{2,1,0:T(8,128)(2,1)S(1)} async-done(((bf16[16,24,128]{2,1,0:T(8,128)(2,1)}), bf16[16,24,128]{2,1,0:T(8,128)(2,1)S(1)}, u32[]{:S(2)}, u32[]{:S(2)}) %all-to-all-start.5) | async-done | bytes 98336 | tf_op jit(solution)/shard_map/all_to_all | solution.py:507
  109.0 1.0 shard_map.150
Async XLA Ops:
  2.9 1.7 %collective-permute-start = (bf16[384,128]{1,0:T(8,128)(2,1)}, bf16[384,128]{1,0:T(8,128)(2,1)S(1)}, u32[]{:S(2)}, u32[]{:S(2)}) collective-permute-start(bf16[384,128]{1,0:T(8,128)(2,1)} %get-tuple-element.36.own), channel_id=1, source_target_pairs={{0,1},{1,0},{2,3},{3,2},{4,5},{5,4},{6,7},{7,6},{8,9},{9,8},{10,11... | collective-permute-start | bytes 294920 | tf_op jit(solution)/shard_map/ppermute | solution.py:448
  4.5 1.0 copy-start.2
  5.5 0.9 copy-start.4
  6.9 24.3 %copy-start.5 = (bf16[12,64,96]{2,1,0:T(8,128)(2,1)S(1)}, bf16[12,64,96]{2,1,0:T(8,128)(2,1)}, u32[]{:S(2)}) copy-start(bf16[12,64,96]{2,1,0:T(8,128)(2,1)} %get-tuple-element.41) | copy-start | bytes 442372
  31.2 1.6 %collective-permute-start.1 = (bf16[12,64,96]{2,1,0:T(8,128)(2,1)S(1)}, bf16[12,64,96]{2,1,0:T(8,128)(2,1)S(1)}, u32[]{:S(2)}, u32[]{:S(2)}) collective-permute-start(bf16[12,64,96]{2,1,0:T(8,128)(2,1)S(1)} %copy-done.5), channel_id=1, source_target_pairs={{0,1},{1,0},{2,3},{3,2},{4,5},{5,4},{6,7},{7,6},{8,9},{9,8},{10,11... | collective-permute-start | bytes 442376 | tf_op jit(solution)/shard_map/ppermute | solution.py:452
  31.2 14.8 %copy-start.3 = (bf16[128,1152]{1,0:T(8,128)(2,1)S(1)}, bf16[128,1152]{1,0:T(8,128)(2,1)}, u32[]{:S(2)}) copy-start(bf16[128,1152]{1,0:T(8,128)(2,1)} %get-tuple-element.35.normed.normed_far) | copy-start | bytes 884740
  32.8 13.2 %copy-start.1 = (bf16[24,96,64]{1,2,0:T(8,128)(2,1)S(1)}, bf16[24,96,64]{1,2,0:T(8,128)(2,1)}, u32[]{:S(2)}) copy-start(bf16[24,96,64]{1,2,0:T(8,128)(2,1)} %param.9) | copy-start | bytes 884740
  62.8 19.6 %copy-start = (bf16[24,96,128]{2,1,0:T(8,128)(2,1)S(1)}, bf16[24,96,128]{2,1,0:T(8,128)(2,1)}, u32[]{:S(2)}) copy-start(bf16[24,96,128]{2,1,0:T(8,128)(2,1)} %pair_far.3) | copy-start | bytes 1769476
  84.8 12.4 %all-to-all-start.4 = ((bf16[32,24,128]{2,1,0:T(8,128)(2,1)}), bf16[32,24,128]{2,1,0:T(8,128)(2,1)S(1)}, u32[]{:S(2)}, u32[]{:S(2)}) async-start(bf16[32,24,128]{2,1,0:T(8,128)(2,1)} %get-tuple-element.50), calls=%async_computation.4 | async-start | bytes 393216 | tf_op jit(solution)/shard_map/all_to_all | solution.py:504
  87.4 14.0 %collective-permute-start.2 = (bf16[2,12,64,96]{3,2,1,0:T(8,128)(2,1)S(1)}, bf16[2,12,64,96]{3,2,1,0:T(8,128)(2,1)S(1)}, u32[]{:S(2)}, u32[]{:S(2)}) collective-permute-start(bf16[2,12,64,96]{3,2,1,0:T(8,128)(2,1)S(1)} %get-tuple-element.53), channel_id=1, source_target_pairs={{0,1},{1,0},{2,3},{3,2},{4,5},{5,4},{6,7},{7,6},{8,9},{9,8},{10,11... | collective-permute-start | bytes 884744 | tf_op jit(solution)/shard_map/ppermute | solution.py:511
  97.9 11.1 %all-to-all-start.5 = ((bf16[16,24,128]{2,1,0:T(8,128)(2,1)}), bf16[16,24,128]{2,1,0:T(8,128)(2,1)S(1)}, u32[]{:S(2)}, u32[]{:S(2)}) async-start(bf16[16,24,128]{2,1,0:T(8,128)(2,1)} %shard_map.149), calls=%async_computation.5 | async-start | bytes 196608 | tf_op jit(solution)/shard_map/all_to_all | solution.py:507

commit v7 on v6

--- a/solution.py
+++ b/solution.py
@@ -198,10 +198,7 @@
     return centred * rstd, rstd
 
 
-def edges(width, normed, own, other, send, weights):
-    core = lax.axis_index("ch")
-    weights[core] = own[...]
-    weights[1 - core] = other[...]
+def edges(width, normed, weights, send):
     gate = jax.nn.sigmoid(dot(rows_of(weights, 0, width), normed[...], (1, 0)))
     value = dot(rows_of(weights, width, width), normed[...], (1, 0))
     send[...] = (gate * value).reshape(send.shape).astype(bf16)
@@ -442,10 +439,9 @@
         far=range(8),
         room=60,
     )
-    send, weights = call(
-        functools.partial(edges, width),
-        [((devices, 2 * share, flat), bf16), ((parts, *weight[0]), bf16)],
-        (normed, weights, lax.ppermute(weights, "ch", swap)),
+    weights = lax.all_gather(weights, "ch")
+    (send,) = call(
+        functools.partial(edges, width), [((devices, 2 * share, flat), bf16)], (normed, weights)
     )
     arrived = lax.all_to_all(send, everyone, 0, 0)
     arrived, other = lax.optimization_barrier((arrived, other))
@@ -503,6 +499,7 @@
     )
     arrived = lax.all_to_all(send, ("ch", "row", "col"), 0, 0)
     rest = devices // parts
+    arrived, others = lax.optimization_barrier((arrived, others))
     (sums,) = call(add_up, [((rest, per, channels), bf16)], (arrived,))
     sums = lax.all_to_all(sums, ("row", "col"), 0, 0)
     updated, grad_pair, *grads = call(

time: 110 us -> 107 us (0.973)
  blocking collectives: 70.5 us -> 95.3 us
  waiting for transfers between devices: 18.4 us -> 0.01 us
  starting transfers between devices: 6.8 us -> 0.01 us
  local copies, waits for them, and re-layouts: 1.88 us -> 0.03 us
  Pallas kernels: 11.8 us -> 10.5 us
    all_to_all x0 -> x2, blocking collectives: none -> 22.4 us  [the longest x1 11.9 us: by_channels(): arrived = lax.all_to_all(send, ('ch', 'row', 'col'), 0, 0)]
    all_to_all x2 -> x0, waiting for transfers between devices: 17.3 us -> none  [the longest x1 9.63 us: by_channels(): arrived = lax.all_to_all(send, ('ch', 'row', 'col'), 0, 0)]
    all_to_all x2 -> x0, starting transfers between devices: 6.11 us -> none  [the longest x1 3.51 us: by_channels(): sums = lax.all_to_all(sums, ('row', 'col'), 0, 0)]
    all_gather x0 -> x1, blocking collectives: none -> 2.39 us  [by_channels(): weights = lax.all_gather(weights, 'ch')]
    unnamed x12 -> x8, local copies, waits for them, and re-layouts: 1.88 us -> 0.03 us
    pallas_call x8, Pallas kernels: 11.8 us -> 10.5 us  [call(): pl.pallas_call(kernel, out_shape=tuple((jax.ShapeDtypeStruct(*out) for ou...]
    ppermute x1 -> x0, waiting for transfers between devices: 1.15 us -> none  [by_channels(): lax.ppermute(weights, 'ch', swap)]
  transfers between devices with their start and end apart: 5 -> 2, of which waited for: 3 -> 0; matrix products, arithmetic and copies ran while one was open for 0% -> 0% of each run, Pallas kernels for 2% -> 1%
where the time goes in v7:
time: 107 us
  blocking collectives  95.3 us (89%)
  Pallas kernels  10.5 us (10%)
    all_to_all x4, blocking collectives, by_channels(): arrived = lax.all_to_all(send, everyone, 0, 0)  70.5 us
    all_to_all x1, blocking collectives, by_channels(): arrived = lax.all_to_all(send, ('ch', 'row', 'col'), 0, 0)  11.9 us
    all_to_all x1, blocking collectives, by_channels(): sums = lax.all_to_all(sums, ('row', 'col'), 0, 0)  10.6 us
    pallas_call x8, Pallas kernels, call(): pl.pallas_call(kernel, out_shape=tuple((jax.ShapeDtypeStruct(*out) for ou...  10.5 us
    all_gather x1, blocking collectives, by_channels(): weights = lax.all_gather(weights, 'ch')  2.39 us
  transfers between devices with their start and end apart: 2, of which 0 were waited for; matrix products, arithmetic and copies ran while one was open for 0% of the time, Pallas kernels for 1%

profile of v7, /device:TPU:0, one launch (start us, length us, event | category | flops | bytes accessed | tf_op | source)
XLA Modules:
  0.0 106.6 jit_solution(494100933313250374)
XLA Ops:
  0.6 2.2 %shard_map.143 = (bf16[384,128]{1,0:T(8,128)(2,1)}, bf16[128,1152]{1,0:T(8,128)(2,1)}, bf16[12,64,96]{2,1,0:T(8,128)(2,1)}) custom-call(bf16[64,128]{1,0:T(8,128)(2,1)} %bitcast.21, bf16[64,128]{1,0:T(8,128)(2,1)} %bitcast.22, bf16[64,128]{1,0:T(8,128)(2,1)} %bitcast.23, bf16[64,128]{1,0:T(8,128)(2,1)} %bitcast.24, bf16[64,128]{1,0:T(8,128)(2,1)} %bitcast.25, ...), custom_call_target="tpu_custom_call" | custom-call | tf_op jit(solution)/shard_map/pallas_call | solution.py:132
  2.9 0.0 copy-start.2
  2.9 2.4 %all-gather = bf16[768,128]{1,0:T(8,128)(2,1)S(1)} all-gather(bf16[384,128]{1,0:T(8,128)(2,1)} %get-tuple-element.36), channel_id=2, replica_groups=mesh['row'=8,'col'=2,'ch'=2] {'ch'}, dimensions={0}, use_global_device_ids=true | all-gather | bytes 294912 | tf_op jit(solution)/shard_map/all_gather | solution.py:442
  5.3 0.0 copy-done.2
  5.3 0.5 shard_map.144
  5.7 0.0 copy-start.3
  5.7 24.3 %all_to_all.30.arrived = bf16[32,8,1152]{2,1,0:T(8,128)(2,1)S(1)} all-to-all(bf16[32,8,1152]{2,1,0:T(8,128)(2,1)S(1)} %shard_map.144), channel_id=1, replica_groups=mesh['row'=8,'col'=2,'ch'=2] {'col','row','ch'}, dimensions={0} | all-to-all | bytes 1179648 | tf_op jit(solution)/shard_map/all_to_all | solution.py:446
  30.1 0.0 copy-done.3
  30.1 0.0 collective-permute-start
  30.1 1.6 %shard_map.145 = (bf16[32,4,1152]{2,1,0:T(4,128)(2,1)S(1)}, bf16[8,192,192]{2,1,0:T(8,128)(2,1)S(1)}) custom-call(bf16[32,8,1152]{2,1,0:T(8,128)(2,1)S(1)} %all_to_all.30.arrived), custom_call_target="tpu_custom_call" | custom-call | tf_op jit(solution)/shard_map/pallas_call | solution.py:132
  31.6 0.0 copy-start.1
  31.7 0.0 collective-permute-done.other_far
  31.7 13.2 %all_to_all.31.arrived = bf16[32,4,1152]{2,1,0:T(4,128)(2,1)S(1)} all-to-all(bf16[32,4,1152]{2,1,0:T(4,128)(2,1)S(1)} %get-tuple-element.41), channel_id=1, replica_groups=mesh['row'=8,'col'=2,'ch'=2] {'col','row','ch'}, dimensions={0} | all-to-all | bytes 589824 | tf_op jit(solution)/shard_map/all_to_all | solution.py:457
  44.8 0.0 copy-done.1
  44.9 1.9 %shard_map.146 = (bf16[32,4,1152]{2,1,0:T(4,128)(2,1)S(1)}, bf16[128,1152]{1,0:T(8,128)(2,1)S(1)}, f32[2,128,128]{2,1,0:T(8,128)S(1)}, bf16[12,64,96]{2,1,0:T(8,128)(2,1)S(1)}, bf16[12,64,96]{2,1,0:T(8,128)(2,1)S(1)}) custom-call(bf16[32,4,1152]{2,1,0:T(4,128)(2,1)S(1)} %all_to_all.31.arrived, bf16[2,384,128]{2,1,0:T(8,128)(2,1)S(1)} %bitcast.17, ...), custom_call_target="tpu_custom_call" | custom-call | tf_op jit(solution)/shard_map/pallas_call | solution.py:132
  46.7 13.3 %all_to_all.32.arrived = bf16[32,4,1152]{2,1,0:T(4,128)(2,1)S(1)} all-to-all(bf16[32,4,1152]{2,1,0:T(4,128)(2,1)S(1)} %get-tuple-element.43), channel_id=1, replica_groups=mesh['row'=8,'col'=2,'ch'=2] {'col','row','ch'}, dimensions={0} | all-to-all | bytes 589824 | tf_op jit(solution)/shard_map/all_to_all | solution.py:477
  60.0 1.6 %shard_map.147 = bf16[32,8,1152]{2,1,0:T(8,128)(2,1)S(1)} custom-call(bf16[32,4,1152]{2,1,0:T(4,128)(2,1)S(1)} %all_to_all.32.arrived, bf16[8,192,192]{2,1,0:T(8,128)(2,1)S(1)} %get-tuple-element.44.kept_far), custom_call_target="tpu_custom_call" | custom-call | tf_op jit(solution)/shard_map/pallas_call | solution.py:132
  61.6 0.0 copy-start
  61.7 19.6 %all_to_all.33.arrived = bf16[32,8,1152]{2,1,0:T(8,128)(2,1)S(1)} all-to-all(bf16[32,8,1152]{2,1,0:T(8,128)(2,1)S(1)} %shard_map.147), channel_id=1, replica_groups=mesh['row'=8,'col'=2,'ch'=2] {'col','row','ch'}, dimensions={0} | all-to-all | bytes 1179648 | tf_op jit(solution)/shard_map/all_to_all | solution.py:485
  81.3 0.0 copy-done
  81.3 1.8 %shard_map.148 = (bf16[32,24,128]{2,1,0:T(8,128)(2,1)S(1)}, bf16[12,64,96]{2,1,0:T(8,128)(2,1)S(1)}, bf16[2,12,64,96]{3,2,1,0:T(8,128)(2,1)S(1)}) custom-call(bf16[32,8,1152]{2,1,0:T(8,128)(2,1)S(1)} %all_to_all.33.arrived, bf16[2,384,128]{2,1,0:T(8,128)(2,1)S(1)} %bitcast.18, bf16[24,96,128]{2,1,0:T(8,128)(2,1)S(1)} %copy-done, ...), custom_call_target="tpu_custom_call" | custom-call | tf_op jit(solution)/shard_map/pallas_call | solution.py:132
  83.1 11.9 %all_to_all.34.arrived = bf16[32,24,128]{2,1,0:T(8,128)(2,1)S(1)} all-to-all(bf16[32,24,128]{2,1,0:T(8,128)(2,1)S(1)} %get-tuple-element.48), channel_id=1, replica_groups=mesh['row'=8,'col'=2,'ch'=2] {'ch','row','col'}, dimensions={0} | all-to-all | bytes 393216 | tf_op jit(solution)/shard_map/all_to_all | solution.py:500
  94.9 0.0 collective-permute-start.1
  95.0 10.6 %all_to_all.35.sums = bf16[16,24,128]{2,1,0:T(8,128)(2,1)S(1)} all-to-all(bf16[16,24,128]{2,1,0:T(8,128)(2,1)S(1)} %shard_map.149), channel_id=1, replica_groups=mesh['row'=8,'col'=2,'ch'=2] {'row','col'}, dimensions={0} | all-to-all | bytes 196608 | tf_op jit(solution)/shard_map/all_to_all | solution.py:504
  105.6 0.0 collective-permute-done.1.others
  105.6 1.0 shard_map.150
  (1 shorter events, 0.0 us)
Async XLA Ops:
  2.9 2.4 %copy-start.2 = (bf16[128,1152]{1,0:T(8,128)(2,1)S(1)}, bf16[128,1152]{1,0:T(8,128)(2,1)}, u32[]{:S(2)}) copy-start(bf16[128,1152]{1,0:T(8,128)(2,1)} %get-tuple-element.35.normed.normed_far) | copy-start | bytes 884740
  5.7 24.3 %copy-start.3 = (bf16[12,64,96]{2,1,0:T(8,128)(2,1)S(1)}, bf16[12,64,96]{2,1,0:T(8,128)(2,1)}, u32[]{:S(2)}) copy-start(bf16[12,64,96]{2,1,0:T(8,128)(2,1)} %get-tuple-element.40) | copy-start | bytes 442372
  30.1 1.6 %collective-permute-start = (bf16[12,64,96]{2,1,0:T(8,128)(2,1)S(1)}, bf16[12,64,96]{2,1,0:T(8,128)(2,1)S(1)}, u32[]{:S(2)}, u32[]{:S(2)}) collective-permute-start(bf16[12,64,96]{2,1,0:T(8,128)(2,1)S(1)} %copy-done.3), channel_id=1, source_target_pairs={{0,1},{1,0},{2,3},{3,2},{4,5},{5,4},{6,7},{7,6},{8,9},{9,8},{10,11... | collective-permute-start | bytes 442376 | tf_op jit(solution)/shard_map/ppermute | solution.py:448
  31.6 13.2 %copy-start.1 = (bf16[24,96,64]{1,2,0:T(8,128)(2,1)S(1)}, bf16[24,96,64]{1,2,0:T(8,128)(2,1)}, u32[]{:S(2)}) copy-start(bf16[24,96,64]{1,2,0:T(8,128)(2,1)} %param.9) | copy-start | bytes 884740
  61.6 19.6 %copy-start = (bf16[24,96,128]{2,1,0:T(8,128)(2,1)S(1)}, bf16[24,96,128]{2,1,0:T(8,128)(2,1)}, u32[]{:S(2)}) copy-start(bf16[24,96,128]{2,1,0:T(8,128)(2,1)} %pair_far.3) | copy-start | bytes 1769476
  94.9 10.6 %collective-permute-start.1 = (bf16[2,12,64,96]{3,2,1,0:T(8,128)(2,1)S(1)}, bf16[2,12,64,96]{3,2,1,0:T(8,128)(2,1)S(1)}, u32[]{:S(2)}, u32[]{:S(2)}) collective-permute-start(bf16[2,12,64,96]{3,2,1,0:T(8,128)(2,1)S(1)} %get-tuple-element.53), channel_id=1, source_target_pairs={{0,1},{1,0},{2,3},{3,2},{4,5},{5,4},{6,7},{7,6},{8,9},{9,8},{10,11... | collective-permute-start | bytes 884744 | tf_op jit(solution)/shard_map/ppermute | solution.py:508

commit v8 on v7

--- a/solution.py
+++ b/solution.py
@@ -160,7 +160,7 @@
 
 
 def prepare(
-    share, ga, pa, gb, pb, go, wo, pair_far, cotangent_far, out, normed, other,
+    share, ga, pa, gb, pb, go, wo, pair_far, cotangent_far, out, normed, inverse, other,
     gates, values, last, pair, arrivals,
 ):
     hidden = go.shape[0]
@@ -182,7 +182,9 @@
     out[width : 2 * width] = dot(order, values[...], (1, 0)).astype(bf16)
     out[2 * width :] = last[...]
     fetch.wait()
-    normed[...] = normalized(pair[...])[0].astype(bf16)
+    hat, rstd = normalized(pair[...])
+    normed[...] = hat.astype(bf16)
+    inverse[...] = rstd
     cut.wait()
 
 
@@ -255,13 +257,10 @@
     pack_rows(block, cols, result, send)
 
 
-def unmix(parts, cols, arrived, kept_far, send, held, result, kept, arrival):
+def unmix(parts, cols, arrived, kept, send, held, result):
     block = 8
     q = arrived.shape[1]
-    copy = pltpu.make_async_copy(kept_far, kept, arrival)
-    copy.start()
     spread_rows(block, cols, arrived, held)
-    copy.wait()
     for e in range(q):
         d_mixed = square(block, parts, cols, held, e)
         put_square(block, parts, cols, result, e, dot(d_mixed, kept[q + e], (1, 0)))
@@ -281,21 +280,15 @@
 
 
 def head(
-    width, scale, arrived, weights, normed_far, own_far, other_far,
+    width, scale, arrived, weights, normed, cotangent, other,
     send, d_gate, terms, updated_own, updated_other,
-    normed, own, other, upstream, arrivals,
+    upstream,
 ):
     parts, total, _ = weights.shape
     hidden = (total - 2 * width) // 2
     devices, q, flat = arrived.shape
     count, _, cols = other.shape
     core = lax.axis_index("ch")
-    copies = [
-        pltpu.make_async_copy(normed_far, normed, arrivals.at[0]),
-        pltpu.make_async_copy(own_far.at[pl.ds(core * count, count)], own, arrivals.at[1]),
-        pltpu.make_async_copy(other_far, other, arrivals.at[2]),
-    ]
-    start_all(copies)
     mixed = jnp.concatenate([arrived[s].astype(f32) for s in range(devices)], 0)
     average = jnp.mean(mixed, 0, keepdims=True)
     spread = jnp.mean(mixed * mixed, 0, keepdims=True) - average * average
@@ -304,8 +297,8 @@
     hat_rounded = hat.astype(bf16)
     w_out = rows_of(weights, 2 * width + hidden, hidden)
     proj = dot(w_out, hat_rounded, (1, 0))
-    wait_all(copies)
-    for part, side in ((own, core), (other, 1 - core)):
+    own = cotangent[pl.ds(core * count, count)]
+    for part, side in ((own, core), (other[...], 1 - core)):
         upstream[pl.ds(pl.multiple_of(side * hidden, hidden), hidden)] = jnp.concatenate(
             [part[i].astype(f32) for i in range(count)], axis=1
         )
@@ -330,24 +323,15 @@
 
 
 def tail(
-    width, scale, arrived, weights, pair_far, d_gate_far, head_terms, updated_other,
-    send, grad_own, others,
-    pair, d_gate, whole, arrivals,
+    width, scale, cols, arrived, weights, pair_hat, inverse, d_gate, head_terms, updated_other,
+    send, grad_own, others, whole,
 ):
     parts, total, channels = weights.shape
     hidden = (total - 2 * width) // 2
     devices, q, flat = arrived.shape
-    count, cols, _ = pair.shape
-    core = lax.axis_index("ch")
-    copies = [
-        pltpu.make_async_copy(pair_far.at[pl.ds(core * count, count)], pair, arrivals.at[0]),
-        pltpu.make_async_copy(d_gate_far, d_gate, arrivals.at[1]),
-    ]
-    start_all(copies)
     others[0] = updated_other[...]
-    wait_all(copies)
-    hat, inverse = normalized(pair[...])
-    normed = hat.astype(bf16)
+    normed = pair_hat[...]
+    hat = normed.astype(f32)
     w_gate, w_value = rows_of(weights, 0, width), rows_of(weights, width, width)
     gate = jax.nn.sigmoid(dot(w_gate, normed, (1, 0)))
     value = dot(w_value, normed, (1, 0))
@@ -366,7 +350,7 @@
         send[s] = whole[s * per : (s + 1) * per].astype(bf16)
     d_input = dot(w_gate, by_gate, (0, 0)) + dot(w_value, by_value, (0, 0))
     d_input = d_input + dot(rows_of(weights, 2 * width, hidden), d_gate[...], (0, 0))
-    back = inverse * (
+    back = inverse[...] * (
         d_input
         - jnp.mean(d_input, 0, keepdims=True)
         - hat * jnp.mean(d_input * hat, 0, keepdims=True)
@@ -425,9 +409,9 @@
     part = ((count, hidden, cols), bf16)
     own = jnp.swapaxes(cotangent, 1, 2)
     whole_weight = pltpu.VMEM((2 * hidden, channels), bf16)
-    weights, normed, other = call(
+    weights, normed, inverse, other = call(
         functools.partial(prepare, share),
-        [weight, ((channels, flat), bf16), part],
+        [weight, ((channels, flat), bf16), ((1, flat), f32), part],
         (w_gate_a.T, w_proj_a.T, w_gate_b.T, w_proj_b.T, w_gate_out.T, w_out.T, pair, own),
         (
             whole_weight,
@@ -465,37 +449,23 @@
             part,
         ],
         (arrived, weights, normed, own, other),
-        (
-            pltpu.VMEM((channels, flat), bf16),
-            pltpu.VMEM(*part),
-            pltpu.VMEM(*part),
-            pltpu.VMEM((hidden * parts, flat), f32),
-            pltpu.SemaphoreType.DMA((3,)),
-        ),
-        far=(2, 3, 4),
+        (pltpu.VMEM((hidden * parts, flat), f32),),
     )
     arrived = lax.all_to_all(send, everyone, 0, 0)
     (send,) = call(
         functools.partial(unmix, col_parts, cols),
         [((devices, 2 * share, flat), bf16)],
         (arrived, kept),
-        (room, room, pltpu.VMEM(kept.shape, bf16), pltpu.SemaphoreType.DMA),
-        far=(1,),
+        (room, room),
     )
     arrived = lax.all_to_all(send, everyone, 0, 0)
     total = 2 * width + 2 * hidden
     per = total * parts // devices
     send, grad_own, others = call(
-        functools.partial(tail, width, scale),
+        functools.partial(tail, width, scale, cols),
         [((devices, per, channels), bf16), part, ((2, *part[0]), bf16)],
-        (arrived, weights, pair, d_gate, head_terms, updated_other),
-        (
-            pltpu.VMEM((count, cols, channels), bf16),
-            pltpu.VMEM((hidden * parts, flat), bf16),
-            pltpu.VMEM((total * parts, channels), f32),
-            pltpu.SemaphoreType.DMA((2,)),
-        ),
-        far=(2, 3),
+        (arrived, weights, normed, inverse, d_gate, head_terms, updated_other),
+        (pltpu.VMEM((total * parts, channels), f32),),
     )
     arrived = lax.all_to_all(send, ("ch", "row", "col"), 0, 0)
     rest = devices // parts

time: 107 us -> 107 us (level)
  no operation moved by 1% of the time
where the time goes in v8:
time: 107 us; the launch traced here: 106 us
  blocking collectives  95.3 us (89%)
  Pallas kernels  9.66 us (9%)
    all_to_all x4, blocking collectives, by_channels(): arrived = lax.all_to_all(send, everyone, 0, 0)  70.5 us
    all_to_all x1, blocking collectives, by_channels(): arrived = lax.all_to_all(send, ('ch', 'row', 'col'), 0, 0)  11.9 us
    all_to_all x1, blocking collectives, by_channels(): sums = lax.all_to_all(sums, ('row', 'col'), 0, 0)  10.6 us
    pallas_call x8, Pallas kernels, call(): pl.pallas_call(kernel, out_shape=tuple((jax.ShapeDtypeStruct(*out) for ou...  9.66 us
    all_gather x1, blocking collectives, by_channels(): weights = lax.all_gather(weights, 'ch')  2.39 us
  transfers between devices with their start and end apart: 2, of which 0 were waited for; matrix products, arithmetic and copies ran while one was open for 0% of the time, Pallas kernels for 1%

profile of v8, /device:TPU:0, one launch (start us, length us, event | category | flops | bytes accessed | tf_op | source)
XLA Modules:
  0.0 106.4 jit_solution(12312983406269929350)
XLA Ops:
  0.6 2.2 %shard_map.143 = (bf16[384,128]{1,0:T(8,128)(2,1)}, bf16[128,1152]{1,0:T(8,128)(2,1)}, f32[1,1152]{1,0:T(1,128)}, bf16[12,64,96]{2,1,0:T(8,128)(2,1)}) custom-call(bf16[64,128]{1,0:T(8,128)(2,1)} %bitcast.21, bf16[64,128]{1,0:T(8,128)(2,1)} %bitcast.22, bf16[64,128]{1,0:T(8,128)(2,1)} %bitcast.23, bf16[64,128]{1,0:T(8,128)(2,1)} %bitcast.24, ...), custom_call_target="tpu_custom_call" | custom-call | tf_op jit(solution)/shard_map/pallas_call | solution.py:132
  2.9 0.0 copy-start
  2.9 2.4 %all-gather = bf16[768,128]{1,0:T(8,128)(2,1)S(1)} all-gather(bf16[384,128]{1,0:T(8,128)(2,1)} %get-tuple-element.37), channel_id=2, replica_groups=mesh['row'=8,'col'=2,'ch'=2] {'ch'}, dimensions={0}, use_global_device_ids=true | all-gather | bytes 294912 | tf_op jit(solution)/shard_map/all_gather | solution.py:426
  5.3 0.0 copy-done
  5.3 0.5 shard_map.144
  5.7 0.0 copy-start.3
  5.8 24.3 %all_to_all.30.arrived = bf16[32,8,1152]{2,1,0:T(8,128)(2,1)S(1)} all-to-all(bf16[32,8,1152]{2,1,0:T(8,128)(2,1)S(1)} %shard_map.144), channel_id=1, replica_groups=mesh['row'=8,'col'=2,'ch'=2] {'col','row','ch'}, dimensions={0} | all-to-all | bytes 1179648 | tf_op jit(solution)/shard_map/all_to_all | solution.py:430
  30.1 0.0 copy-done.3
  30.1 0.0 collective-permute-start
  30.1 1.6 %shard_map.145 = (bf16[32,4,1152]{2,1,0:T(4,128)(2,1)S(1)}, bf16[8,192,192]{2,1,0:T(8,128)(2,1)S(1)}) custom-call(bf16[32,8,1152]{2,1,0:T(8,128)(2,1)S(1)} %all_to_all.30.arrived), custom_call_target="tpu_custom_call" | custom-call | tf_op jit(solution)/shard_map/pallas_call | solution.py:132
  31.6 0.0 copy-start.1
  31.7 0.0 collective-permute-done.other
  31.7 13.2 %all_to_all.31.arrived = bf16[32,4,1152]{2,1,0:T(4,128)(2,1)S(1)} all-to-all(bf16[32,4,1152]{2,1,0:T(4,128)(2,1)S(1)} %get-tuple-element.42), channel_id=1, replica_groups=mesh['row'=8,'col'=2,'ch'=2] {'col','row','ch'}, dimensions={0} | all-to-all | bytes 589824 | tf_op jit(solution)/shard_map/all_to_all | solution.py:441
  44.9 0.0 copy-done.1
  44.9 1.1 %shard_map.146 = (bf16[32,4,1152]{2,1,0:T(4,128)(2,1)S(1)}, bf16[128,1152]{1,0:T(8,128)(2,1)S(1)}, f32[2,128,128]{2,1,0:T(8,128)S(1)}, bf16[12,64,96]{2,1,0:T(8,128)(2,1)S(1)}, bf16[12,64,96]{2,1,0:T(8,128)(2,1)S(1)}) custom-call(bf16[32,4,1152]{2,1,0:T(4,128)(2,1)S(1)} %all_to_all.31.arrived, bf16[2,384,128]{2,1,0:T(8,128)(2,1)S(1)} %bitcast.17, ...), custom_call_target="tpu_custom_call" | custom-call | tf_op jit(solution)/shard_map/pallas_call | solution.py:132
  46.0 13.3 %all_to_all.32.arrived = bf16[32,4,1152]{2,1,0:T(4,128)(2,1)S(1)} all-to-all(bf16[32,4,1152]{2,1,0:T(4,128)(2,1)S(1)} %get-tuple-element.44), channel_id=1, replica_groups=mesh['row'=8,'col'=2,'ch'=2] {'col','row','ch'}, dimensions={0} | all-to-all | bytes 589824 | tf_op jit(solution)/shard_map/all_to_all | solution.py:454
  59.3 1.8 %shard_map.147 = bf16[32,8,1152]{2,1,0:T(8,128)(2,1)S(1)} custom-call(bf16[32,4,1152]{2,1,0:T(4,128)(2,1)S(1)} %all_to_all.32.arrived, bf16[8,192,192]{2,1,0:T(8,128)(2,1)S(1)} %get-tuple-element.45.kept), custom_call_target="tpu_custom_call" | custom-call | tf_op jit(solution)/shard_map/pallas_call | solution.py:132
  61.1 19.6 %all_to_all.33.arrived = bf16[32,8,1152]{2,1,0:T(8,128)(2,1)S(1)} all-to-all(bf16[32,8,1152]{2,1,0:T(8,128)(2,1)S(1)} %shard_map.147), channel_id=1, replica_groups=mesh['row'=8,'col'=2,'ch'=2] {'col','row','ch'}, dimensions={0} | all-to-all | bytes 1179648 | tf_op jit(solution)/shard_map/all_to_all | solution.py:461
  80.7 0.0 copy-start.2
  80.7 0.7 copy-done.2
  81.4 1.5 %shard_map.148 = (bf16[32,24,128]{2,1,0:T(8,128)(2,1)S(1)}, bf16[12,64,96]{2,1,0:T(8,128)(2,1)S(1)}, bf16[2,12,64,96]{3,2,1,0:T(8,128)(2,1)S(1)}) custom-call(bf16[32,8,1152]{2,1,0:T(8,128)(2,1)S(1)} %all_to_all.33.arrived, bf16[2,384,128]{2,1,0:T(8,128)(2,1)S(1)} %bitcast.18, bf16[128,1152]{1,0:T(8,128)(2,1)S(1)} %copy-done, f32[1,1152]{1,0:T(1,128)S(1)} %copy-done.2, ...), custom_call_target="tpu_custom_call" | custom-call | tf_op jit(solution)/shard_map/pallas_call | solution.py:132
  82.9 11.9 %all_to_all.34.arrived = bf16[32,24,128]{2,1,0:T(8,128)(2,1)S(1)} all-to-all(bf16[32,24,128]{2,1,0:T(8,128)(2,1)S(1)} %get-tuple-element.50), channel_id=1, replica_groups=mesh['row'=8,'col'=2,'ch'=2] {'ch','row','col'}, dimensions={0} | all-to-all | bytes 393216 | tf_op jit(solution)/shard_map/all_to_all | solution.py:470
  94.7 0.0 collective-permute-start.1
  94.8 10.6 %all_to_all.35.sums = bf16[16,24,128]{2,1,0:T(8,128)(2,1)S(1)} all-to-all(bf16[16,24,128]{2,1,0:T(8,128)(2,1)S(1)} %shard_map.149), channel_id=1, replica_groups=mesh['row'=8,'col'=2,'ch'=2] {'row','col'}, dimensions={0} | all-to-all | bytes 196608 | tf_op jit(solution)/shard_map/all_to_all | solution.py:474
  105.4 0.0 collective-permute-done.1.others
  105.4 1.0 shard_map.150
  (1 shorter events, 0.0 us)
Async XLA Ops:
  2.9 2.4 %copy-start = (bf16[128,1152]{1,0:T(8,128)(2,1)S(1)}, bf16[128,1152]{1,0:T(8,128)(2,1)}, u32[]{:S(2)}) copy-start(bf16[128,1152]{1,0:T(8,128)(2,1)} %get-tuple-element.36.normed.pair_hat) | copy-start | bytes 884740
  5.7 24.3 %copy-start.3 = (bf16[12,64,96]{2,1,0:T(8,128)(2,1)S(1)}, bf16[12,64,96]{2,1,0:T(8,128)(2,1)}, u32[]{:S(2)}) copy-start(bf16[12,64,96]{2,1,0:T(8,128)(2,1)} %get-tuple-element.41) | copy-start | bytes 442372
  30.1 1.6 %collective-permute-start = (bf16[12,64,96]{2,1,0:T(8,128)(2,1)S(1)}, bf16[12,64,96]{2,1,0:T(8,128)(2,1)S(1)}, u32[]{:S(2)}, u32[]{:S(2)}) collective-permute-start(bf16[12,64,96]{2,1,0:T(8,128)(2,1)S(1)} %copy-done.3), channel_id=1, source_target_pairs={{0,1},{1,0},{2,3},{3,2},{4,5},{5,4},{6,7},{7,6},{8,9},{9,8},{10,11... | collective-permute-start | bytes 442376 | tf_op jit(solution)/shard_map/ppermute | solution.py:432
  31.6 13.2 %copy-start.1 = (bf16[24,96,64]{1,2,0:T(8,128)(2,1)S(1)}, bf16[24,96,64]{1,2,0:T(8,128)(2,1)}, u32[]{:S(2)}) copy-start(bf16[24,96,64]{1,2,0:T(8,128)(2,1)} %param.9) | copy-start | bytes 884740
  80.7 0.7 copy-start.2
  94.7 10.6 %collective-permute-start.1 = (bf16[2,12,64,96]{3,2,1,0:T(8,128)(2,1)S(1)}, bf16[2,12,64,96]{3,2,1,0:T(8,128)(2,1)S(1)}, u32[]{:S(2)}, u32[]{:S(2)}) collective-permute-start(bf16[2,12,64,96]{3,2,1,0:T(8,128)(2,1)S(1)} %get-tuple-element.55), channel_id=1, source_target_pairs={{0,1},{1,0},{2,3},{3,2},{4,5},{5,4},{6,7},{7,6},{8,9},{9,8},{10,11... | collective-permute-start | bytes 884744 | tf_op jit(solution)/shard_map/ppermute | solution.py:478

commit v9 on v8

--- a/solution.py
+++ b/solution.py
@@ -200,7 +200,8 @@
     return centred * rstd, rstd
 
 
-def edges(width, normed, weights, send):
+def edges(width, normed, weights, inverse, send, inverse_on):
+    inverse_on[...] = inverse[...]
     gate = jax.nn.sigmoid(dot(rows_of(weights, 0, width), normed[...], (1, 0)))
     value = dot(rows_of(weights, width, width), normed[...], (1, 0))
     send[...] = (gate * value).reshape(send.shape).astype(bf16)
@@ -257,10 +258,13 @@
     pack_rows(block, cols, result, send)
 
 
-def unmix(parts, cols, arrived, kept, send, held, result):
+def unmix(parts, cols, arrived, kept_far, send, held, result, kept, arrival):
     block = 8
     q = arrived.shape[1]
+    copy = pltpu.make_async_copy(kept_far, kept, arrival)
+    copy.start()
     spread_rows(block, cols, arrived, held)
+    copy.wait()
     for e in range(q):
         d_mixed = square(block, parts, cols, held, e)
         put_square(block, parts, cols, result, e, dot(d_mixed, kept[q + e], (1, 0)))
@@ -424,8 +428,10 @@
         room=60,
     )
     weights = lax.all_gather(weights, "ch")
-    (send,) = call(
-        functools.partial(edges, width), [((devices, 2 * share, flat), bf16)], (normed, weights)
+    send, inverse = call(
+        functools.partial(edges, width),
+        [((devices, 2 * share, flat), bf16), ((1, flat), f32)],
+        (normed, weights, inverse),
     )
     arrived = lax.all_to_all(send, everyone, 0, 0)
     arrived, other = lax.optimization_barrier((arrived, other))
@@ -456,7 +462,8 @@
         functools.partial(unmix, col_parts, cols),
         [((devices, 2 * share, flat), bf16)],
         (arrived, kept),
-        (room, room),
+        (room, room, pltpu.VMEM(kept.shape, bf16), pltpu.SemaphoreType.DMA),
+        far=(1,),
     )
     arrived = lax.all_to_all(send, everyone, 0, 0)
     total = 2 * width + 2 * hidden

time: 107 us -> 107 us (level)
  no operation moved by 1% of the time
where the time goes in v9:
time: 107 us; the launch traced here: 106 us
  blocking collectives  95.3 us (89%)
  Pallas kernels  9.45 us (9%)
    all_to_all x4, blocking collectives, by_channels(): arrived = lax.all_to_all(send, everyone, 0, 0)  70.4 us
    all_to_all x1, blocking collectives, by_channels(): arrived = lax.all_to_all(send, ('ch', 'row', 'col'), 0, 0)  11.9 us
    all_to_all x1, blocking collectives, by_channels(): sums = lax.all_to_all(sums, ('row', 'col'), 0, 0)  10.6 us
    pallas_call x8, Pallas kernels, call(): pl.pallas_call(kernel, out_shape=tuple((jax.ShapeDtypeStruct(*out) for ou...  9.45 us
    all_gather x1, blocking collectives, by_channels(): weights = lax.all_gather(weights, 'ch')  2.39 us
  transfers between devices with their start and end apart: 2, of which 0 were waited for; matrix products, arithmetic and copies ran while one was open for 0% of the time, Pallas kernels for 1%

profile of v9, /device:TPU:0, one launch (start us, length us, event | category | flops | bytes accessed | tf_op | source)
XLA Modules:
  0.0 106.2 jit_solution(1647964795491823848)
XLA Ops:
  0.6 2.2 %shard_map.143 = (bf16[384,128]{1,0:T(8,128)(2,1)}, bf16[128,1152]{1,0:T(8,128)(2,1)}, f32[1,1152]{1,0:T(1,128)}, bf16[12,64,96]{2,1,0:T(8,128)(2,1)}) custom-call(bf16[64,128]{1,0:T(8,128)(2,1)} %bitcast.21, bf16[64,128]{1,0:T(8,128)(2,1)} %bitcast.22, bf16[64,128]{1,0:T(8,128)(2,1)} %bitcast.23, bf16[64,128]{1,0:T(8,128)(2,1)} %bitcast.24, ...), custom_call_target="tpu_custom_call" | custom-call | tf_op jit(solution)/shard_map/pallas_call | solution.py:132
  2.9 0.0 copy-start
  2.9 2.4 %all-gather = bf16[768,128]{1,0:T(8,128)(2,1)S(1)} all-gather(bf16[384,128]{1,0:T(8,128)(2,1)} %get-tuple-element.39), channel_id=2, replica_groups=mesh['row'=8,'col'=2,'ch'=2] {'ch'}, dimensions={0}, use_global_device_ids=true | all-gather | bytes 294912 | tf_op jit(solution)/shard_map/all_gather | solution.py:430
  5.3 0.0 copy-start.2
  5.3 0.0 copy-done
  5.3 0.7 copy-done.2
  6.0 0.5 shard_map.144
  6.4 0.0 copy-start.3
  6.4 24.3 %all_to_all.30.arrived = bf16[32,8,1152]{2,1,0:T(8,128)(2,1)S(1)} all-to-all(bf16[32,8,1152]{2,1,0:T(8,128)(2,1)S(1)} %get-tuple-element.41), channel_id=1, replica_groups=mesh['row'=8,'col'=2,'ch'=2] {'col','row','ch'}, dimensions={0} | all-to-all | bytes 1179648 | tf_op jit(solution)/shard_map/all_to_all | solution.py:436
  30.8 0.0 copy-done.3
  30.8 0.0 collective-permute-start
  30.8 1.5 %shard_map.145 = (bf16[32,4,1152]{2,1,0:T(4,128)(2,1)S(1)}, bf16[8,192,192]{2,1,0:T(8,128)(2,1)S(1)}) custom-call(bf16[32,8,1152]{2,1,0:T(8,128)(2,1)S(1)} %all_to_all.30.arrived), custom_call_target="tpu_custom_call" | custom-call | tf_op jit(solution)/shard_map/pallas_call | solution.py:132
  32.3 0.0 copy-start.1
  32.3 0.0 collective-permute-done.other
  32.4 13.2 %all_to_all.31.arrived = bf16[32,4,1152]{2,1,0:T(4,128)(2,1)S(1)} all-to-all(bf16[32,4,1152]{2,1,0:T(4,128)(2,1)S(1)} %get-tuple-element.46), channel_id=1, replica_groups=mesh['row'=8,'col'=2,'ch'=2] {'col','row','ch'}, dimensions={0} | all-to-all | bytes 589824 | tf_op jit(solution)/shard_map/all_to_all | solution.py:447
  45.5 0.0 copy-done.1
  45.5 1.1 %shard_map.146 = (bf16[32,4,1152]{2,1,0:T(4,128)(2,1)S(1)}, bf16[128,1152]{1,0:T(8,128)(2,1)S(1)}, f32[2,128,128]{2,1,0:T(8,128)S(1)}, bf16[12,64,96]{2,1,0:T(8,128)(2,1)S(1)}, bf16[12,64,96]{2,1,0:T(8,128)(2,1)S(1)}) custom-call(bf16[32,4,1152]{2,1,0:T(4,128)(2,1)S(1)} %all_to_all.31.arrived, bf16[2,384,128]{2,1,0:T(8,128)(2,1)S(1)} %bitcast.17, ...), custom_call_target="tpu_custom_call" | custom-call | tf_op jit(solution)/shard_map/pallas_call | solution.py:132
  46.6 13.3 %all_to_all.32.arrived = bf16[32,4,1152]{2,1,0:T(4,128)(2,1)S(1)} all-to-all(bf16[32,4,1152]{2,1,0:T(4,128)(2,1)S(1)} %get-tuple-element.48), channel_id=1, replica_groups=mesh['row'=8,'col'=2,'ch'=2] {'col','row','ch'}, dimensions={0} | all-to-all | bytes 589824 | tf_op jit(solution)/shard_map/all_to_all | solution.py:460
  59.9 1.6 %shard_map.147 = bf16[32,8,1152]{2,1,0:T(8,128)(2,1)S(1)} custom-call(bf16[32,4,1152]{2,1,0:T(4,128)(2,1)S(1)} %all_to_all.32.arrived, bf16[8,192,192]{2,1,0:T(8,128)(2,1)S(1)} %get-tuple-element.49.kept_far), custom_call_target="tpu_custom_call" | custom-call | tf_op jit(solution)/shard_map/pallas_call | solution.py:132
  61.6 19.6 %all_to_all.33.arrived = bf16[32,8,1152]{2,1,0:T(8,128)(2,1)S(1)} all-to-all(bf16[32,8,1152]{2,1,0:T(8,128)(2,1)S(1)} %shard_map.147), channel_id=1, replica_groups=mesh['row'=8,'col'=2,'ch'=2] {'col','row','ch'}, dimensions={0} | all-to-all | bytes 1179648 | tf_op jit(solution)/shard_map/all_to_all | solution.py:468
  81.2 1.5 %shard_map.148 = (bf16[32,24,128]{2,1,0:T(8,128)(2,1)S(1)}, bf16[12,64,96]{2,1,0:T(8,128)(2,1)S(1)}, bf16[2,12,64,96]{3,2,1,0:T(8,128)(2,1)S(1)}) custom-call(bf16[32,8,1152]{2,1,0:T(8,128)(2,1)S(1)} %all_to_all.33.arrived, bf16[2,384,128]{2,1,0:T(8,128)(2,1)S(1)} %bitcast.18, bf16[128,1152]{1,0:T(8,128)(2,1)S(1)} %copy-done, ...), custom_call_target="tpu_custom_call" | custom-call | tf_op jit(solution)/shard_map/pallas_call | solution.py:132
  82.6 11.9 %all_to_all.34.arrived = bf16[32,24,128]{2,1,0:T(8,128)(2,1)S(1)} all-to-all(bf16[32,24,128]{2,1,0:T(8,128)(2,1)S(1)} %get-tuple-element.54), channel_id=1, replica_groups=mesh['row'=8,'col'=2,'ch'=2] {'ch','row','col'}, dimensions={0} | all-to-all | bytes 393216 | tf_op jit(solution)/shard_map/all_to_all | solution.py:477
  94.5 0.0 collective-permute-start.1
  94.6 10.6 %all_to_all.35.sums = bf16[16,24,128]{2,1,0:T(8,128)(2,1)S(1)} all-to-all(bf16[16,24,128]{2,1,0:T(8,128)(2,1)S(1)} %shard_map.149), channel_id=1, replica_groups=mesh['row'=8,'col'=2,'ch'=2] {'row','col'}, dimensions={0} | all-to-all | bytes 196608 | tf_op jit(solution)/shard_map/all_to_all | solution.py:481
  105.1 0.0 collective-permute-done.1.others
  105.1 1.0 shard_map.150
  (1 shorter events, 0.0 us)
Async XLA Ops:
  2.9 2.4 %copy-start = (bf16[128,1152]{1,0:T(8,128)(2,1)S(1)}, bf16[128,1152]{1,0:T(8,128)(2,1)}, u32[]{:S(2)}) copy-start(bf16[128,1152]{1,0:T(8,128)(2,1)} %get-tuple-element.38.normed.pair_hat) | copy-start | bytes 884740
  5.3 0.7 copy-start.2
  6.4 24.3 %copy-start.3 = (bf16[12,64,96]{2,1,0:T(8,128)(2,1)S(1)}, bf16[12,64,96]{2,1,0:T(8,128)(2,1)}, u32[]{:S(2)}) copy-start(bf16[12,64,96]{2,1,0:T(8,128)(2,1)} %get-tuple-element.45) | copy-start | bytes 442372
  30.8 1.6 %collective-permute-start = (bf16[12,64,96]{2,1,0:T(8,128)(2,1)S(1)}, bf16[12,64,96]{2,1,0:T(8,128)(2,1)S(1)}, u32[]{:S(2)}, u32[]{:S(2)}) collective-permute-start(bf16[12,64,96]{2,1,0:T(8,128)(2,1)S(1)} %copy-done.3), channel_id=1, source_target_pairs={{0,1},{1,0},{2,3},{3,2},{4,5},{5,4},{6,7},{7,6},{8,9},{9,8},{10,11... | collective-permute-start | bytes 442376 | tf_op jit(solution)/shard_map/ppermute | solution.py:438
  32.3 13.2 %copy-start.1 = (bf16[24,96,64]{1,2,0:T(8,128)(2,1)S(1)}, bf16[24,96,64]{1,2,0:T(8,128)(2,1)}, u32[]{:S(2)}) copy-start(bf16[24,96,64]{1,2,0:T(8,128)(2,1)} %param.9) | copy-start | bytes 884740
  94.5 10.6 %collective-permute-start.1 = (bf16[2,12,64,96]{3,2,1,0:T(8,128)(2,1)S(1)}, bf16[2,12,64,96]{3,2,1,0:T(8,128)(2,1)S(1)}, u32[]{:S(2)}, u32[]{:S(2)}) collective-permute-start(bf16[2,12,64,96]{3,2,1,0:T(8,128)(2,1)S(1)} %get-tuple-element.59), channel_id=1, source_target_pairs={{0,1},{1,0},{2,3},{3,2},{4,5},{5,4},{6,7},{7,6},{8,9},{9,8},{10,11... | collective-permute-start | bytes 884744 | tf_op jit(solution)/shard_map/ppermute | solution.py:485

commit v10 on v8

--- a/solution.py
+++ b/solution.py
@@ -244,7 +244,8 @@
         ]
 
 
-def mix(parts, cols, arrived, send, kept, held, result):
+def mix(parts, cols, arrived, inverse, send, kept, inverse_on, held, result):
+    inverse_on[...] = inverse[...]
     block = 8
     q = arrived.shape[1]
     spread_rows(block, cols, arrived, held)
@@ -257,10 +258,13 @@
     pack_rows(block, cols, result, send)
 
 
-def unmix(parts, cols, arrived, kept, send, held, result):
+def unmix(parts, cols, arrived, kept_far, send, held, result, kept, arrival):
     block = 8
     q = arrived.shape[1]
+    copy = pltpu.make_async_copy(kept_far, kept, arrival)
+    copy.start()
     spread_rows(block, cols, arrived, held)
+    copy.wait()
     for e in range(q):
         d_mixed = square(block, parts, cols, held, e)
         put_square(block, parts, cols, result, e, dot(d_mixed, kept[q + e], (1, 0)))
@@ -431,10 +435,14 @@
     arrived, other = lax.optimization_barrier((arrived, other))
     other = lax.ppermute(other, "ch", swap)
     room = pltpu.VMEM((col_parts * tokens * 8, -(-cols // 128) * 128), f32)
-    send, kept = call(
+    send, kept, inverse = call(
         functools.partial(mix, col_parts, cols),
-        [((devices, share, flat), bf16), ((2 * share, tokens, tokens), bf16)],
-        (arrived,),
+        [
+            ((devices, share, flat), bf16),
+            ((2 * share, tokens, tokens), bf16),
+            ((1, flat), f32),
+        ],
+        (arrived, inverse),
         (room, room),
     )
     send, other = lax.optimization_barrier((send, other))
@@ -456,7 +464,8 @@
         functools.partial(unmix, col_parts, cols),
         [((devices, 2 * share, flat), bf16)],
         (arrived, kept),
-        (room, room),
+        (room, room, pltpu.VMEM(kept.shape, bf16), pltpu.SemaphoreType.DMA),
+        far=(1,),
     )
     arrived = lax.all_to_all(send, everyone, 0, 0)
     total = 2 * width + 2 * hidden

time: 107 us -> 106 us (level)
  transfers between devices with their start and end apart: 2 -> 2, of which waited for: 0 -> 0; matrix products, arithmetic and copies ran while one was open for 0% -> 0% of each run, Pallas kernels for 1% -> 2%
where the time goes in v10:
time: 106 us
  blocking collectives  95.3 us (90%)
  Pallas kernels  9.45 us (9%)
    all_to_all x4, blocking collectives, by_channels(): arrived = lax.all_to_all(send, everyone, 0, 0)  70.5 us
    all_to_all x1, blocking collectives, by_channels(): arrived = lax.all_to_all(send, ('ch', 'row', 'col'), 0, 0)  11.9 us
    all_to_all x1, blocking collectives, by_channels(): sums = lax.all_to_all(sums, ('row', 'col'), 0, 0)  10.6 us
    pallas_call x8, Pallas kernels, call(): pl.pallas_call(kernel, out_shape=tuple((jax.ShapeDtypeStruct(*out) for ou...  9.45 us
    all_gather x1, blocking collectives, by_channels(): weights = lax.all_gather(weights, 'ch')  2.39 us
  transfers between devices with their start and end apart: 2, of which 0 were waited for; matrix products, arithmetic and copies ran while one was open for 0% of the time, Pallas kernels for 2%

profile of v10, /device:TPU:0, one launch (start us, length us, event | category | flops | bytes accessed | tf_op | source)
XLA Modules:
  0.0 105.5 jit_solution(2739986085737264661)
XLA Ops:
  0.6 2.2 %shard_map.143 = (bf16[384,128]{1,0:T(8,128)(2,1)}, bf16[128,1152]{1,0:T(8,128)(2,1)}, f32[1,1152]{1,0:T(1,128)}, bf16[12,64,96]{2,1,0:T(8,128)(2,1)}) custom-call(bf16[64,128]{1,0:T(8,128)(2,1)} %bitcast.21, bf16[64,128]{1,0:T(8,128)(2,1)} %bitcast.22, bf16[64,128]{1,0:T(8,128)(2,1)} %bitcast.23, bf16[64,128]{1,0:T(8,128)(2,1)} %bitcast.24, ...), custom_call_target="tpu_custom_call" | custom-call | tf_op jit(solution)/shard_map/pallas_call | solution.py:132
  2.9 0.0 copy-start
  2.9 2.4 %all-gather = bf16[768,128]{1,0:T(8,128)(2,1)S(1)} all-gather(bf16[384,128]{1,0:T(8,128)(2,1)} %get-tuple-element.38), channel_id=2, replica_groups=mesh['row'=8,'col'=2,'ch'=2] {'ch'}, dimensions={0}, use_global_device_ids=true | all-gather | bytes 294912 | tf_op jit(solution)/shard_map/all_gather | solution.py:430
  5.3 0.0 copy-done
  5.3 0.5 shard_map.144
  5.7 0.0 copy-start.3
  5.8 0.0 copy-start.2
  5.8 24.3 %all_to_all.30.arrived = bf16[32,8,1152]{2,1,0:T(8,128)(2,1)S(1)} all-to-all(bf16[32,8,1152]{2,1,0:T(8,128)(2,1)S(1)} %shard_map.144), channel_id=1, replica_groups=mesh['row'=8,'col'=2,'ch'=2] {'col','row','ch'}, dimensions={0} | all-to-all | bytes 1179648 | tf_op jit(solution)/shard_map/all_to_all | solution.py:434
  30.1 0.0 copy-done.3
  30.1 0.0 collective-permute-start
  30.1 0.0 copy-done.2
  30.1 1.5 %shard_map.145 = (bf16[32,4,1152]{2,1,0:T(4,128)(2,1)S(1)}, bf16[8,192,192]{2,1,0:T(8,128)(2,1)S(1)}, f32[1,1152]{1,0:T(1,128)S(1)}) custom-call(bf16[32,8,1152]{2,1,0:T(8,128)(2,1)S(1)} %all_to_all.30.arrived, f32[1,1152]{1,0:T(1,128)S(1)} %copy-done.2), custom_call_target="tpu_custom_call" | custom-call | tf_op jit(solution)/shard_map/pallas_call | solution.py:132
  31.7 0.0 copy-start.1
  31.7 0.0 collective-permute-done.other
  31.7 13.2 %all_to_all.31.arrived = bf16[32,4,1152]{2,1,0:T(4,128)(2,1)S(1)} all-to-all(bf16[32,4,1152]{2,1,0:T(4,128)(2,1)S(1)} %get-tuple-element.44), channel_id=1, replica_groups=mesh['row'=8,'col'=2,'ch'=2] {'col','row','ch'}, dimensions={0} | all-to-all | bytes 589824 | tf_op jit(solution)/shard_map/all_to_all | solution.py:449
  44.9 0.0 copy-done.1
  44.9 1.1 %shard_map.146 = (bf16[32,4,1152]{2,1,0:T(4,128)(2,1)S(1)}, bf16[128,1152]{1,0:T(8,128)(2,1)S(1)}, f32[2,128,128]{2,1,0:T(8,128)S(1)}, bf16[12,64,96]{2,1,0:T(8,128)(2,1)S(1)}, bf16[12,64,96]{2,1,0:T(8,128)(2,1)S(1)}) custom-call(bf16[32,4,1152]{2,1,0:T(4,128)(2,1)S(1)} %all_to_all.31.arrived, bf16[2,384,128]{2,1,0:T(8,128)(2,1)S(1)} %bitcast.17, ...), custom_call_target="tpu_custom_call" | custom-call | tf_op jit(solution)/shard_map/pallas_call | solution.py:132
  46.0 13.3 %all_to_all.32.arrived = bf16[32,4,1152]{2,1,0:T(4,128)(2,1)S(1)} all-to-all(bf16[32,4,1152]{2,1,0:T(4,128)(2,1)S(1)} %get-tuple-element.46), channel_id=1, replica_groups=mesh['row'=8,'col'=2,'ch'=2] {'col','row','ch'}, dimensions={0} | all-to-all | bytes 589824 | tf_op jit(solution)/shard_map/all_to_all | solution.py:462
  59.3 1.6 %shard_map.147 = bf16[32,8,1152]{2,1,0:T(8,128)(2,1)S(1)} custom-call(bf16[32,4,1152]{2,1,0:T(4,128)(2,1)S(1)} %all_to_all.32.arrived, bf16[8,192,192]{2,1,0:T(8,128)(2,1)S(1)} %get-tuple-element.47.kept_far), custom_call_target="tpu_custom_call" | custom-call | tf_op jit(solution)/shard_map/pallas_call | solution.py:132
  60.9 19.6 %all_to_all.33.arrived = bf16[32,8,1152]{2,1,0:T(8,128)(2,1)S(1)} all-to-all(bf16[32,8,1152]{2,1,0:T(8,128)(2,1)S(1)} %shard_map.147), channel_id=1, replica_groups=mesh['row'=8,'col'=2,'ch'=2] {'col','row','ch'}, dimensions={0} | all-to-all | bytes 1179648 | tf_op jit(solution)/shard_map/all_to_all | solution.py:470
  80.5 1.5 %shard_map.148 = (bf16[32,24,128]{2,1,0:T(8,128)(2,1)S(1)}, bf16[12,64,96]{2,1,0:T(8,128)(2,1)S(1)}, bf16[2,12,64,96]{3,2,1,0:T(8,128)(2,1)S(1)}) custom-call(bf16[32,8,1152]{2,1,0:T(8,128)(2,1)S(1)} %all_to_all.33.arrived, bf16[2,384,128]{2,1,0:T(8,128)(2,1)S(1)} %bitcast.18, bf16[128,1152]{1,0:T(8,128)(2,1)S(1)} %copy-done, ...), custom_call_target="tpu_custom_call" | custom-call | tf_op jit(solution)/shard_map/pallas_call | solution.py:132
  82.0 11.9 %all_to_all.34.arrived = bf16[32,24,128]{2,1,0:T(8,128)(2,1)S(1)} all-to-all(bf16[32,24,128]{2,1,0:T(8,128)(2,1)S(1)} %get-tuple-element.52), channel_id=1, replica_groups=mesh['row'=8,'col'=2,'ch'=2] {'ch','row','col'}, dimensions={0} | all-to-all | bytes 393216 | tf_op jit(solution)/shard_map/all_to_all | solution.py:479
  93.9 0.0 collective-permute-start.1
  93.9 10.6 %all_to_all.35.sums = bf16[16,24,128]{2,1,0:T(8,128)(2,1)S(1)} all-to-all(bf16[16,24,128]{2,1,0:T(8,128)(2,1)S(1)} %shard_map.149), channel_id=1, replica_groups=mesh['row'=8,'col'=2,'ch'=2] {'row','col'}, dimensions={0} | all-to-all | bytes 196608 | tf_op jit(solution)/shard_map/all_to_all | solution.py:483
  104.5 0.0 collective-permute-done.1.others
  104.5 1.0 shard_map.150
  (1 shorter events, 0.0 us)
Async XLA Ops:
  2.9 2.4 %copy-start = (bf16[128,1152]{1,0:T(8,128)(2,1)S(1)}, bf16[128,1152]{1,0:T(8,128)(2,1)}, u32[]{:S(2)}) copy-start(bf16[128,1152]{1,0:T(8,128)(2,1)} %get-tuple-element.37.normed.pair_hat) | copy-start | bytes 884740
  5.7 24.4 %copy-start.3 = (bf16[12,64,96]{2,1,0:T(8,128)(2,1)S(1)}, bf16[12,64,96]{2,1,0:T(8,128)(2,1)}, u32[]{:S(2)}) copy-start(bf16[12,64,96]{2,1,0:T(8,128)(2,1)} %get-tuple-element.43) | copy-start | bytes 442372
  5.8 24.4 %copy-start.2 = (f32[1,1152]{1,0:T(1,128)S(1)}, f32[1,1152]{1,0:T(1,128)}, u32[]{:S(2)}) copy-start(f32[1,1152]{1,0:T(1,128)} %get-tuple-element.41.inverse) | copy-start | bytes 13828
  30.1 1.6 %collective-permute-start = (bf16[12,64,96]{2,1,0:T(8,128)(2,1)S(1)}, bf16[12,64,96]{2,1,0:T(8,128)(2,1)S(1)}, u32[]{:S(2)}, u32[]{:S(2)}) collective-permute-start(bf16[12,64,96]{2,1,0:T(8,128)(2,1)S(1)} %copy-done.3), channel_id=1, source_target_pairs={{0,1},{1,0},{2,3},{3,2},{4,5},{5,4},{6,7},{7,6},{8,9},{9,8},{10,11... | collective-permute-start | bytes 442376 | tf_op jit(solution)/shard_map/ppermute | solution.py:436
  31.7 13.2 %copy-start.1 = (bf16[24,96,64]{1,2,0:T(8,128)(2,1)S(1)}, bf16[24,96,64]{1,2,0:T(8,128)(2,1)}, u32[]{:S(2)}) copy-start(bf16[24,96,64]{1,2,0:T(8,128)(2,1)} %param.9) | copy-start | bytes 884740
  93.9 10.6 %collective-permute-start.1 = (bf16[2,12,64,96]{3,2,1,0:T(8,128)(2,1)S(1)}, bf16[2,12,64,96]{3,2,1,0:T(8,128)(2,1)S(1)}, u32[]{:S(2)}, u32[]{:S(2)}) collective-permute-start(bf16[2,12,64,96]{3,2,1,0:T(8,128)(2,1)S(1)} %get-tuple-element.57), channel_id=1, source_target_pairs={{0,1},{1,0},{2,3},{3,2},{4,5},{5,4},{6,7},{7,6},{8,9},{9,8},{10,11... | collective-permute-start | bytes 884744 | tf_op jit(solution)/shard_map/ppermute | solution.py:487

commit v11 on v10

--- a/solution.py
+++ b/solution.py
@@ -476,11 +476,11 @@
         (arrived, weights, normed, inverse, d_gate, head_terms, updated_other),
         (pltpu.VMEM((total * parts, channels), f32),),
     )
-    arrived = lax.all_to_all(send, ("ch", "row", "col"), 0, 0)
+    arrived = lax.all_to_all(send, ("ch", "col", "row"), 0, 0)
     rest = devices // parts
     arrived, others = lax.optimization_barrier((arrived, others))
     (sums,) = call(add_up, [((rest, per, channels), bf16)], (arrived,))
-    sums = lax.all_to_all(sums, ("row", "col"), 0, 0)
+    sums = lax.all_to_all(sums, ("col", "row"), 0, 0)
     updated, grad_pair, *grads = call(
         functools.partial(finish, share),
         [((row_count, hidden, cols), bf16)] * 2 + [((hidden, channels), f32)] * 6,

time: 106 us -> 106 us (level)
  blocking collectives: 95.3 us -> 94 us
  starting transfers between devices: 0.01 us -> 1.08 us
    all_to_all x2, blocking collectives: 22.4 us -> 21.1 us  [the longest x1 10.6 us: by_channels(): arrived = lax.all_to_all(send, ('ch', 'col', 'row'), 0, 0)]
    ppermute x1, starting transfers between devices: 0.01 us -> 1.08 us  [by_channels(): lax.ppermute(others, 'ch', swap)]
where the time goes in v11:
time: 106 us; the launch traced here: 105 us
  blocking collectives  94 us (89%)
  Pallas kernels  9.45 us (9%)
  starting transfers between devices  1.08 us (1%)
    all_to_all x4, blocking collectives, by_channels(): arrived = lax.all_to_all(send, everyone, 0, 0)  70.5 us
    all_to_all x1, blocking collectives, by_channels(): arrived = lax.all_to_all(send, ('ch', 'col', 'row'), 0, 0)  10.6 us
    all_to_all x1, blocking collectives, by_channels(): sums = lax.all_to_all(sums, ('col', 'row'), 0, 0)  10.5 us
    pallas_call x8, Pallas kernels, call(): pl.pallas_call(kernel, out_shape=tuple((jax.ShapeDtypeStruct(*out) for ou...  9.45 us
    all_gather x1, blocking collectives, by_channels(): weights = lax.all_gather(weights, 'ch')  2.39 us
  transfers between devices with their start and end apart: 2, of which 0 were waited for; matrix products, arithmetic and copies ran while one was open for 0% of the time, Pallas kernels for 2%

profile of v11, /device:TPU:0, one launch (start us, length us, event | category | flops | bytes accessed | tf_op | source)
XLA Modules:
  0.0 105.3 jit_solution(838544172096587224)
XLA Ops:
  0.6 2.2 %shard_map.143 = (bf16[384,128]{1,0:T(8,128)(2,1)}, bf16[128,1152]{1,0:T(8,128)(2,1)}, f32[1,1152]{1,0:T(1,128)}, bf16[12,64,96]{2,1,0:T(8,128)(2,1)}) custom-call(bf16[64,128]{1,0:T(8,128)(2,1)} %bitcast.21, bf16[64,128]{1,0:T(8,128)(2,1)} %bitcast.22, bf16[64,128]{1,0:T(8,128)(2,1)} %bitcast.23, bf16[64,128]{1,0:T(8,128)(2,1)} %bitcast.24, ...), custom_call_target="tpu_custom_call" | custom-call | tf_op jit(solution)/shard_map/pallas_call | solution.py:132
  2.9 0.0 copy-start
  2.9 2.4 %all-gather = bf16[768,128]{1,0:T(8,128)(2,1)S(1)} all-gather(bf16[384,128]{1,0:T(8,128)(2,1)} %get-tuple-element.38), channel_id=2, replica_groups=mesh['row'=8,'col'=2,'ch'=2] {'ch'}, dimensions={0}, use_global_device_ids=true | all-gather | bytes 294912 | tf_op jit(solution)/shard_map/all_gather | solution.py:430
  5.3 0.0 copy-done
  5.3 0.5 shard_map.144
  5.7 0.0 copy-start.3
  5.8 0.0 copy-start.2
  5.8 24.3 %all_to_all.30.arrived = bf16[32,8,1152]{2,1,0:T(8,128)(2,1)S(1)} all-to-all(bf16[32,8,1152]{2,1,0:T(8,128)(2,1)S(1)} %shard_map.144), channel_id=1, replica_groups=mesh['row'=8,'col'=2,'ch'=2] {'col','row','ch'}, dimensions={0} | all-to-all | bytes 1179648 | tf_op jit(solution)/shard_map/all_to_all | solution.py:434
  30.1 0.0 copy-done.3
  30.1 0.0 collective-permute-start
  30.1 0.0 copy-done.2
  30.1 1.5 %shard_map.145 = (bf16[32,4,1152]{2,1,0:T(4,128)(2,1)S(1)}, bf16[8,192,192]{2,1,0:T(8,128)(2,1)S(1)}, f32[1,1152]{1,0:T(1,128)S(1)}) custom-call(bf16[32,8,1152]{2,1,0:T(8,128)(2,1)S(1)} %all_to_all.30.arrived, f32[1,1152]{1,0:T(1,128)S(1)} %copy-done.2), custom_call_target="tpu_custom_call" | custom-call | tf_op jit(solution)/shard_map/pallas_call | solution.py:132
  31.7 0.0 copy-start.1
  31.7 0.0 collective-permute-done.other
  31.7 13.2 %all_to_all.31.arrived = bf16[32,4,1152]{2,1,0:T(4,128)(2,1)S(1)} all-to-all(bf16[32,4,1152]{2,1,0:T(4,128)(2,1)S(1)} %get-tuple-element.44), channel_id=1, replica_groups=mesh['row'=8,'col'=2,'ch'=2] {'col','row','ch'}, dimensions={0} | all-to-all | bytes 589824 | tf_op jit(solution)/shard_map/all_to_all | solution.py:449
  44.9 0.0 copy-done.1
  44.9 1.1 %shard_map.146 = (bf16[32,4,1152]{2,1,0:T(4,128)(2,1)S(1)}, bf16[128,1152]{1,0:T(8,128)(2,1)S(1)}, f32[2,128,128]{2,1,0:T(8,128)S(1)}, bf16[12,64,96]{2,1,0:T(8,128)(2,1)S(1)}, bf16[12,64,96]{2,1,0:T(8,128)(2,1)S(1)}) custom-call(bf16[32,4,1152]{2,1,0:T(4,128)(2,1)S(1)} %all_to_all.31.arrived, bf16[2,384,128]{2,1,0:T(8,128)(2,1)S(1)} %bitcast.17, ...), custom_call_target="tpu_custom_call" | custom-call | tf_op jit(solution)/shard_map/pallas_call | solution.py:132
  46.0 13.3 %all_to_all.32.arrived = bf16[32,4,1152]{2,1,0:T(4,128)(2,1)S(1)} all-to-all(bf16[32,4,1152]{2,1,0:T(4,128)(2,1)S(1)} %get-tuple-element.46), channel_id=1, replica_groups=mesh['row'=8,'col'=2,'ch'=2] {'col','row','ch'}, dimensions={0} | all-to-all | bytes 589824 | tf_op jit(solution)/shard_map/all_to_all | solution.py:462
  59.3 1.6 %shard_map.147 = bf16[32,8,1152]{2,1,0:T(8,128)(2,1)S(1)} custom-call(bf16[32,4,1152]{2,1,0:T(4,128)(2,1)S(1)} %all_to_all.32.arrived, bf16[8,192,192]{2,1,0:T(8,128)(2,1)S(1)} %get-tuple-element.47.kept_far), custom_call_target="tpu_custom_call" | custom-call | tf_op jit(solution)/shard_map/pallas_call | solution.py:132
  60.9 19.6 %all_to_all.33.arrived = bf16[32,8,1152]{2,1,0:T(8,128)(2,1)S(1)} all-to-all(bf16[32,8,1152]{2,1,0:T(8,128)(2,1)S(1)} %shard_map.147), channel_id=1, replica_groups=mesh['row'=8,'col'=2,'ch'=2] {'col','row','ch'}, dimensions={0} | all-to-all | bytes 1179648 | tf_op jit(solution)/shard_map/all_to_all | solution.py:470
  80.5 1.5 %shard_map.148 = (bf16[32,24,128]{2,1,0:T(8,128)(2,1)S(1)}, bf16[12,64,96]{2,1,0:T(8,128)(2,1)S(1)}, bf16[2,12,64,96]{3,2,1,0:T(8,128)(2,1)S(1)}) custom-call(bf16[32,8,1152]{2,1,0:T(8,128)(2,1)S(1)} %all_to_all.33.arrived, bf16[2,384,128]{2,1,0:T(8,128)(2,1)S(1)} %bitcast.18, bf16[128,1152]{1,0:T(8,128)(2,1)S(1)} %copy-done, ...), custom_call_target="tpu_custom_call" | custom-call | tf_op jit(solution)/shard_map/pallas_call | solution.py:132
  82.0 10.6 %all_to_all.34.arrived = bf16[32,24,128]{2,1,0:T(8,128)(2,1)S(1)} all-to-all(bf16[32,24,128]{2,1,0:T(8,128)(2,1)S(1)} %get-tuple-element.52), channel_id=1, replica_groups=mesh['row'=8,'col'=2,'ch'=2] {'ch','col','row'}, dimensions={0} | all-to-all | bytes 393216 | tf_op jit(solution)/shard_map/all_to_all | solution.py:479
  92.6 1.1 %collective-permute-start.1 = (bf16[2,12,64,96]{3,2,1,0:T(8,128)(2,1)S(1)}, bf16[2,12,64,96]{3,2,1,0:T(8,128)(2,1)S(1)}, u32[]{:S(2)}, u32[]{:S(2)}) collective-permute-start(bf16[2,12,64,96]{3,2,1,0:T(8,128)(2,1)S(1)} %get-tuple-element.57), channel_id=1, source_target_pairs={{0,1},{1,0},{2,3},{3,2},{4,5},{5,4},{6,7},{7,6},{8,9},{9,8},{10,11... | collective-permute-start | bytes 884744 | tf_op jit(solution)/shard_map/ppermute | solution.py:487
  93.7 10.5 %all_to_all.35.sums = bf16[16,24,128]{2,1,0:T(8,128)(2,1)S(1)} all-to-all(bf16[16,24,128]{2,1,0:T(8,128)(2,1)S(1)} %shard_map.149), channel_id=1, replica_groups=mesh['row'=8,'col'=2,'ch'=2] {'col','row'}, dimensions={0} | all-to-all | bytes 196608 | tf_op jit(solution)/shard_map/all_to_all | solution.py:483
  104.2 0.0 collective-permute-done.1.others
  104.2 1.0 shard_map.150
  (1 shorter events, 0.0 us)
Async XLA Ops:
  2.9 2.4 %copy-start = (bf16[128,1152]{1,0:T(8,128)(2,1)S(1)}, bf16[128,1152]{1,0:T(8,128)(2,1)}, u32[]{:S(2)}) copy-start(bf16[128,1152]{1,0:T(8,128)(2,1)} %get-tuple-element.37.normed.pair_hat) | copy-start | bytes 884740
  5.7 24.4 %copy-start.3 = (bf16[12,64,96]{2,1,0:T(8,128)(2,1)S(1)}, bf16[12,64,96]{2,1,0:T(8,128)(2,1)}, u32[]{:S(2)}) copy-start(bf16[12,64,96]{2,1,0:T(8,128)(2,1)} %get-tuple-element.43) | copy-start | bytes 442372
  5.8 24.4 %copy-start.2 = (f32[1,1152]{1,0:T(1,128)S(1)}, f32[1,1152]{1,0:T(1,128)}, u32[]{:S(2)}) copy-start(f32[1,1152]{1,0:T(1,128)} %get-tuple-element.41.inverse) | copy-start | bytes 13828
  30.1 1.6 %collective-permute-start = (bf16[12,64,96]{2,1,0:T(8,128)(2,1)S(1)}, bf16[12,64,96]{2,1,0:T(8,128)(2,1)S(1)}, u32[]{:S(2)}, u32[]{:S(2)}) collective-permute-start(bf16[12,64,96]{2,1,0:T(8,128)(2,1)S(1)} %copy-done.3), channel_id=1, source_target_pairs={{0,1},{1,0},{2,3},{3,2},{4,5},{5,4},{6,7},{7,6},{8,9},{9,8},{10,11... | collective-permute-start | bytes 442376 | tf_op jit(solution)/shard_map/ppermute | solution.py:436
  31.7 13.2 %copy-start.1 = (bf16[24,96,64]{1,2,0:T(8,128)(2,1)S(1)}, bf16[24,96,64]{1,2,0:T(8,128)(2,1)}, u32[]{:S(2)}) copy-start(bf16[24,96,64]{1,2,0:T(8,128)(2,1)} %param.9) | copy-start | bytes 884740
  92.6 11.6 %collective-permute-start.1 = (bf16[2,12,64,96]{3,2,1,0:T(8,128)(2,1)S(1)}, bf16[2,12,64,96]{3,2,1,0:T(8,128)(2,1)S(1)}, u32[]{:S(2)}, u32[]{:S(2)}) collective-permute-start(bf16[2,12,64,96]{3,2,1,0:T(8,128)(2,1)S(1)} %get-tuple-element.57), channel_id=1, source_target_pairs={{0,1},{1,0},{2,3},{3,2},{4,5},{5,4},{6,7},{7,6},{8,9},{9,8},{10,11... | collective-permute-start | bytes 884744 | tf_op jit(solution)/shard_map/ppermute | solution.py:487
